TPU v7x, 256 devices: a whole 4x4x8 slice. The times are simulated.
256 devices in a mesh: region: 32 (over z, y), scan: 8 (over x, core).
Axes of the slice: x: 4, y: 4, z: 8, core: 2. Of those that a mesh axis runs over, the one named last changes fastest.
Arguments:
- object_field: float32 [2, 8192, 2048], P(None, 'region', 'scan'), may hold values from -5 to 5
- probe_modes: float32 [2, 8, 256, 256], replicated, may hold values from -4 to 4
- pattern: float32 [32, 8, 2, 256, 256], P('region', 'scan'), may hold values from 0.1 to 8
- rows_at: int32 [32, 8, 2], P('region', 'scan'), may hold values from 0 to 8191, as said below
- cols_at: int32 [32, 8, 2], P('region', 'scan'), may hold values from 0 to 2047, as said below
- object_step: float32 [1], replicated, may hold values from 0.1 to 0.4
- probe_step: float32 [1], replicated, may hold values from 0.05 to 0.1
Outputs:
- object_new: float32 [2, 8192, 2048], P(None, 'region', 'scan')
- probe_new: float32 [2, 8, 256, 256], replicated
Inputs may be any that keep to these rules, and one draw needn't show every extreme that they name: `rows_at`: the windows of the 2 scans k of device (r, s) start at padded rows r * 256 + o + k * 128, with one o of that device and 0 <= o + k * 128 < 256. `cols_at`: the window of scan (r, s, k) starts at padded column s * 256 + o with 0 <= o < 256.
All inputs are finite; a program needn't handle non-finite values.
Results may differ from a plain program's by a relative error of at most 0.002.
The roundings to bfloat16 on the way count: a program that leaves them out, or rounds other values in their place, can miss the bound.
Values may be sent and summed in bfloat16 or wider, within the bound.
No kernel may reach another device: no remote copies, remote signals or barrier semaphores. Data moves between devices by JAX's collectives and lax.ppermute only.
A program may use at most 64 MiB of HBM per device.

v0:
```python
import math

import jax
import jax.numpy as jnp
import ml_dtypes
import numpy as np
from jax import lax
from jax.experimental import pallas as pl
from jax.experimental.pallas import tpu as pltpu
from jax.sharding import PartitionSpec as P


UNROLL = 4


def padded_2(cells, sides, width):
    for axis, dim in sides:
        count = lax.axis_size(axis)
        ends = count - 1
        head = lax.slice_in_dim(cells, 0, width, axis=dim)
        tail = lax.slice_in_dim(cells, cells.shape[dim] - width, cells.shape[dim], axis=dim)
        cells = jnp.concatenate(
            [
                lax.ppermute(tail, axis, [(i, (i + 1) % count) for i in range(ends)]),
                cells,
                lax.ppermute(head, axis, [((i + 1) % count, i) for i in range(ends)]),
            ],
            axis=dim,
        )
    return cells


def fourier_blocks(length):
    position = np.arange(length)
    angles = (position[:, None] * position[None, :] % length) * (2.0 * math.pi / length)
    table_scale = 1.0 / math.sqrt(length)
    cosine_table = (np.cos(angles) * table_scale).astype(ml_dtypes.bfloat16)
    sine_table = (np.sin(angles) * table_scale).astype(ml_dtypes.bfloat16)
    forward = np.block([[cosine_table, sine_table], [-sine_table, cosine_table]])
    return (jnp.asarray(forward), jnp.asarray(np.ascontiguousarray(forward.T)))


def fourier_pass(real_part, imag_part, left, right):
    length = real_part.shape[-1]
    stacked = jnp.concatenate([real_part, imag_part], axis=0)
    middle = jnp.dot(left, stacked, preferred_element_type=jnp.float32).astype(jnp.bfloat16)
    middle = jnp.concatenate([middle[:length], middle[length:]], axis=1)
    return jnp.dot(middle, right, preferred_element_type=jnp.float32)


def gradients_kernel(
    place_ref,
    block_ref,
    above_ref,
    below_ref,
    left_ref,
    right_ref,
    probe_ref,
    pattern_ref,
    forward_ref,
    backward_ref,
    grad_ref,
    mine_ref,
    other_ref,
    padded_ref,
    window_ref,
    far_ref,
    level_ref,
    object_ref,
    term_ref,
):
    modes, length = probe_ref.shape[1], probe_ref.shape[2]
    half = length // 2
    rows, cols = block_ref.shape[1], block_ref.shape[2]
    wide = padded_ref.shape[2]
    slots = pattern_ref.shape[0]
    padded_ref[:, half : half + rows, half : half + cols] = (
        block_ref[...].astype(jnp.bfloat16).astype(jnp.float32)
    )
    padded_ref[:, :half, half : half + cols] = above_ref[...].astype(jnp.float32)
    padded_ref[:, half + rows :, half : half + cols] = below_ref[...].astype(jnp.float32)
    padded_ref[:, :, :half] = left_ref[...].astype(jnp.float32)
    padded_ref[:, :, half + cols :] = right_ref[...].astype(jnp.float32)
    grad_ref[...] = jnp.zeros_like(grad_ref)
    first = place_ref[2, 0] == 0
    for slot in range(slots):
        row = place_ref[0, slot]
        col = place_ref[1, slot]
        shift = row % 8
        span = pl.ds(pl.multiple_of(row - shift, 8), length + 8)
        for part in range(2):
            strip = pltpu.roll(padded_ref[part, span, :], wide - col, 1)[:, :length]
            window_ref[part] = pltpu.roll(strip, length + 8 - shift, 0)[:length]

        level_ref[...] = jnp.zeros_like(level_ref)

        def go_forward(mode, carry):
            win_real, win_imag = window_ref[0], window_ref[1]
            probe_real, probe_imag = probe_ref[0, mode], probe_ref[1, mode]
            far = fourier_pass(
                (probe_real * win_real - probe_imag * win_imag).astype(jnp.bfloat16),
                (probe_real * win_imag + probe_imag * win_real).astype(jnp.bfloat16),
                forward_ref[...],
                backward_ref[...],
            )
            far_ref[mode] = far
            far_real, far_imag = far[:, :length], far[:, length:]
            level_ref[...] += far_real * far_real + far_imag * far_imag
            return carry

        lax.fori_loop(0, modes, go_forward, 0, unroll=UNROLL)
        amplitude = jnp.maximum(jnp.sqrt(level_ref[...]), 1.0)
        level_ref[...] = 1.0 - jnp.sqrt(pattern_ref[slot]) / amplitude
        object_ref[...] = jnp.zeros_like(object_ref)

        def go_back(mode, carry):
            factor = level_ref[...]
            far = far_ref[mode]
            back = fourier_pass(
                (factor * far[:, :length]).astype(jnp.bfloat16),
                (factor * far[:, length:]).astype(jnp.bfloat16),
                backward_ref[...],
                forward_ref[...],
            )
            back_real, back_imag = back[:, :length], back[:, length:]
            probe_real, probe_imag = probe_ref[0, mode], probe_ref[1, mode]
            object_ref[0] += probe_real * back_real + probe_imag * back_imag
            object_ref[1] += probe_real * back_imag - probe_imag * back_real
            win_real, win_imag = window_ref[0], window_ref[1]
            term_real = win_real * back_real + win_imag * back_imag
            term_imag = win_real * back_imag - win_imag * back_real
            if slot > 0:
                term_real += term_ref[0, mode]
                term_imag += term_ref[1, mode]
            if slot < slots - 1:
                term_ref[0, mode] = term_real
                term_ref[1, mode] = term_imag
            else:
                mine_ref[mode] = jnp.where(first, term_real, term_imag)
                other_ref[mode] = jnp.where(first, term_imag, term_real)
            return carry

        lax.fori_loop(0, modes, go_back, 0, unroll=UNROLL)
        for part in range(2):
            strip = jnp.concatenate(
                [object_ref[part], jnp.zeros((8, length), jnp.float32)], axis=0
            )
            strip = pltpu.roll(strip, shift, 0)
            strip = jnp.concatenate(
                [strip, jnp.zeros((length + 8, wide - length), jnp.float32)], axis=1
            )
            grad_ref[part, span, :] += pltpu.roll(strip, col, 1)


def device_gradients(place, block, above, below, left, right, probe, pattern):
    forward, backward = fourier_blocks(probe.shape[-1])
    _, modes, length, _ = probe.shape
    rows, cols = block.shape[1] + length, block.shape[2] + length
    slots = pattern.shape[0]
    vmem = pl.BlockSpec(memory_space=pltpu.VMEM)
    f32 = jnp.float32
    return pl.pallas_call(
        gradients_kernel,
        out_shape=(
            jax.ShapeDtypeStruct((2, rows, cols), f32),
            jax.ShapeDtypeStruct((modes, length, length), f32),
            jax.ShapeDtypeStruct((modes, length, length), f32),
        ),
        in_specs=[pl.BlockSpec(memory_space=pltpu.SMEM)] + [vmem] * 9,
        out_specs=(vmem, vmem, vmem),
        scratch_shapes=[
            pltpu.VMEM((2, rows, cols), f32),
            pltpu.VMEM((2, length, length), f32),
            pltpu.VMEM((modes, length, 2 * length), f32),
            pltpu.VMEM((length, length), f32),
            pltpu.VMEM((2, length, length), f32),
            pltpu.VMEM((2, modes, length, length), f32),
        ],
        compiler_params=pltpu.CompilerParams(vmem_limit_bytes=48 * 1024 * 1024),
        cost_estimate=pl.CostEstimate(
            flops=slots * modes * 32 * length**3, bytes_accessed=16 * 2**20, transcendentals=0
        ),
    )(place, block, above, below, left, right, probe, pattern, forward, backward)


def return_rims(grad_field, half_width):
    cols_rim = jnp.concatenate(
        [grad_field[:, :, :half_width], grad_field[:, :, -half_width:]], axis=2
    )
    cols_ext = padded_2(cols_rim, (("scan", 2),), half_width)
    core_block = grad_field[:, :, half_width:-half_width]
    core_block = core_block.at[:, :, :half_width].add(cols_ext[:, :, :half_width])
    core_block = core_block.at[:, :, -half_width:].add(cols_ext[:, :, -half_width:])
    rows_rim = jnp.concatenate([core_block[:, :half_width], core_block[:, -half_width:]], axis=1)
    rows_ext = padded_2(rows_rim, (("region", 1),), half_width)
    inner_block = core_block[:, half_width:-half_width]
    inner_block = inner_block.at[:, :half_width].add(rows_ext[:, :half_width])
    inner_block = inner_block.at[:, -half_width:].add(rows_ext[:, -half_width:])
    return inner_block


def axis_groups(kept):
    rows, cols = lax.axis_size("region"), lax.axis_size("scan")
    sizes = {"z": rows // 4, "y": 4, "x": cols // 2, "core": 2}
    groups = {}
    for device in range(rows * cols):
        place, rest = {}, device
        for name in ("core", "x", "y", "z"):
            place[name] = rest % sizes[name]
            rest = rest // sizes[name]
        key = tuple(place[name] for name in place if name not in kept)
        groups.setdefault(key, []).append(device)
    return [groups[key] for key in sorted(groups)]


def narrow(values, scale):
    return (values * (1.0 / scale)).astype(jnp.float16)


def widen(values, scale):
    return values.astype(jnp.float32) * scale


def exchange(parts, kept):
    return lax.all_to_all(parts, ("region", "scan"), 0, 0, axis_index_groups=axis_groups(kept))


def swap_cores(values):
    count = lax.axis_size("region") * lax.axis_size("scan")
    return lax.ppermute(values, ("region", "scan"), [(i, i ^ 1) for i in range(count)])


def sum_everywhere(mine, other):
    modes, rows, cols = mine.shape
    core = lax.axis_index("scan") % 2
    pair = mine + widen(swap_cores(narrow(other, 8.0)), 8.0)
    plane = 16
    slab = modes * rows // plane
    pieces = exchange(narrow(pair, 16.0).reshape(plane, slab, cols), ("y", "x"))
    slab_sum = jnp.sum(widen(pieces, 16.0), axis=0)
    depth = lax.axis_size("region") // 4
    pieces = exchange(slab_sum.reshape(depth, slab // depth, cols), ("z",))
    total = narrow(jnp.sum(pieces, axis=0), 2048.0)
    total = exchange(jnp.broadcast_to(total, (depth, slab // depth, cols)), ("z",))
    total = exchange(jnp.broadcast_to(total.reshape(slab, cols), (plane, slab, cols)), ("y", "x"))
    total = total.reshape(modes, rows, cols)
    swapped = swap_cores(total)
    first = core == 0
    return widen(
        jnp.stack([jnp.where(first, total, swapped), jnp.where(first, swapped, total)]), 2048.0
    )


def edges(cells, axis, dim, width):
    count = lax.axis_size(axis)
    ends = count - 1
    head = lax.slice_in_dim(cells, 0, width, axis=dim)
    tail = lax.slice_in_dim(cells, cells.shape[dim] - width, cells.shape[dim], axis=dim)
    before = lax.ppermute(tail, axis, [(i, (i + 1) % count) for i in range(ends)])
    after = lax.ppermute(head, axis, [((i + 1) % count, i) for i in range(ends)])
    return (before, after)


def on_device(object_field, probe_modes, pattern, rows_at, cols_at, object_step, probe_step):
    half_width = probe_modes.shape[-1] // 2
    block_rows = object_field.shape[1]
    block_cols = object_field.shape[2]
    core = lax.axis_index("scan") % 2
    place = jnp.stack(
        [
            rows_at[0, 0] % block_rows,
            cols_at[0, 0] % block_cols,
            jnp.broadcast_to(core, rows_at.shape[2:]).astype(jnp.int32),
        ]
    )
    cells = object_field.astype(jnp.bfloat16)
    above, below = edges(cells, "region", 1, half_width)
    tall = jnp.concatenate([above, cells, below], axis=1)
    left, right = edges(tall, "scan", 2, half_width)
    grad_field, mine, other = device_gradients(
        place, object_field, above, below, left, right, probe_modes, pattern[0, 0]
    )
    probe_total = sum_everywhere(mine, other)
    grad_block = return_rims(grad_field, half_width)
    object_field = object_field - object_step[0] * grad_block
    probe_modes = probe_modes - probe_step[0] * probe_total
    return (object_field, probe_modes)


def solution(mesh):
    return jax.shard_map(
        on_device,
        mesh=mesh,
        in_specs=(
            P(None, "region", "scan"),
            P(),
            P("region", "scan", None, None, None),
            P("region", "scan", None),
            P("region", "scan", None),
            P(),
            P(),
        ),
        out_specs=(P(None, "region", "scan"), P()),
        check_vma=False,
    )
```

profile of v0, /device:TPU:124, one launch (start us, length us, event | category | flops | bytes accessed | tf_op | source)
XLA Modules:
  0.0 156.0 jit_solution(3374184222489368745)
XLA Ops:
  0.7 1.2 convert_element_type.21
  1.9 2.7 %collective-permute-start.1 = (bf16[2,128,256]{2,1,0:T(8,128)(2,1)S(1)}, bf16[2,128,256]{2,1,0:T(8,128)(2,1)S(1)}, u32[]{:S(2)}, u32[]{:S(2)}) collective-permute-start(bf16[2,128,256]{2,1,0:T(8,128)(2,1)S(1)} %get-tuple-element.64), channel_id=1, source_target_pairs={{8,0},{16,8},{24,16},{32,24},{40,32},{48,40},{56,48},{64,56},{72,6... | collective-permute-start | bytes 393224 | tf_op jit(solution)/shard_map/ppermute | solution.py:260
  4.5 6.5 %collective-permute-start = (bf16[2,128,256]{2,1,0:T(8,128)(2,1)S(1)}, bf16[2,128,256]{2,1,0:T(8,128)(2,1)S(1)}, u32[]{:S(2)}, u32[]{:S(2)}) collective-permute-start(bf16[2,128,256]{2,1,0:T(8,128)(2,1)S(1)} %get-tuple-element.65), channel_id=1, source_target_pairs={{0,8},{8,16},{16,24},{24,32},{32,40},{40,48},{48,56},{56,64},{64,7... | collective-permute-start | bytes 393224 | tf_op jit(solution)/shard_map/ppermute | solution.py:259
  11.0 1.3 collective-permute-done.1.below_ref
  12.3 1.2 collective-permute-done.above_ref
  13.6 0.1 fusion.7
  13.7 1.9 %collective-permute-start.3 = (bf16[2,512,128]{2,1,0:T(8,128)(2,1)S(1)}, bf16[2,512,128]{2,1,0:T(8,128)(2,1)S(1)}, u32[]{:S(2)}, u32[]{:S(2)}) collective-permute-start(bf16[2,512,128]{2,1,0:T(8,128)(2,1)S(1)} %get-tuple-element.62), channel_id=1, source_target_pairs={{1,0},{2,1},{3,2},{4,3},{5,4},{6,5},{7,6},{9,8},{10,9},{11,10},{12... | collective-permute-start | bytes 786440 | tf_op jit(solution)/shard_map/ppermute | solution.py:260
  15.6 2.4 %collective-permute-start.2 = (bf16[2,512,128]{2,1,0:T(8,128)(2,1)S(1)}, bf16[2,512,128]{2,1,0:T(8,128)(2,1)S(1)}, u32[]{:S(2)}, u32[]{:S(2)}) collective-permute-start(bf16[2,512,128]{2,1,0:T(8,128)(2,1)S(1)} %get-tuple-element.63), channel_id=1, source_target_pairs={{0,1},{1,2},{2,3},{3,4},{4,5},{5,6},{6,7},{8,9},{9,10},{10,11},{11... | collective-permute-start | bytes 786440 | tf_op jit(solution)/shard_map/ppermute | solution.py:259
  18.2 1.3 collective-permute-done.3.right_ref
  19.5 0.7 copy-done.2
  20.2 3.1 %collective-permute-done.2.left_ref = bf16[2,512,128]{2,1,0:T(8,128)(2,1)S(1)} collective-permute-done((bf16[2,512,128]{2,1,0:T(8,128)(2,1)S(1)}, bf16[2,512,128]{2,1,0:T(8,128)(2,1)S(1)}, u32[]{:S(2)}, u32[]{:S(2)}) %collective-permute-start.2) | collective-permute-done | bytes 262176 | tf_op jit(solution)/shard_map/ppermute | solution.py:259
  23.3 0.7 copy-done.4
  24.0 0.9 copy-done.3
  24.9 0.9 copy-done.5
  25.9 1.0 copy-done.6
  26.9 1.0 copy-done.7
  28.0 21.6 %shard_map.104 = (f32[2,512,512]{2,1,0:T(8,128)S(1)}, f32[8,256,256]{2,1,0:T(8,128)}, f32[8,256,256]{2,1,0:T(8,128)}) custom-call(s32[3,2]{1,0:T(4,128)S(1)} %add_add_fusion.place_ref, f32[2,256,256]{2,1,0:T(8,128)S(1)} %copy-done, bf16[2,128,256]{2,1,0:T(8,128)(2,1)S(1)} %collective-permute-done.above_ref, ...), custom_call_target="tpu_custom_call" | custom-call | flops 8589934592 | bytes 16777216 | tf_op jit(solution)/shard_map/pallas_call | solution.py:162
  49.5 2.0 %multiply_convert_fusion.1 = f16[8,256,256]{2,1,0:T(8,128)(2,1)S(1)} fusion(f32[8,256,256]{2,1,0:T(8,128)} %get-tuple-element.55), kind=kLoop, calls=%fused_computation.3 | loop fusion | flops 1048576 | bytes 3145728 | tf_op jit(solution)/shard_map/convert_element_type | solution.py:217
  51.5 0.1 collective-permute-start.8
  51.6 2.6 %collective-permute-done.8 = f16[8,256,256]{2,1,0:T(8,128)(2,1)S(1)} collective-permute-done((f16[8,256,256]{2,1,0:T(8,128)(2,1)S(1)}, f16[8,256,256]{2,1,0:T(8,128)(2,1)S(1)}, u32[]{:S(2)}, u32[]{:S(2)}) %collective-permute-start.8) | collective-permute-done | bytes 1048608 | tf_op jit(solution)/shard_map/ppermute | solution.py:230
  54.3 0.4 multiply_convert_fusion
  54.7 20.0 %all_to_all.20 = f16[16,128,256]{2,1,0:T(8,128)(2,1)S(1)} all-to-all(f16[16,128,256]{2,1,0:T(8,128)(2,1)S(1)} %bitcast.21), channel_id=1, replica_groups={{0,2,4,6,8,10,12,14,16,18,20,22,24,26,28,30},{32,34,36,38,40,42,44,46,4..., dimensions={0} | all-to-all | bytes 2097152 | tf_op jit(solution)/shard_map/all_to_all | solution.py:225
  74.7 0.2 multiply_reduce_fusion
  74.9 13.5 %all_to_all.21 = f32[8,16,256]{2,1,0:T(8,128)S(1)} all-to-all(f32[8,16,256]{2,1,0:T(8,128)S(1)} %bitcast.22), channel_id=1, replica_groups={{0,32,64,96,128,160,192,224},{8,40,72,104,136,168,200,232},{16,48,80,11..., dimensions={0} | all-to-all | bytes 262144 | tf_op jit(solution)/shard_map/all_to_all | solution.py:225
  88.4 0.6 broadcast_in_dim.6
  89.0 6.9 %all-to-all-start.2 = ((f16[8,16,256]{2,1,0:T(8,128)(2,1)}), f16[8,16,256]{2,1,0:T(8,128)(2,1)S(1)}, u32[]{:S(2)}, u32[]{:S(2)}) async-start(f16[8,16,256]{2,1,0:T(8,128)(2,1)} %broadcast_in_dim.6), calls=%async_computation.2 | async-start | bytes 131072 | tf_op jit(solution)/shard_map/all_to_all | solution.py:225
  95.9 1.0 fusion.5
  96.9 1.9 %collective-permute-start.4 = (f32[2,512,128]{2,1,0:T(8,128)}, f32[2,512,128]{2,1,0:T(8,128)S(1)}, u32[]{:S(2)}, u32[]{:S(2)}) collective-permute-start(f32[2,512,128]{2,1,0:T(8,128)} %get-tuple-element.59), channel_id=1, source_target_pairs={{0,1},{1,2},{2,3},{3,4},{4,5},{5,6},{6,7},{8,9},{9,10},{10,11},{11... | collective-permute-start | bytes 1572872 | tf_op jit(solution)/shard_map/ppermute | solution.py:24
  98.9 2.0 %all-to-all-done.2 = f16[8,16,256]{2,1,0:T(8,128)(2,1)S(1)} async-done(((f16[8,16,256]{2,1,0:T(8,128)(2,1)}), f16[8,16,256]{2,1,0:T(8,128)(2,1)S(1)}, u32[]{:S(2)}, u32[]{:S(2)}) %all-to-all-start.2) | async-done | bytes 65568 | tf_op jit(solution)/shard_map/all_to_all | solution.py:225
  100.9 1.1 broadcast_in_dim.7
  101.9 8.4 %all-to-all-start.3 = ((f16[16,128,256]{2,1,0:T(8,128)(2,1)}), f16[16,128,256]{2,1,0:T(8,128)(2,1)}, u32[]{:S(2)}, u32[]{:S(2)}) async-start(f16[16,128,256]{2,1,0:T(8,128)(2,1)} %broadcast_in_dim.7), calls=%async_computation.3 | async-start | bytes 2097152 | tf_op jit(solution)/shard_map/all_to_all | solution.py:225
  110.4 2.1 %collective-permute-start.5 = (f32[2,512,128]{2,1,0:T(8,128)}, f32[2,512,128]{2,1,0:T(8,128)S(1)}, u32[]{:S(2)}, u32[]{:S(2)}) collective-permute-start(f32[2,512,128]{2,1,0:T(8,128)} %get-tuple-element.58), channel_id=1, source_target_pairs={{1,0},{2,1},{3,2},{4,3},{5,4},{6,5},{7,6},{9,8},{10,9},{11,10},{12... | collective-permute-start | bytes 1572872 | tf_op jit(solution)/shard_map/ppermute | solution.py:26
  112.5 1.1 slice.132
  113.5 0.9 add_dynamic-update-slice_fusion
  114.4 11.9 %collective-permute-done.5 = f32[2,512,128]{2,1,0:T(8,128)S(1)} collective-permute-done((f32[2,512,128]{2,1,0:T(8,128)}, f32[2,512,128]{2,1,0:T(8,128)S(1)}, u32[]{:S(2)}, u32[]{:S(2)}) %collective-permute-start.5) | collective-permute-done | bytes 524320 | tf_op jit(solution)/shard_map/ppermute | solution.py:26
  126.3 1.9 %fusion = f32[2,512,256]{2,1,0:T(8,128)} fusion(f32[2,512,256]{2,1,0:T(8,128)} %add_dynamic-update-slice_fusion, f32[2,512,128]{2,1,0:T(8,128)S(1)} %collective-permute-done.5), kind=kLoop, calls=%fused_computation.7 | loop fusion | flops 131072 | bytes 1572864 | tf_op jit(solution)/shard_map/scatter-add | solution.py:193
  128.2 1.6 %collective-permute-start.9 = (f16[8,256,256]{2,1,0:T(8,128)(2,1)}, f16[8,256,256]{2,1,0:T(8,128)(2,1)S(1)}, u32[]{:S(2)}, u32[]{:S(2)}) collective-permute-start(f16[8,256,256]{2,1,0:T(8,128)(2,1)} %bitcast.7), channel_id=1, source_target_pairs={{0,1},{1,0},{2,3},{3,2},{4,5},{5,4},{6,7},{7,6},{8,9},{9,8},{10,11... | collective-permute-start | bytes 3145736 | tf_op jit(solution)/shard_map/ppermute | solution.py:230
  129.8 1.1 fusion.6
  130.8 5.9 %collective-permute-start.6 = (f32[2,128,256]{2,1,0:T(8,128)S(1)}, f32[2,128,256]{2,1,0:T(8,128)S(1)}, u32[]{:S(2)}, u32[]{:S(2)}) collective-permute-start(f32[2,128,256]{2,1,0:T(8,128)S(1)} %get-tuple-element.61), channel_id=1, source_target_pairs={{0,8},{8,16},{16,24},{24,32},{32,40},{40,48},{48,56},{56,64},{64,7... | collective-permute-start | bytes 786440 | tf_op jit(solution)/shard_map/ppermute | solution.py:24
  136.7 1.9 %collective-permute-start.7 = (f32[2,128,256]{2,1,0:T(8,128)S(1)}, f32[2,128,256]{2,1,0:T(8,128)S(1)}, u32[]{:S(2)}, u32[]{:S(2)}) collective-permute-start(f32[2,128,256]{2,1,0:T(8,128)S(1)} %get-tuple-element.60), channel_id=1, source_target_pairs={{8,0},{16,8},{24,16},{32,24},{40,32},{48,40},{56,48},{64,56},{72,6... | collective-permute-start | bytes 786440 | tf_op jit(solution)/shard_map/ppermute | solution.py:26
  140.0 1.1 slice.147
  141.1 1.4 collective-permute-done.6
  142.5 1.0 fusion.2
  143.4 6.5 %collective-permute-done.7 = f32[2,128,256]{2,1,0:T(8,128)S(1)} collective-permute-done((f32[2,128,256]{2,1,0:T(8,128)S(1)}, f32[2,128,256]{2,1,0:T(8,128)S(1)}, u32[]{:S(2)}, u32[]{:S(2)}) %collective-permute-start.7) | collective-permute-done | bytes 262176 | tf_op jit(solution)/shard_map/ppermute | solution.py:26
  150.0 0.9 multiply_subtract_fusion.1
  150.8 1.9 %select_bitcast_fusion.1 = (f16[1,8,256,256]{3,2,1,0:T(8,128)(2,1)S(1)}, f16[1,8,256,256]{3,2,1,0:T(8,128)(2,1)S(1)}) fusion(f16[8,256,256]{2,1,0:T(8,128)(2,1)S(1)} %collective-permute-done.9, pred[]{:T(512)S(6)} %eq.9, f16[8,256,256]{2,1,0:T(8,128)(2,1)} %bitcast.18), kind=kLoop, calls=%fused_computation.5 | loop fusion | flops 1048576 | bytes 4194305 | tf_op jit(solution)/shard_map/stack | solution.py:250
  152.8 0.6 copy-done.8
  153.3 2.6 %multiply_subtract_fusion = f32[2,8,256,256]{3,2,1,0:T(8,128)} fusion(f32[2,8,256,256]{3,2,1,0:T(8,128)S(1)} %copy-done.8, f16[1,8,256,256]{3,2,1,0:T(8,128)(2,1)S(1)} %get-tuple-element.57, f16[1,8,256,256]{3,2,1,0:T(8,128)(2,1)S(1)} %get-tuple-element.56, f32[]{:T(128)} %bitcast.10), kind=kLoop, calls=%fused_computation | loop fusion | flops 4194304 | bytes 10485764 | tf_op jit(solution)/shard_map/sub | solution.py:286
  (28 shorter events, 0.3 us)
Async XLA Ops:
  0.6 23.4 %copy-start = (f32[2,256,256]{2,1,0:T(8,128)S(1)}, f32[2,256,256]{2,1,0:T(8,128)}, u32[]{:S(2)}) copy-start(f32[2,256,256]{2,1,0:T(8,128)} %block_ref.1) | copy-start | bytes 1572868
  0.6 17.4 %copy-start.10 = (s32[1,1,2]{2,1,0:T(1,128)S(1)}, s32[1,1,2]{2,1,0:T(1,128)}, u32[]{:S(2)}) copy-start(s32[1,1,2]{2,1,0:T(1,128)} %param.21) | copy-start | bytes 28
  0.7 17.4 %copy-start.11 = (s32[1,1,2]{2,1,0:T(1,128)S(1)}, s32[1,1,2]{2,1,0:T(1,128)}, u32[]{:S(2)}) copy-start(s32[1,1,2]{2,1,0:T(1,128)} %param.20) | copy-start | bytes 28
  0.7 23.3 %copy-start.1 = (f32[1,1,2,256,256]{4,3,2,1,0:T(8,128)S(1)}, f32[1,1,2,256,256]{4,3,2,1,0:T(8,128)}, u32[]{:S(2)}) copy-start(f32[1,1,2,256,256]{4,3,2,1,0:T(8,128)} %param.19) | copy-start | bytes 1572868
  1.9 10.5 %collective-permute-start.1 = (bf16[2,128,256]{2,1,0:T(8,128)(2,1)S(1)}, bf16[2,128,256]{2,1,0:T(8,128)(2,1)S(1)}, u32[]{:S(2)}, u32[]{:S(2)}) collective-permute-start(bf16[2,128,256]{2,1,0:T(8,128)(2,1)S(1)} %get-tuple-element.64), channel_id=1, source_target_pairs={{8,0},{16,8},{24,16},{32,24},{40,32},{48,40},{56,48},{64,56},{72,6... | collective-permute-start | bytes 393224 | tf_op jit(solution)/shard_map/ppermute | solution.py:260
  4.5 9.0 %collective-permute-start = (bf16[2,128,256]{2,1,0:T(8,128)(2,1)S(1)}, bf16[2,128,256]{2,1,0:T(8,128)(2,1)S(1)}, u32[]{:S(2)}, u32[]{:S(2)}) collective-permute-start(bf16[2,128,256]{2,1,0:T(8,128)(2,1)S(1)} %get-tuple-element.65), channel_id=1, source_target_pairs={{0,8},{8,16},{16,24},{24,32},{32,40},{40,48},{48,56},{56,64},{64,7... | collective-permute-start | bytes 393224 | tf_op jit(solution)/shard_map/ppermute | solution.py:259
  13.7 5.8 %collective-permute-start.3 = (bf16[2,512,128]{2,1,0:T(8,128)(2,1)S(1)}, bf16[2,512,128]{2,1,0:T(8,128)(2,1)S(1)}, u32[]{:S(2)}, u32[]{:S(2)}) collective-permute-start(bf16[2,512,128]{2,1,0:T(8,128)(2,1)S(1)} %get-tuple-element.62), channel_id=1, source_target_pairs={{1,0},{2,1},{3,2},{4,3},{5,4},{6,5},{7,6},{9,8},{10,9},{11,10},{12... | collective-permute-start | bytes 786440 | tf_op jit(solution)/shard_map/ppermute | solution.py:260
  15.6 7.7 %collective-permute-start.2 = (bf16[2,512,128]{2,1,0:T(8,128)(2,1)S(1)}, bf16[2,512,128]{2,1,0:T(8,128)(2,1)S(1)}, u32[]{:S(2)}, u32[]{:S(2)}) collective-permute-start(bf16[2,512,128]{2,1,0:T(8,128)(2,1)S(1)} %get-tuple-element.63), channel_id=1, source_target_pairs={{0,1},{1,2},{2,3},{3,4},{4,5},{5,6},{6,7},{8,9},{9,10},{10,11},{11... | collective-permute-start | bytes 786440 | tf_op jit(solution)/shard_map/ppermute | solution.py:259
  19.5 0.7 copy-start.2
  23.3 0.7 copy-start.4
  24.0 1.0 copy-start.3
  24.9 0.9 copy-start.5
  25.9 1.0 copy-start.6
  26.9 1.0 copy-start.7
  49.5 4.7 %copy-start.9 = (f32[8,256,256]{2,1,0:T(8,128)S(1)}, f32[8,256,256]{2,1,0:T(8,128)}, u32[]{:S(2)}) copy-start(f32[8,256,256]{2,1,0:T(8,128)} %get-tuple-element.54) | copy-start | bytes 6291460
  51.5 2.7 %collective-permute-start.8 = (f16[8,256,256]{2,1,0:T(8,128)(2,1)S(1)}, f16[8,256,256]{2,1,0:T(8,128)(2,1)S(1)}, u32[]{:S(2)}, u32[]{:S(2)}) collective-permute-start(f16[8,256,256]{2,1,0:T(8,128)(2,1)S(1)} %multiply_convert_fusion.1), channel_id=1, source_target_pairs={{0,1},{1,0},{2,3},{3,2},{4,5},{5,4},{6,7},{7,6},{8,9},{9,8},{10,11... | collective-permute-start | bytes 3145736 | tf_op jit(solution)/shard_map/ppermute | solution.py:230
  89.0 11.9 %all-to-all-start.2 = ((f16[8,16,256]{2,1,0:T(8,128)(2,1)}), f16[8,16,256]{2,1,0:T(8,128)(2,1)S(1)}, u32[]{:S(2)}, u32[]{:S(2)}) async-start(f16[8,16,256]{2,1,0:T(8,128)(2,1)} %broadcast_in_dim.6), calls=%async_computation.2 | async-start | bytes 131072 | tf_op jit(solution)/shard_map/all_to_all | solution.py:225
  96.9 16.6 %collective-permute-start.4 = (f32[2,512,128]{2,1,0:T(8,128)}, f32[2,512,128]{2,1,0:T(8,128)S(1)}, u32[]{:S(2)}, u32[]{:S(2)}) collective-permute-start(f32[2,512,128]{2,1,0:T(8,128)} %get-tuple-element.59), channel_id=1, source_target_pairs={{0,1},{1,2},{2,3},{3,4},{4,5},{5,6},{6,7},{8,9},{9,10},{10,11},{11... | collective-permute-start | bytes 1572872 | tf_op jit(solution)/shard_map/ppermute | solution.py:24
  101.9 26.3 %all-to-all-start.3 = ((f16[16,128,256]{2,1,0:T(8,128)(2,1)}), f16[16,128,256]{2,1,0:T(8,128)(2,1)}, u32[]{:S(2)}, u32[]{:S(2)}) async-start(f16[16,128,256]{2,1,0:T(8,128)(2,1)} %broadcast_in_dim.7), calls=%async_computation.3 | async-start | bytes 2097152 | tf_op jit(solution)/shard_map/all_to_all | solution.py:225
  110.4 15.9 %collective-permute-start.5 = (f32[2,512,128]{2,1,0:T(8,128)}, f32[2,512,128]{2,1,0:T(8,128)S(1)}, u32[]{:S(2)}, u32[]{:S(2)}) collective-permute-start(f32[2,512,128]{2,1,0:T(8,128)} %get-tuple-element.58), channel_id=1, source_target_pairs={{1,0},{2,1},{3,2},{4,3},{5,4},{6,5},{7,6},{9,8},{10,9},{11,10},{12... | collective-permute-start | bytes 1572872 | tf_op jit(solution)/shard_map/ppermute | solution.py:26
  128.2 22.6 %collective-permute-start.9 = (f16[8,256,256]{2,1,0:T(8,128)(2,1)}, f16[8,256,256]{2,1,0:T(8,128)(2,1)S(1)}, u32[]{:S(2)}, u32[]{:S(2)}) collective-permute-start(f16[8,256,256]{2,1,0:T(8,128)(2,1)} %bitcast.7), channel_id=1, source_target_pairs={{0,1},{1,0},{2,3},{3,2},{4,5},{5,4},{6,7},{7,6},{8,9},{9,8},{10,11... | collective-permute-start | bytes 3145736 | tf_op jit(solution)/shard_map/ppermute | solution.py:230
  130.8 11.6 %collective-permute-start.6 = (f32[2,128,256]{2,1,0:T(8,128)S(1)}, f32[2,128,256]{2,1,0:T(8,128)S(1)}, u32[]{:S(2)}, u32[]{:S(2)}) collective-permute-start(f32[2,128,256]{2,1,0:T(8,128)S(1)} %get-tuple-element.61), channel_id=1, source_target_pairs={{0,8},{8,16},{16,24},{24,32},{32,40},{40,48},{48,56},{56,64},{64,7... | collective-permute-start | bytes 786440 | tf_op jit(solution)/shard_map/ppermute | solution.py:24
  136.7 13.1 %collective-permute-start.7 = (f32[2,128,256]{2,1,0:T(8,128)S(1)}, f32[2,128,256]{2,1,0:T(8,128)S(1)}, u32[]{:S(2)}, u32[]{:S(2)}) collective-permute-start(f32[2,128,256]{2,1,0:T(8,128)S(1)} %get-tuple-element.60), channel_id=1, source_target_pairs={{8,0},{16,8},{24,16},{32,24},{40,32},{48,40},{56,48},{64,56},{72,6... | collective-permute-start | bytes 786440 | tf_op jit(solution)/shard_map/ppermute | solution.py:26
  150.8 2.5 %copy-start.8 = (f32[2,8,256,256]{3,2,1,0:T(8,128)S(1)}, f32[2,8,256,256]{3,2,1,0:T(8,128)}, u32[]{:S(2)}) copy-start(f32[2,8,256,256]{3,2,1,0:T(8,128)} %probe_ref.1) | copy-start | bytes 12582916
where the time goes:
time: 157 us; the launch traced here: 156 us
  starting transfers between devices  42.3 us (27%)
  blocking collectives  33.4 us (21%)
  waiting for transfers between devices  31.3 us (20%)
  Pallas kernels  21.6 us (14%)
  other arithmetic  13.1 us (8%)
  local copies, waits for them, and re-layouts  12.1 us (8%)
  between operations  2.15 us (1%)
    all_to_all x2, blocking collectives, exchange(): lax.all_to_all(parts, ('region', 'scan'), 0, 0, axis_index_groups=axis_gr...  33.4 us
    pallas_call x1, Pallas kernels, device_gradients(): pl.pallas_call(gradients_kernel, out_shape=(jax.ShapeDtypeStruct((2, rows...  21.6 us
    ppermute x2, waiting for transfers between devices, padded_2(): lax.ppermute(head, axis, [((i + 1) % count, i) for i in range(ends)])  18.3 us
    all_to_all x2, starting transfers between devices, exchange(): lax.all_to_all(parts, ('region', 'scan'), 0, 0, axis_index_groups=axis_gr...  15.3 us
    ppermute x2, starting transfers between devices, edges(): lax.ppermute(tail, axis, [(i, (i + 1) % count) for i in range(ends)])  8.92 us
    ppermute x2, starting transfers between devices, padded_2(): lax.ppermute(tail, axis, [(i, (i + 1) % count) for i in range(ends)])  7.81 us
    unnamed x24, local copies, waits for them, and re-layouts  5.99 us
    ppermute x2, starting transfers between devices, edges(): lax.ppermute(head, axis, [((i + 1) % count, i) for i in range(ends)])  4.57 us
  transfers between devices with their start and end apart: 12, of which 9 were waited for; matrix products, arithmetic and copies ran while one was open for 7% of the time, Pallas kernels for 0%

commit v1 on v0

v1 whole, which is shorter than its diff:
```python
import math

import jax
import jax.numpy as jnp
import ml_dtypes
import numpy as np
from jax import lax
from jax.experimental import pallas as pl
from jax.experimental.pallas import tpu as pltpu
from jax.sharding import PartitionSpec as P


UNROLL = 8
GRANT = 52


def padded_2(cells, sides, width):
    for axis, dim in sides:
        count = lax.axis_size(axis)
        ends = count - 1
        head = lax.slice_in_dim(cells, 0, width, axis=dim)
        tail = lax.slice_in_dim(cells, cells.shape[dim] - width, cells.shape[dim], axis=dim)
        cells = jnp.concatenate(
            [
                lax.ppermute(tail, axis, [(i, (i + 1) % count) for i in range(ends)]),
                cells,
                lax.ppermute(head, axis, [((i + 1) % count, i) for i in range(ends)]),
            ],
            axis=dim,
        )
    return cells


def fourier_blocks(length):
    position = np.arange(length)
    angles = (position[:, None] * position[None, :] % length) * (2.0 * math.pi / length)
    table_scale = 1.0 / math.sqrt(length)
    cosine_table = (np.cos(angles) * table_scale).astype(ml_dtypes.bfloat16)
    sine_table = (np.sin(angles) * table_scale).astype(ml_dtypes.bfloat16)
    forward = np.block([[cosine_table, sine_table], [-sine_table, cosine_table]])
    return (jnp.asarray(forward), jnp.asarray(np.ascontiguousarray(forward.T)))


def fourier_pass(wide, left, right):
    length = wide.shape[0] // 2
    middle = jnp.dot(left, wide, preferred_element_type=jnp.float32).astype(jnp.bfloat16)
    middle = jnp.concatenate(
        [
            jnp.concatenate([middle[:length, cut], middle[length:, cut]], axis=1)
            for cut in (slice(i, i + length) for i in range(0, wide.shape[1], length))
        ],
        axis=0,
    )
    return jnp.dot(middle, right, preferred_element_type=jnp.float32)


def stacked(pairs):
    return jnp.concatenate(
        [jnp.concatenate(pair, axis=0).astype(jnp.bfloat16) for pair in pairs], axis=1
    )


def gradients_kernel(
    place_ref,
    block_hbm,
    above_hbm,
    below_hbm,
    left_hbm,
    right_hbm,
    probe_hbm,
    pattern_hbm,
    forward_hbm,
    backward_hbm,
    rim_left_hbm,
    center_hbm,
    rim_right_hbm,
    mine_hbm,
    other_hbm,
    block_ref,
    above_ref,
    below_ref,
    left_ref,
    right_ref,
    probe_ref,
    pattern_ref,
    forward_ref,
    backward_ref,
    rim_left_ref,
    center_ref,
    rim_right_ref,
    mine_ref,
    other_ref,
    padded_ref,
    window_ref,
    far_ref,
    level_ref,
    object_ref,
    probe_sem,
    piece_sem,
    mine_sem,
    other_sem,
    grad_sem,
):
    modes, length = probe_ref.shape[1], probe_ref.shape[2]
    half = length // 2
    rows, cols = block_ref.shape[1], block_ref.shape[2]
    wide = padded_ref.shape[2]
    slots = pattern_ref.shape[0]

    def fetch_probe(mode):
        return pltpu.make_async_copy(
            probe_hbm.at[:, mode], probe_ref.at[:, mode], probe_sem.at[mode]
        )

    def send_mine(mode):
        return pltpu.make_async_copy(mine_ref.at[mode], mine_hbm.at[mode], mine_sem.at[mode])

    def send_other(mode):
        return pltpu.make_async_copy(other_ref.at[mode], other_hbm.at[mode], other_sem.at[mode])

    fetches = [
        pltpu.make_async_copy(source, target, piece_sem.at[index])
        for index, (source, target) in enumerate(
            (
                (left_hbm, left_ref),
                (right_hbm, right_ref),
                (above_hbm, above_ref),
                (below_hbm, below_ref),
                (block_hbm, block_ref),
                (forward_hbm, forward_ref),
                (backward_hbm, backward_ref),
                (pattern_hbm, pattern_ref),
            )
        )
    ]
    for fetch in fetches:
        fetch.start()
    for mode in range(modes):
        fetch_probe(mode).start()
    for part_ref in (rim_left_ref, center_ref, rim_right_ref, level_ref, object_ref):
        part_ref[...] = jnp.zeros_like(part_ref)
    for fetch in fetches[:5]:
        fetch.wait()
    padded_ref[:, :, :half] = left_ref[...].astype(jnp.float32)
    padded_ref[:, :, half + cols :] = right_ref[...].astype(jnp.float32)
    padded_ref[:, :half, half : half + cols] = above_ref[...].astype(jnp.float32)
    padded_ref[:, half + rows :, half : half + cols] = below_ref[...].astype(jnp.float32)
    padded_ref[:, half : half + rows, half : half + cols] = (
        block_ref[...].astype(jnp.bfloat16).astype(jnp.float32)
    )
    first = place_ref[2, 0] == 0
    places = []
    for slot in range(slots):
        row, col = place_ref[0, slot], place_ref[1, slot]
        shift = row % 8
        span = pl.ds(pl.multiple_of(row - shift, 8), length + 8)
        places.append((span, shift, col))
        for part in range(2):
            strip = pltpu.roll(padded_ref[part, span, :], wide - col, 1)[:, :length]
            window_ref[slot, part] = pltpu.roll(strip, length + 8 - shift, 0)[:length]
    for fetch in fetches[5:]:
        fetch.wait()

    def go_forward(mode, carry):
        fetch_probe(mode).wait()
        probe_real, probe_imag = probe_ref[0, mode], probe_ref[1, mode]
        waves = []
        for slot in range(slots):
            win_real, win_imag = window_ref[slot, 0], window_ref[slot, 1]
            waves.append(
                (
                    probe_real * win_real - probe_imag * win_imag,
                    probe_real * win_imag + probe_imag * win_real,
                )
            )
        far = fourier_pass(stacked(waves), forward_ref[...], backward_ref[...])
        far_ref[mode] = far
        far_real, far_imag = far[:, :length], far[:, length:]
        level_ref[...] += far_real * far_real + far_imag * far_imag
        return carry

    lax.fori_loop(0, modes, go_forward, 0, unroll=UNROLL)
    amplitude = jnp.maximum(jnp.sqrt(level_ref[...]), 1.0)
    targets = jnp.concatenate([pattern_ref[slot] for slot in range(slots)], axis=0)
    level_ref[...] = 1.0 - jnp.sqrt(targets) / amplitude

    def go_back(mode, carry):
        corrected = []
        for slot in range(slots):
            band = slice(slot * length, (slot + 1) * length)
            factor = level_ref[band]
            far = far_ref[mode, band]
            corrected.append((factor * far[:, :length], factor * far[:, length:]))
        back = fourier_pass(stacked(corrected), backward_ref[...], forward_ref[...])
        probe_real, probe_imag = probe_ref[0, mode], probe_ref[1, mode]
        term_real = term_imag = 0.0
        for slot in range(slots):
            band = slice(slot * length, (slot + 1) * length)
            back_real, back_imag = back[band, :length], back[band, length:]
            object_ref[slot, 0] += probe_real * back_real + probe_imag * back_imag
            object_ref[slot, 1] += probe_real * back_imag - probe_imag * back_real
            win_real, win_imag = window_ref[slot, 0], window_ref[slot, 1]
            term_real += win_real * back_real + win_imag * back_imag
            term_imag += win_real * back_imag - win_imag * back_real
        mine_ref[mode] = jnp.where(first, term_real, term_imag)
        other_ref[mode] = jnp.where(first, term_imag, term_real)
        send_other(mode).start()
        send_mine(mode).start()
        return carry

    lax.fori_loop(0, modes, go_back, 0, unroll=UNROLL)
    for slot in range(slots):
        span, shift, col = places[slot]
        for part in range(2):
            strip = jnp.concatenate(
                [object_ref[slot, part], jnp.zeros((8, length), jnp.float32)], axis=0
            )
            strip = pltpu.roll(strip, shift, 0)
            strip = jnp.concatenate(
                [strip, jnp.zeros((length + 8, wide - length), jnp.float32)], axis=1
            )
            strip = pltpu.roll(strip, col, 1)
            rim_left_ref[part, span, :] += strip[:, :half]
            center_ref[part, span, :] += strip[:, half : half + cols]
            rim_right_ref[part, span, :] += strip[:, half + cols :]
    sends = [
        pltpu.make_async_copy(source, target, grad_sem.at[index])
        for index, (source, target) in enumerate(
            (
                (rim_left_ref, rim_left_hbm),
                (center_ref, center_hbm),
                (rim_right_ref, rim_right_hbm),
            )
        )
    ]
    for send in sends:
        send.start()
    for mode in range(modes):
        send_other(mode).wait()
        send_mine(mode).wait()
    for send in sends:
        send.wait()


def device_gradients(place, block, above, below, left, right, probe, pattern):
    forward, backward = fourier_blocks(probe.shape[-1])
    _, modes, length, _ = probe.shape
    rows, cols = block.shape[1] + length, block.shape[2] + length
    slots = pattern.shape[0]
    anywhere = pl.BlockSpec(memory_space=pl.ANY)
    f32 = jnp.float32
    fetched = (block, above, below, left, right, probe, pattern, forward, backward)
    made = (
        jax.ShapeDtypeStruct((2, rows, length // 2), f32),
        jax.ShapeDtypeStruct((2, rows, block.shape[2]), f32),
        jax.ShapeDtypeStruct((2, rows, length // 2), f32),
        jax.ShapeDtypeStruct((modes, length, length), f32),
        jax.ShapeDtypeStruct((modes, length, length), f32),
    )
    return pl.pallas_call(
        gradients_kernel,
        out_shape=made,
        in_specs=[pl.BlockSpec(memory_space=pltpu.SMEM)] + [anywhere] * len(fetched),
        out_specs=(anywhere,) * len(made),
        scratch_shapes=[pltpu.VMEM(item.shape, item.dtype) for item in fetched + made]
        + [
            pltpu.VMEM((2, rows, cols), f32),
            pltpu.VMEM((slots, 2, length, length), f32),
            pltpu.VMEM((modes, slots * length, 2 * length), f32),
            pltpu.VMEM((slots * length, length), f32),
            pltpu.VMEM((slots, 2, length, length), f32),
            pltpu.SemaphoreType.DMA((modes,)),
            pltpu.SemaphoreType.DMA((8,)),
            pltpu.SemaphoreType.DMA((modes,)),
            pltpu.SemaphoreType.DMA((modes,)),
            pltpu.SemaphoreType.DMA((3,)),
        ],
        compiler_params=pltpu.CompilerParams(vmem_limit_bytes=GRANT * 1024 * 1024),
        cost_estimate=pl.CostEstimate(
            flops=slots * modes * 32 * length**3, bytes_accessed=16 * 2**20, transcendentals=0
        ),
    )(place, *fetched)


def axis_groups(kept):
    rows, cols = lax.axis_size("region"), lax.axis_size("scan")
    sizes = {"core": 2, "x": cols // 2, "y": 4, "pair": 2, "far": rows // 8}
    groups = {}
    for device in range(rows * cols):
        place, rest = {}, device
        for name in sizes:
            place[name] = rest % sizes[name]
            rest = rest // sizes[name]
        key = tuple(place[name] for name in place if name not in kept)
        groups.setdefault(key, []).append(device)
    return [groups[key] for key in sorted(groups)]


def narrow(values, scale):
    return (values * (1.0 / scale)).astype(jnp.float16)


def widen(values, scale):
    return values.astype(jnp.float32) * scale


def exchange(parts, kept):
    return lax.all_to_all(parts, ("region", "scan"), 0, 0, axis_index_groups=axis_groups(kept))


def swap_cores(values):
    count = lax.axis_size("region") * lax.axis_size("scan")
    return lax.ppermute(values, ("region", "scan"), [(i, i ^ 1) for i in range(count)])


def shift_far(values, step):
    cols = lax.axis_size("scan")
    count = lax.axis_size("region") * cols
    stride = 8 * cols
    pairs = [(i, (i + step * stride) % count) for i in range(count)]
    return lax.ppermute(values, ("region", "scan"), pairs)


def sum_scattered(mine, other):
    modes, rows, cols = mine.shape
    pair = mine + widen(swap_cores(narrow(other, 8.0)), 8.0)
    places = 8 * (lax.axis_size("scan") // 2)
    pieces = narrow(pair, 16.0).reshape(places, modes * rows // places, cols)
    pieces = exchange(pieces, ("pair", "y", "x"))
    return jnp.sum(widen(pieces, 16.0), axis=0)


def sum_far(piece):
    sent = narrow(piece, 512.0)
    one, two, three = (widen(shift_far(sent, step), 512.0) for step in (1, 2, 3))
    return (widen(sent, 512.0) + two) + (one + three)


def gather_sum(total, modes):
    rows, cols = total.shape
    places = 8 * (lax.axis_size("scan") // 2)
    pieces = jnp.broadcast_to(narrow(total, 2048.0), (places, rows, cols))
    return exchange(pieces, ("pair", "y", "x")).reshape(modes, -1, cols)


def neighbours(head, tail, axis):
    count = lax.axis_size(axis)
    ends = count - 1
    before = lax.ppermute(tail, axis, [(i, (i + 1) % count) for i in range(ends)])
    after = lax.ppermute(head, axis, [((i + 1) % count, i) for i in range(ends)])
    return (before, after)


def edges(cells, axis, dim, width):
    head = lax.slice_in_dim(cells, 0, width, axis=dim)
    tail = lax.slice_in_dim(cells, cells.shape[dim] - width, cells.shape[dim], axis=dim)
    return neighbours(head, tail, axis)


def trade(head, tail, axis):
    return neighbours(narrow(head, 64.0), narrow(tail, 64.0), axis)


def on_device(object_field, probe_modes, pattern, rows_at, cols_at, object_step, probe_step):
    half_width = probe_modes.shape[-1] // 2
    block_rows = object_field.shape[1]
    block_cols = object_field.shape[2]
    core = lax.axis_index("scan") % 2
    place = jnp.stack(
        [
            rows_at[0, 0] % block_rows,
            cols_at[0, 0] % block_cols,
            jnp.broadcast_to(core, rows_at.shape[2:]).astype(jnp.int32),
        ]
    )
    cells = object_field.astype(jnp.bfloat16)
    above, below = edges(cells, "region", 1, half_width)
    tall = jnp.concatenate([above, cells, below], axis=1)
    left, right = edges(tall, "scan", 2, half_width)
    rim_left, center, rim_right, mine, other = device_gradients(
        place, object_field, above, below, left, right, probe_modes, pattern[0, 0]
    )
    piece = sum_scattered(mine, other)
    from_left, from_right = trade(rim_left, rim_right, "scan")
    center = center + widen(jnp.concatenate([from_left, from_right], axis=2), 64.0)
    piece, center = lax.optimization_barrier((piece, center))
    total = sum_far(piece)
    total, center = lax.optimization_barrier((total, center))
    from_above, from_below = trade(center[:, :half_width], center[:, -half_width:], "region")
    plane = gather_sum(total, probe_modes.shape[1])
    plane, from_above, from_below = lax.optimization_barrier((plane, from_above, from_below))
    swapped = swap_cores(plane)
    inner = center[:, half_width:-half_width]
    inner = inner + widen(jnp.concatenate([from_above, from_below], axis=1), 64.0)
    object_field = object_field - object_step[0] * inner
    own = lax.broadcasted_iota(jnp.int32, probe_modes.shape, 0) == core
    probe_total = widen(jnp.where(own, plane[None], swapped[None]), 2048.0)
    probe_modes = probe_modes - probe_step[0] * probe_total
    return (object_field, probe_modes)


def solution(mesh):
    return jax.shard_map(
        on_device,
        mesh=mesh,
        in_specs=(
            P(None, "region", "scan"),
            P(),
            P("region", "scan", None, None, None),
            P("region", "scan", None),
            P("region", "scan", None),
            P(),
            P(),
        ),
        out_specs=(P(None, "region", "scan"), P()),
        check_vma=False,
    )
```

time: 157 us -> 120 us (0.76)
  the two profiles are of different devices: /device:TPU:124 before, /device:TPU:33 now
where the time goes in v1:
time: 120 us
  starting transfers between devices  50.8 us (42%)
  waiting for transfers between devices  36.2 us (30%)
  Pallas kernels  18.4 us (15%)
  other arithmetic  11 us (9%)
  between operations  2.2 us (2%)
  local copies, waits for them, and re-layouts  1.3 us (1%)
    ppermute x4, waiting for transfers between devices, neighbours(): lax.ppermute(head, axis, [((i + 1) % count, i) for i in range(ends)])  24.6 us
    pallas_call x1, Pallas kernels, device_gradients(): pl.pallas_call(gradients_kernel, out_shape=made, in_specs=[pl.BlockSpec(m...  18.4 us
    ppermute x4, starting transfers between devices, neighbours(): lax.ppermute(head, axis, [((i + 1) % count, i) for i in range(ends)])  15.3 us
    all_to_all x2, starting transfers between devices, exchange(): lax.all_to_all(parts, ('region', 'scan'), 0, 0, axis_index_groups=axis_gr...  13.3 us
    ppermute x3, starting transfers between devices, shift_far(): return lax.ppermute(values, ('region', 'scan'), pairs)  10.6 us
    ppermute x4, starting transfers between devices, neighbours(): lax.ppermute(tail, axis, [(i, (i + 1) % count) for i in range(ends)])  9.85 us
    ppermute x4, waiting for transfers between devices, neighbours(): lax.ppermute(tail, axis, [(i, (i + 1) % count) for i in range(ends)])  6.87 us
    sub x1, other arithmetic, on_device(): probe_modes = probe_modes - probe_step[0] * probe_total  4.96 us
  transfers between devices with their start and end apart: 15, of which 9 were waited for; matrix products, arithmetic and copies ran while one was open for 1% of the time, Pallas kernels for 0%

profile of v1, /device:TPU:33, one launch (start us, length us, event | category | flops | bytes accessed | tf_op | source)
XLA Modules:
  0.0 119.9 jit_solution(1624065282833191821)
XLA Ops:
  0.6 1.1 convert_element_type.54
  1.8 4.2 %collective-permute-start.1 = (bf16[2,128,256]{2,1,0:T(8,128)(2,1)S(1)}, bf16[2,128,256]{2,1,0:T(8,128)(2,1)S(1)}, u32[]{:S(2)}, u32[]{:S(2)}) collective-permute-start(bf16[2,128,256]{2,1,0:T(8,128)(2,1)S(1)} %get-tuple-element.30), channel_id=1, source_target_pairs={{8,0},{16,8},{24,16},{32,24},{40,32},{48,40},{56,48},{64,56},{72,6... | collective-permute-start | bytes 393224 | tf_op jit(solution)/shard_map/ppermute | solution.py:350
  6.0 1.9 %collective-permute-start = (bf16[2,128,256]{2,1,0:T(8,128)(2,1)S(1)}, bf16[2,128,256]{2,1,0:T(8,128)(2,1)S(1)}, u32[]{:S(2)}, u32[]{:S(2)}) collective-permute-start(bf16[2,128,256]{2,1,0:T(8,128)(2,1)S(1)} %get-tuple-element.31), channel_id=1, source_target_pairs={{0,8},{8,16},{16,24},{24,32},{32,40},{40,48},{48,56},{56,64},{64,7... | collective-permute-start | bytes 393224 | tf_op jit(solution)/shard_map/ppermute | solution.py:349
  7.9 0.2 collective-permute-done.1.below_hbm
  8.1 5.7 %collective-permute-done.above_hbm = bf16[2,128,256]{2,1,0:T(8,128)(2,1)S(1)} collective-permute-done((bf16[2,128,256]{2,1,0:T(8,128)(2,1)S(1)}, bf16[2,128,256]{2,1,0:T(8,128)(2,1)S(1)}, u32[]{:S(2)}, u32[]{:S(2)}) %collective-permute-start) | collective-permute-done | bytes 131104 | tf_op jit(solution)/shard_map/ppermute | solution.py:349
  13.8 0.1 fusion.2
  13.9 4.0 %collective-permute-start.3 = (bf16[2,512,128]{2,1,0:T(8,128)(2,1)S(1)}, bf16[2,512,128]{2,1,0:T(8,128)(2,1)S(1)}, u32[]{:S(2)}, u32[]{:S(2)}) collective-permute-start(bf16[2,512,128]{2,1,0:T(8,128)(2,1)S(1)} %get-tuple-element.28), channel_id=1, source_target_pairs={{1,0},{2,1},{3,2},{4,3},{5,4},{6,5},{7,6},{9,8},{10,9},{11,10},{12... | collective-permute-start | bytes 786440 | tf_op jit(solution)/shard_map/ppermute | solution.py:350
  17.9 3.0 %collective-permute-start.2 = (bf16[2,512,128]{2,1,0:T(8,128)(2,1)S(1)}, bf16[2,512,128]{2,1,0:T(8,128)(2,1)S(1)}, u32[]{:S(2)}, u32[]{:S(2)}) collective-permute-start(bf16[2,512,128]{2,1,0:T(8,128)(2,1)S(1)} %get-tuple-element.29), channel_id=1, source_target_pairs={{0,1},{1,2},{2,3},{3,4},{4,5},{5,6},{6,7},{8,9},{9,10},{10,11},{11... | collective-permute-start | bytes 786440 | tf_op jit(solution)/shard_map/ppermute | solution.py:349
  21.0 0.0 copy-done.3
  21.0 0.1 pad.9.clone
  21.1 0.1 add_add_fusion.place_ref
  21.2 1.9 %collective-permute-done.3.right_hbm = bf16[2,512,128]{2,1,0:T(8,128)(2,1)S(1)} collective-permute-done((bf16[2,512,128]{2,1,0:T(8,128)(2,1)S(1)}, bf16[2,512,128]{2,1,0:T(8,128)(2,1)S(1)}, u32[]{:S(2)}, u32[]{:S(2)}) %collective-permute-start.3) | collective-permute-done | bytes 262176 | tf_op jit(solution)/shard_map/ppermute | solution.py:350
  23.1 1.2 collective-permute-done.2.left_hbm
  24.3 18.4 %shard_map.104 = (f32[2,512,128]{2,1,0:T(8,128)S(1)}, f32[2,512,256]{2,1,0:T(8,128)}, f32[2,512,128]{2,1,0:T(8,128)S(1)}, f32[8,256,256]{2,1,0:T(8,128)}, f32[8,256,256]{2,1,0:T(8,128)}) custom-call(s32[3,2]{1,0:T(4,128)S(1)} %add_add_fusion.place_ref, f32[2,256,256]{2,1,0:T(8,128)} %block_hbm.1, bf16[2,128,256]{2,1,0:T(8,128)(2,1)S(1)} %collective-permute-done.above_hbm, ...), custom_call_target="tpu_custom_call" | custom-call | flops 8589934592 | bytes 16777216 | tf_op jit(solution)/shard_map/pallas_call | solution.py:260
  42.7 0.0 copy-start
  42.7 2.0 %multiply_convert_fusion.1 = f16[8,256,256]{2,1,0:T(8,128)(2,1)S(1)} fusion(f32[8,256,256]{2,1,0:T(8,128)} %get-tuple-element.15), kind=kLoop, calls=%fused_computation.3 | loop fusion | flops 1048576 | bytes 3145728 | tf_op jit(solution)/shard_map/convert_element_type | solution.py:300
  44.7 0.1 collective-permute-start.4
  44.8 2.6 %collective-permute-done.4 = f16[8,256,256]{2,1,0:T(8,128)(2,1)S(1)} collective-permute-done((f16[8,256,256]{2,1,0:T(8,128)(2,1)S(1)}, f16[8,256,256]{2,1,0:T(8,128)(2,1)S(1)}, u32[]{:S(2)}, u32[]{:S(2)}) %collective-permute-start.4) | collective-permute-done | bytes 1048608 | tf_op jit(solution)/shard_map/ppermute | solution.py:313
  47.4 1.4 %multiply_convert_fusion = f16[8,256,256]{2,1,0:T(8,128)(2,1)} fusion(f32[8,256,256]{2,1,0:T(8,128)S(1)} %copy-done, f16[8,256,256]{2,1,0:T(8,128)(2,1)S(1)} %collective-permute-done.4), kind=kLoop, calls=%fused_computation.2 | loop fusion | flops 2621440 | bytes 4194304 | tf_op jit(solution)/shard_map/convert_element_type | solution.py:300
  48.8 6.5 %all-to-all-start = ((f16[32,64,256]{2,1,0:T(8,128)(2,1)}), f16[32,64,256]{2,1,0:T(8,128)(2,1)S(1)}, u32[]{:S(2)}, u32[]{:S(2)}) async-start(f16[32,64,256]{2,1,0:T(8,128)(2,1)} %bitcast.4), calls=%async_computation | async-start | bytes 2097152 | tf_op jit(solution)/shard_map/all_to_all | solution.py:308
  55.3 0.1 multiply_convert_fusion.3
  55.4 0.1 multiply_convert_fusion.2
  55.5 2.8 %collective-permute-start.6 = (f16[2,512,128]{2,1,0:T(8,128)(2,1)S(1)}, f16[2,512,128]{2,1,0:T(8,128)(2,1)S(1)}, u32[]{:S(2)}, u32[]{:S(2)}) collective-permute-start(f16[2,512,128]{2,1,0:T(8,128)(2,1)S(1)} %multiply_convert_fusion.2), channel_id=1, source_target_pairs={{1,0},{2,1},{3,2},{4,3},{5,4},{6,5},{7,6},{9,8},{10,9},{11,10},{12... | collective-permute-start | bytes 786440 | tf_op jit(solution)/shard_map/ppermute | solution.py:350
  58.3 3.0 %collective-permute-start.5 = (f16[2,512,128]{2,1,0:T(8,128)(2,1)S(1)}, f16[2,512,128]{2,1,0:T(8,128)(2,1)S(1)}, u32[]{:S(2)}, u32[]{:S(2)}) collective-permute-start(f16[2,512,128]{2,1,0:T(8,128)(2,1)S(1)} %multiply_convert_fusion.3), channel_id=1, source_target_pairs={{0,1},{1,2},{2,3},{3,4},{4,5},{5,6},{6,7},{8,9},{9,10},{10,11},{11... | collective-permute-start | bytes 786440 | tf_op jit(solution)/shard_map/ppermute | solution.py:349
  61.3 10.6 %collective-permute-done.6 = f16[2,512,128]{2,1,0:T(8,128)(2,1)S(1)} collective-permute-done((f16[2,512,128]{2,1,0:T(8,128)(2,1)S(1)}, f16[2,512,128]{2,1,0:T(8,128)(2,1)S(1)}, u32[]{:S(2)}, u32[]{:S(2)}) %collective-permute-start.6) | collective-permute-done | bytes 262176 | tf_op jit(solution)/shard_map/ppermute | solution.py:350
  71.9 0.0 collective-permute-done.5
  71.9 0.2 multiply_add_fusion
  72.1 0.0 all-to-all-done
  72.1 0.2 multiply_reduce_fusion
  72.3 0.0 copy-start.1
  72.3 3.8 %collective-permute-start.8 = (f16[64,256]{1,0:T(8,128)(2,1)S(1)}, f16[64,256]{1,0:T(8,128)(2,1)S(1)}, u32[]{:S(2)}, u32[]{:S(2)}) collective-permute-start(f16[64,256]{1,0:T(8,128)(2,1)S(1)} %multiply_convert_fusion.7), channel_id=1, source_target_pairs={{0,64},{1,65},{2,66},{3,67},{4,68},{5,69},{6,70},{7,71},{8,72},{9,... | collective-permute-start | bytes 98312 | tf_op jit(solution)/shard_map/ppermute | solution.py:321
  76.1 4.4 %collective-permute-start.7 = (f16[64,256]{1,0:T(8,128)(2,1)S(1)}, f16[64,256]{1,0:T(8,128)(2,1)S(1)}, u32[]{:S(2)}, u32[]{:S(2)}) collective-permute-start(f16[64,256]{1,0:T(8,128)(2,1)S(1)} %multiply_convert_fusion.7), channel_id=1, source_target_pairs={{0,128},{1,129},{2,130},{3,131},{4,132},{5,133},{6,134},{7,135},{8... | collective-permute-start | bytes 98312 | tf_op jit(solution)/shard_map/ppermute | solution.py:321
  80.5 2.4 %collective-permute-start.9 = (f16[64,256]{1,0:T(8,128)(2,1)S(1)}, f16[64,256]{1,0:T(8,128)(2,1)S(1)}, u32[]{:S(2)}, u32[]{:S(2)}) collective-permute-start(f16[64,256]{1,0:T(8,128)(2,1)S(1)} %multiply_convert_fusion.7), channel_id=1, source_target_pairs={{0,192},{1,193},{2,194},{3,195},{4,196},{5,197},{6,198},{7,199},{8... | collective-permute-start | bytes 98312 | tf_op jit(solution)/shard_map/ppermute | solution.py:321
  82.9 0.0 collective-permute-done.8
  82.9 0.0 collective-permute-done.7
  82.9 2.0 %collective-permute-done.9 = f16[64,256]{1,0:T(8,128)(2,1)S(1)} collective-permute-done((f16[64,256]{1,0:T(8,128)(2,1)S(1)}, f16[64,256]{1,0:T(8,128)(2,1)S(1)}, u32[]{:S(2)}, u32[]{:S(2)}) %collective-permute-start.9) | collective-permute-done | bytes 32800 | tf_op jit(solution)/shard_map/ppermute | solution.py:321
  84.9 1.1 broadcast_in_dim.21
  86.0 6.8 %all-to-all-start.1 = ((f16[32,64,256]{2,1,0:T(8,128)(2,1)}), f16[32,64,256]{2,1,0:T(8,128)(2,1)S(1)}, u32[]{:S(2)}, u32[]{:S(2)}) async-start(f16[32,64,256]{2,1,0:T(8,128)(2,1)} %broadcast_in_dim.21), calls=%async_computation.1 | async-start | bytes 2097152 | tf_op jit(solution)/shard_map/all_to_all | solution.py:308
  92.8 0.1 multiply_convert_fusion.4
  92.9 4.3 %collective-permute-start.11 = (f16[2,128,256]{2,1,0:T(8,128)(2,1)S(1)}, f16[2,128,256]{2,1,0:T(8,128)(2,1)S(1)}, u32[]{:S(2)}, u32[]{:S(2)}) collective-permute-start(f16[2,128,256]{2,1,0:T(8,128)(2,1)S(1)} %get-tuple-element.26), channel_id=1, source_target_pairs={{8,0},{16,8},{24,16},{32,24},{40,32},{48,40},{56,48},{64,56},{72,6... | collective-permute-start | bytes 393224 | tf_op jit(solution)/shard_map/ppermute | solution.py:350
  97.2 1.9 %collective-permute-start.10 = (f16[2,128,256]{2,1,0:T(8,128)(2,1)S(1)}, f16[2,128,256]{2,1,0:T(8,128)(2,1)S(1)}, u32[]{:S(2)}, u32[]{:S(2)}) collective-permute-start(f16[2,128,256]{2,1,0:T(8,128)(2,1)S(1)} %get-tuple-element.27), channel_id=1, source_target_pairs={{0,8},{8,16},{16,24},{24,32},{32,40},{40,48},{48,56},{56,64},{64,7... | collective-permute-start | bytes 393224 | tf_op jit(solution)/shard_map/ppermute | solution.py:349
  99.1 11.9 %collective-permute-done.11 = f16[2,128,256]{2,1,0:T(8,128)(2,1)S(1)} collective-permute-done((f16[2,128,256]{2,1,0:T(8,128)(2,1)S(1)}, f16[2,128,256]{2,1,0:T(8,128)(2,1)S(1)}, u32[]{:S(2)}, u32[]{:S(2)}) %collective-permute-start.11) | collective-permute-done | bytes 131104 | tf_op jit(solution)/shard_map/ppermute | solution.py:350
  111.0 0.0 collective-permute-done.10
  111.0 0.0 all-to-all-done.1
  111.0 1.6 %collective-permute-start.12 = (f16[8,256,256]{2,1,0:T(8,128)(2,1)S(1)}, f16[8,256,256]{2,1,0:T(8,128)(2,1)S(1)}, u32[]{:S(2)}, u32[]{:S(2)}) collective-permute-start(f16[8,256,256]{2,1,0:T(8,128)(2,1)S(1)} %bitcast.11), channel_id=1, source_target_pairs={{0,1},{1,0},{2,3},{3,2},{4,5},{5,4},{6,7},{7,6},{8,9},{9,8},{10,11... | collective-permute-start | bytes 3145736 | tf_op jit(solution)/shard_map/ppermute | solution.py:313
  114.0 0.9 multiply_subtract_fusion.1
  114.9 0.1 collective-permute-done.12
  115.0 5.0 %multiply_subtract_fusion = f32[2,8,256,256]{3,2,1,0:T(8,128)} fusion(f32[2,8,256,256]{3,2,1,0:T(8,128)} %probe_hbm.1, f32[]{:T(128)} %bitcast.6, pred[2]{0:T(512)(128)(4,1)S(1)} %iota_compare_fusion, f16[8,256,256]{2,1,0:T(8,128)(2,1)S(1)} %collective-permute-done.12, f16[8,256,256]{2,1,0:T(8,128)(2,1)S(1)} %bitcast.12), kind=kLoop, calls=%fused_computation | loop fusion | flops 4194304 | bytes 10485766 | tf_op jit(solution)/shard_map/sub | solution.py:398
  (14 shorter events, 0.1 us)
Async XLA Ops:
  0.6 20.3 %copy-start.3 = (s32[1,1,2]{2,1,0:T(1,128)S(1)}, s32[1,1,2]{2,1,0:T(1,128)}, u32[]{:S(2)}) copy-start(s32[1,1,2]{2,1,0:T(1,128)} %param.13) | copy-start | bytes 28
  0.6 20.3 %copy-start.4 = (s32[1,1,2]{2,1,0:T(1,128)S(1)}, s32[1,1,2]{2,1,0:T(1,128)}, u32[]{:S(2)}) copy-start(s32[1,1,2]{2,1,0:T(1,128)} %param.12) | copy-start | bytes 28
  1.8 6.3 %collective-permute-start.1 = (bf16[2,128,256]{2,1,0:T(8,128)(2,1)S(1)}, bf16[2,128,256]{2,1,0:T(8,128)(2,1)S(1)}, u32[]{:S(2)}, u32[]{:S(2)}) collective-permute-start(bf16[2,128,256]{2,1,0:T(8,128)(2,1)S(1)} %get-tuple-element.30), channel_id=1, source_target_pairs={{8,0},{16,8},{24,16},{32,24},{40,32},{48,40},{56,48},{64,56},{72,6... | collective-permute-start | bytes 393224 | tf_op jit(solution)/shard_map/ppermute | solution.py:350
  6.0 7.8 %collective-permute-start = (bf16[2,128,256]{2,1,0:T(8,128)(2,1)S(1)}, bf16[2,128,256]{2,1,0:T(8,128)(2,1)S(1)}, u32[]{:S(2)}, u32[]{:S(2)}) collective-permute-start(bf16[2,128,256]{2,1,0:T(8,128)(2,1)S(1)} %get-tuple-element.31), channel_id=1, source_target_pairs={{0,8},{8,16},{16,24},{24,32},{32,40},{40,48},{48,56},{56,64},{64,7... | collective-permute-start | bytes 393224 | tf_op jit(solution)/shard_map/ppermute | solution.py:349
  13.9 9.2 %collective-permute-start.3 = (bf16[2,512,128]{2,1,0:T(8,128)(2,1)S(1)}, bf16[2,512,128]{2,1,0:T(8,128)(2,1)S(1)}, u32[]{:S(2)}, u32[]{:S(2)}) collective-permute-start(bf16[2,512,128]{2,1,0:T(8,128)(2,1)S(1)} %get-tuple-element.28), channel_id=1, source_target_pairs={{1,0},{2,1},{3,2},{4,3},{5,4},{6,5},{7,6},{9,8},{10,9},{11,10},{12... | collective-permute-start | bytes 786440 | tf_op jit(solution)/shard_map/ppermute | solution.py:350
  17.9 6.3 %collective-permute-start.2 = (bf16[2,512,128]{2,1,0:T(8,128)(2,1)S(1)}, bf16[2,512,128]{2,1,0:T(8,128)(2,1)S(1)}, u32[]{:S(2)}, u32[]{:S(2)}) collective-permute-start(bf16[2,512,128]{2,1,0:T(8,128)(2,1)S(1)} %get-tuple-element.29), channel_id=1, source_target_pairs={{0,1},{1,2},{2,3},{3,4},{4,5},{5,6},{6,7},{8,9},{9,10},{10,11},{11... | collective-permute-start | bytes 786440 | tf_op jit(solution)/shard_map/ppermute | solution.py:349
  42.7 4.7 %copy-start = (f32[8,256,256]{2,1,0:T(8,128)S(1)}, f32[8,256,256]{2,1,0:T(8,128)}, u32[]{:S(2)}) copy-start(f32[8,256,256]{2,1,0:T(8,128)} %get-tuple-element.14) | copy-start | bytes 6291460
  44.7 2.7 %collective-permute-start.4 = (f16[8,256,256]{2,1,0:T(8,128)(2,1)S(1)}, f16[8,256,256]{2,1,0:T(8,128)(2,1)S(1)}, u32[]{:S(2)}, u32[]{:S(2)}) collective-permute-start(f16[8,256,256]{2,1,0:T(8,128)(2,1)S(1)} %multiply_convert_fusion.1), channel_id=1, source_target_pairs={{0,1},{1,0},{2,3},{3,2},{4,5},{5,4},{6,7},{7,6},{8,9},{9,8},{10,11... | collective-permute-start | bytes 3145736 | tf_op jit(solution)/shard_map/ppermute | solution.py:313
  48.8 23.1 %copy-start.2 = (f32[2,512,256]{2,1,0:T(8,128)S(1)}, f32[2,512,256]{2,1,0:T(8,128)}, u32[]{:S(2)}) copy-start(f32[2,512,256]{2,1,0:T(8,128)} %get-tuple-element.16) | copy-start | bytes 3145732
  48.8 23.2 %all-to-all-start = ((f16[32,64,256]{2,1,0:T(8,128)(2,1)}), f16[32,64,256]{2,1,0:T(8,128)(2,1)S(1)}, u32[]{:S(2)}, u32[]{:S(2)}) async-start(f16[32,64,256]{2,1,0:T(8,128)(2,1)} %bitcast.4), calls=%async_computation | async-start | bytes 2097152 | tf_op jit(solution)/shard_map/all_to_all | solution.py:308
  55.5 16.4 %collective-permute-start.6 = (f16[2,512,128]{2,1,0:T(8,128)(2,1)S(1)}, f16[2,512,128]{2,1,0:T(8,128)(2,1)S(1)}, u32[]{:S(2)}, u32[]{:S(2)}) collective-permute-start(f16[2,512,128]{2,1,0:T(8,128)(2,1)S(1)} %multiply_convert_fusion.2), channel_id=1, source_target_pairs={{1,0},{2,1},{3,2},{4,3},{5,4},{6,5},{7,6},{9,8},{10,9},{11,10},{12... | collective-permute-start | bytes 786440 | tf_op jit(solution)/shard_map/ppermute | solution.py:350
  58.3 13.6 %collective-permute-start.5 = (f16[2,512,128]{2,1,0:T(8,128)(2,1)S(1)}, f16[2,512,128]{2,1,0:T(8,128)(2,1)S(1)}, u32[]{:S(2)}, u32[]{:S(2)}) collective-permute-start(f16[2,512,128]{2,1,0:T(8,128)(2,1)S(1)} %multiply_convert_fusion.3), channel_id=1, source_target_pairs={{0,1},{1,2},{2,3},{3,4},{4,5},{5,6},{6,7},{8,9},{9,10},{10,11},{11... | collective-permute-start | bytes 786440 | tf_op jit(solution)/shard_map/ppermute | solution.py:349
  72.3 41.7 %copy-start.1 = (f32[2,256,256]{2,1,0:T(8,128)S(1)}, f32[2,256,256]{2,1,0:T(8,128)}, u32[]{:S(2)}) copy-start(f32[2,256,256]{2,1,0:T(8,128)} %block_hbm.1) | copy-start | bytes 1572868
  72.3 10.6 %collective-permute-start.8 = (f16[64,256]{1,0:T(8,128)(2,1)S(1)}, f16[64,256]{1,0:T(8,128)(2,1)S(1)}, u32[]{:S(2)}, u32[]{:S(2)}) collective-permute-start(f16[64,256]{1,0:T(8,128)(2,1)S(1)} %multiply_convert_fusion.7), channel_id=1, source_target_pairs={{0,64},{1,65},{2,66},{3,67},{4,68},{5,69},{6,70},{7,71},{8,72},{9,... | collective-permute-start | bytes 98312 | tf_op jit(solution)/shard_map/ppermute | solution.py:321
  76.1 6.8 %collective-permute-start.7 = (f16[64,256]{1,0:T(8,128)(2,1)S(1)}, f16[64,256]{1,0:T(8,128)(2,1)S(1)}, u32[]{:S(2)}, u32[]{:S(2)}) collective-permute-start(f16[64,256]{1,0:T(8,128)(2,1)S(1)} %multiply_convert_fusion.7), channel_id=1, source_target_pairs={{0,128},{1,129},{2,130},{3,131},{4,132},{5,133},{6,134},{7,135},{8... | collective-permute-start | bytes 98312 | tf_op jit(solution)/shard_map/ppermute | solution.py:321
  80.5 4.4 %collective-permute-start.9 = (f16[64,256]{1,0:T(8,128)(2,1)S(1)}, f16[64,256]{1,0:T(8,128)(2,1)S(1)}, u32[]{:S(2)}, u32[]{:S(2)}) collective-permute-start(f16[64,256]{1,0:T(8,128)(2,1)S(1)} %multiply_convert_fusion.7), channel_id=1, source_target_pairs={{0,192},{1,193},{2,194},{3,195},{4,196},{5,197},{6,198},{7,199},{8... | collective-permute-start | bytes 98312 | tf_op jit(solution)/shard_map/ppermute | solution.py:321
  86.0 25.0 %all-to-all-start.1 = ((f16[32,64,256]{2,1,0:T(8,128)(2,1)}), f16[32,64,256]{2,1,0:T(8,128)(2,1)S(1)}, u32[]{:S(2)}, u32[]{:S(2)}) async-start(f16[32,64,256]{2,1,0:T(8,128)(2,1)} %broadcast_in_dim.21), calls=%async_computation.1 | async-start | bytes 2097152 | tf_op jit(solution)/shard_map/all_to_all | solution.py:308
  92.9 18.1 %collective-permute-start.11 = (f16[2,128,256]{2,1,0:T(8,128)(2,1)S(1)}, f16[2,128,256]{2,1,0:T(8,128)(2,1)S(1)}, u32[]{:S(2)}, u32[]{:S(2)}) collective-permute-start(f16[2,128,256]{2,1,0:T(8,128)(2,1)S(1)} %get-tuple-element.26), channel_id=1, source_target_pairs={{8,0},{16,8},{24,16},{32,24},{40,32},{48,40},{56,48},{64,56},{72,6... | collective-permute-start | bytes 393224 | tf_op jit(solution)/shard_map/ppermute | solution.py:350
  97.2 13.8 %collective-permute-start.10 = (f16[2,128,256]{2,1,0:T(8,128)(2,1)S(1)}, f16[2,128,256]{2,1,0:T(8,128)(2,1)S(1)}, u32[]{:S(2)}, u32[]{:S(2)}) collective-permute-start(f16[2,128,256]{2,1,0:T(8,128)(2,1)S(1)} %get-tuple-element.27), channel_id=1, source_target_pairs={{0,8},{8,16},{16,24},{24,32},{32,40},{40,48},{48,56},{56,64},{64,7... | collective-permute-start | bytes 393224 | tf_op jit(solution)/shard_map/ppermute | solution.py:349
  111.0 3.9 %collective-permute-start.12 = (f16[8,256,256]{2,1,0:T(8,128)(2,1)S(1)}, f16[8,256,256]{2,1,0:T(8,128)(2,1)S(1)}, u32[]{:S(2)}, u32[]{:S(2)}) collective-permute-start(f16[8,256,256]{2,1,0:T(8,128)(2,1)S(1)} %bitcast.11), channel_id=1, source_target_pairs={{0,1},{1,0},{2,3},{3,2},{4,5},{5,4},{6,7},{7,6},{8,9},{9,8},{10,11... | collective-permute-start | bytes 3145736 | tf_op jit(solution)/shard_map/ppermute | solution.py:313

commit v2 on v1

--- a/solution.py
+++ b/solution.py
@@ -336,19 +336,23 @@
     return (widen(sent, 512.0) + two) + (one + three)
 
 
-def gather_sum(total, modes):
+def gather_all(total, modes):
     rows, cols = total.shape
     places = 8 * (lax.axis_size("scan") // 2)
-    pieces = jnp.broadcast_to(narrow(total, 2048.0), (places, rows, cols))
+    pieces = jnp.broadcast_to(total, (places, rows, cols))
     return exchange(pieces, ("pair", "y", "x")).reshape(modes, -1, cols)
 
 
 def neighbours(head, tail, axis):
     count = lax.axis_size(axis)
-    ends = count - 1
-    before = lax.ppermute(tail, axis, [(i, (i + 1) % count) for i in range(ends)])
-    after = lax.ppermute(head, axis, [((i + 1) % count, i) for i in range(ends)])
-    return (before, after)
+    even = lax.axis_index(axis) % 2 == 0
+    swaps = [
+        [pair for i in range(start, count - 1, 2) for pair in ((i, i + 1), (i + 1, i))]
+        for start in (0, 1)
+    ]
+    inner = lax.ppermute(jnp.where(even, tail, head), axis, swaps[0])
+    outer = lax.ppermute(jnp.where(even, head, tail), axis, swaps[1])
+    return (jnp.where(even, outer, inner), jnp.where(even, inner, outer))
 
 
 def edges(cells, axis, dim, width):
@@ -385,17 +389,21 @@
     center = center + widen(jnp.concatenate([from_left, from_right], axis=2), 64.0)
     piece, center = lax.optimization_barrier((piece, center))
     total = sum_far(piece)
-    total, center = lax.optimization_barrier((total, center))
+    region, scan = lax.axis_index("region"), lax.axis_index("scan")
+    spot = (region % 8 * 4 + scan // 2) * total.shape[0]
+    flat = probe_modes.reshape(2, -1, probe_modes.shape[-1])
+    mine = lax.dynamic_slice(flat, (core, spot, 0), (1, *total.shape))[0]
+    updated = narrow(mine - probe_step[0] * total, 128.0)
+    updated, center = lax.optimization_barrier((updated, center))
     from_above, from_below = trade(center[:, :half_width], center[:, -half_width:], "region")
-    plane = gather_sum(total, probe_modes.shape[1])
+    plane = gather_all(updated, probe_modes.shape[1])
     plane, from_above, from_below = lax.optimization_barrier((plane, from_above, from_below))
     swapped = swap_cores(plane)
     inner = center[:, half_width:-half_width]
     inner = inner + widen(jnp.concatenate([from_above, from_below], axis=1), 64.0)
     object_field = object_field - object_step[0] * inner
     own = lax.broadcasted_iota(jnp.int32, probe_modes.shape, 0) == core
-    probe_total = widen(jnp.where(own, plane[None], swapped[None]), 2048.0)
-    probe_modes = probe_modes - probe_step[0] * probe_total
+    probe_modes = widen(jnp.where(own, plane[None], swapped[None]), 128.0)
     return (object_field, probe_modes)
 
 

time: 120 us -> 116 us (0.967)
  starting transfers between devices: 50.8 us -> 46.1 us
    ppermute x8, starting transfers between devices: 25.2 us -> 18.8 us  [the longest x4 13.8 us: neighbours(): outer = lax.ppermute(jnp.where(even, head, tail), axis, swaps[1])]
    sub x1 -> x0, other arithmetic: 4.96 us -> none  [on_device(): probe_modes = probe_modes - probe_step[0] * probe_total]
    mul x0 -> x1, other arithmetic: none -> 2.64 us  [widen(): return values.astype(jnp.float32) * scale]
    ppermute x8, waiting for transfers between devices: 31.5 us -> 33.1 us  [the longest x4 21.7 us: neighbours(): outer = lax.ppermute(jnp.where(even, head, tail), axis, swaps[1])]
    ppermute x2, starting transfers between devices: 1.71 us -> 3.21 us  [swap_cores(): lax.ppermute(values, ('region', 'scan'), [(i, i ^ 1) for i in range(count)])]
    convert_element_type x7 -> x4, other arithmetic: 3.56 us -> 4.25 us  [narrow(): return (values * (1.0 / scale)).astype(jnp.float16)]
where the time goes in v2:
time: 116 us; the launch traced here: 115 us
  starting transfers between devices  46.1 us (40%)
  waiting for transfers between devices  37.3 us (32%)
  Pallas kernels  18.4 us (16%)
  other arithmetic  9.9 us (9%)
  between operations  2.25 us (2%)
  local copies, waits for them, and re-layouts  1.19 us (1%)
    ppermute x4, waiting for transfers between devices, neighbours(): outer = lax.ppermute(jnp.where(even, head, tail), axis, swaps[1])  21.7 us
    pallas_call x1, Pallas kernels, device_gradients(): pl.pallas_call(gradients_kernel, out_shape=made, in_specs=[pl.BlockSpec(m...  18.4 us
    all_to_all x2, starting transfers between devices, exchange(): lax.all_to_all(parts, ('region', 'scan'), 0, 0, axis_index_groups=axis_gr...  14.4 us
    ppermute x4, starting transfers between devices, neighbours(): outer = lax.ppermute(jnp.where(even, head, tail), axis, swaps[1])  13.8 us
    ppermute x4, waiting for transfers between devices, neighbours(): inner = lax.ppermute(jnp.where(even, tail, head), axis, swaps[0])  11.3 us
    ppermute x3, starting transfers between devices, shift_far(): return lax.ppermute(values, ('region', 'scan'), pairs)  9.66 us
    ppermute x4, starting transfers between devices, neighbours(): inner = lax.ppermute(jnp.where(even, tail, head), axis, swaps[0])  4.95 us
    convert_element_type x4, other arithmetic, narrow(): return (values * (1.0 / scale)).astype(jnp.float16)  4.25 us
  transfers between devices with their start and end apart: 15, of which 9 were waited for; matrix products, arithmetic and copies ran while one was open for 1% of the time, Pallas kernels for 0%

profile of v2, /device:TPU:33, one launch (start us, length us, event | category | flops | bytes accessed | tf_op | source)
XLA Modules:
  0.0 115.2 jit_solution(5352584183217236642)
XLA Ops:
  0.7 1.1 convert_element_type.54
  1.8 1.4 %collective-permute-start.1 = (bf16[2,128,256]{2,1,0:T(8,128)(2,1)S(1)}, bf16[2,128,256]{2,1,0:T(8,128)(2,1)S(1)}, u32[]{:S(2)}, u32[]{:S(2)}) collective-permute-start(bf16[2,128,256]{2,1,0:T(8,128)(2,1)S(1)} %get-tuple-element.40), channel_id=1, source_target_pairs={{0,8},{8,0},{16,24},{24,16},{32,40},{40,32},{48,56},{56,48},{64,72... | collective-permute-start | bytes 393224 | tf_op jit(solution)/shard_map/ppermute | solution.py:353
  3.2 3.3 %collective-permute-start = (bf16[2,128,256]{2,1,0:T(8,128)(2,1)S(1)}, bf16[2,128,256]{2,1,0:T(8,128)(2,1)S(1)}, u32[]{:S(2)}, u32[]{:S(2)}) collective-permute-start(bf16[2,128,256]{2,1,0:T(8,128)(2,1)S(1)} %get-tuple-element.41), channel_id=1, source_target_pairs={{8,16},{16,8},{24,32},{32,24},{40,48},{48,40},{56,64},{64,56},{72,... | collective-permute-start | bytes 393224 | tf_op jit(solution)/shard_map/ppermute | solution.py:354
  6.5 0.0 collective-permute-done.1
  6.5 4.4 %collective-permute-done = bf16[2,128,256]{2,1,0:T(8,128)(2,1)S(1)} collective-permute-done((bf16[2,128,256]{2,1,0:T(8,128)(2,1)S(1)}, bf16[2,128,256]{2,1,0:T(8,128)(2,1)S(1)}, u32[]{:S(2)}, u32[]{:S(2)}) %collective-permute-start) | collective-permute-done | bytes 131104 | tf_op jit(solution)/shard_map/ppermute | solution.py:354
  11.1 2.2 %collective-permute-start.3 = (bf16[2,512,128]{2,1,0:T(8,128)(2,1)S(1)}, bf16[2,512,128]{2,1,0:T(8,128)(2,1)S(1)}, u32[]{:S(2)}, u32[]{:S(2)}) collective-permute-start(bf16[2,512,128]{2,1,0:T(8,128)(2,1)S(1)} %get-tuple-element.34), channel_id=1, source_target_pairs={{0,1},{1,0},{2,3},{3,2},{4,5},{5,4},{6,7},{7,6},{8,9},{9,8},{10,11... | collective-permute-start | bytes 786440 | tf_op jit(solution)/shard_map/ppermute | solution.py:353
  13.3 3.0 %collective-permute-start.2 = (bf16[2,512,128]{2,1,0:T(8,128)(2,1)S(1)}, bf16[2,512,128]{2,1,0:T(8,128)(2,1)S(1)}, u32[]{:S(2)}, u32[]{:S(2)}) collective-permute-start(bf16[2,512,128]{2,1,0:T(8,128)(2,1)S(1)} %get-tuple-element.35), channel_id=1, source_target_pairs={{1,2},{2,1},{3,4},{4,3},{5,6},{6,5},{9,10},{10,9},{11,12},{12,11},... | collective-permute-start | bytes 786440 | tf_op jit(solution)/shard_map/ppermute | solution.py:354
  16.3 0.1 pad.9.clone
  16.4 0.1 add_add_fusion.place_ref
  16.5 0.0 collective-permute-done.3
  16.5 4.5 %collective-permute-done.2 = bf16[2,512,128]{2,1,0:T(8,128)(2,1)S(1)} collective-permute-done((bf16[2,512,128]{2,1,0:T(8,128)(2,1)S(1)}, bf16[2,512,128]{2,1,0:T(8,128)(2,1)S(1)}, u32[]{:S(2)}, u32[]{:S(2)}) %collective-permute-start.2) | collective-permute-done | bytes 262176 | tf_op jit(solution)/shard_map/ppermute | solution.py:354
  21.0 18.4 %shard_map.104 = (f32[2,512,128]{2,1,0:T(8,128)S(1)}, f32[2,512,256]{2,1,0:T(8,128)}, f32[2,512,128]{2,1,0:T(8,128)S(1)}, f32[8,256,256]{2,1,0:T(8,128)}, f32[8,256,256]{2,1,0:T(8,128)}) custom-call(s32[3,2]{1,0:T(4,128)S(1)} %add_add_fusion.place_ref, f32[2,256,256]{2,1,0:T(8,128)} %block_hbm.1, bf16[2,128,256]{2,1,0:T(8,128)(2,1)S(1)} %get-tuple-element.39.above_hbm, ...), custom_call_target="tpu_custom_call" | custom-call | flops 8589934592 | bytes 16777216 | tf_op jit(solution)/shard_map/pallas_call | solution.py:260
  39.4 0.0 copy-start
  39.4 2.0 %multiply_convert_fusion.1 = f16[8,256,256]{2,1,0:T(8,128)(2,1)S(1)} fusion(f32[8,256,256]{2,1,0:T(8,128)} %get-tuple-element.15), kind=kLoop, calls=%fused_computation.3 | loop fusion | flops 1048576 | bytes 3145728 | tf_op jit(solution)/shard_map/convert_element_type | solution.py:300
  41.4 0.1 collective-permute-start.4
  41.5 2.6 %collective-permute-done.4 = f16[8,256,256]{2,1,0:T(8,128)(2,1)S(1)} collective-permute-done((f16[8,256,256]{2,1,0:T(8,128)(2,1)S(1)}, f16[8,256,256]{2,1,0:T(8,128)(2,1)S(1)}, u32[]{:S(2)}, u32[]{:S(2)}) %collective-permute-start.4) | collective-permute-done | bytes 1048608 | tf_op jit(solution)/shard_map/ppermute | solution.py:313
  44.2 1.4 %multiply_convert_fusion = f16[8,256,256]{2,1,0:T(8,128)(2,1)} fusion(f32[8,256,256]{2,1,0:T(8,128)S(1)} %copy-done, f16[8,256,256]{2,1,0:T(8,128)(2,1)S(1)} %collective-permute-done.4), kind=kLoop, calls=%fused_computation.2 | loop fusion | flops 2621440 | bytes 4194304 | tf_op jit(solution)/shard_map/convert_element_type | solution.py:300
  45.6 7.0 %all-to-all-start = ((f16[32,64,256]{2,1,0:T(8,128)(2,1)}), f16[32,64,256]{2,1,0:T(8,128)(2,1)S(1)}, u32[]{:S(2)}, u32[]{:S(2)}) async-start(f16[32,64,256]{2,1,0:T(8,128)(2,1)} %bitcast.6), calls=%async_computation | async-start | bytes 2097152 | tf_op jit(solution)/shard_map/all_to_all | solution.py:308
  52.6 0.1 broadcast_select_fusion.3
  52.7 3.8 %collective-permute-start.5 = (f16[2,512,128]{2,1,0:T(8,128)(2,1)S(1)}, f16[2,512,128]{2,1,0:T(8,128)(2,1)S(1)}, u32[]{:S(2)}, u32[]{:S(2)}) collective-permute-start(f16[2,512,128]{2,1,0:T(8,128)(2,1)S(1)} %get-tuple-element.28), channel_id=1, source_target_pairs={{1,2},{2,1},{3,4},{4,3},{5,6},{6,5},{9,10},{10,9},{11,12},{12,11},... | collective-permute-start | bytes 786440 | tf_op jit(solution)/shard_map/ppermute | solution.py:354
  56.5 0.1 collective-permute-start.6
  56.6 12.5 %collective-permute-done.5 = f16[2,512,128]{2,1,0:T(8,128)(2,1)S(1)} collective-permute-done((f16[2,512,128]{2,1,0:T(8,128)(2,1)S(1)}, f16[2,512,128]{2,1,0:T(8,128)(2,1)S(1)}, u32[]{:S(2)}, u32[]{:S(2)}) %collective-permute-start.5) | collective-permute-done | bytes 262176 | tf_op jit(solution)/shard_map/ppermute | solution.py:354
  69.1 0.0 collective-permute-done.6
  69.1 0.1 broadcast_select_fusion.1
  69.3 0.2 multiply_add_fusion
  69.4 0.0 all-to-all-done
  69.5 0.2 multiply_reduce_fusion
  69.7 4.3 %collective-permute-start.8 = (f16[64,256]{1,0:T(8,128)(2,1)S(1)}, f16[64,256]{1,0:T(8,128)(2,1)S(1)}, u32[]{:S(2)}, u32[]{:S(2)}) collective-permute-start(f16[64,256]{1,0:T(8,128)(2,1)S(1)} %multiply_convert_fusion.6), channel_id=1, source_target_pairs={{0,64},{1,65},{2,66},{3,67},{4,68},{5,69},{6,70},{7,71},{8,72},{9,... | collective-permute-start | bytes 98312 | tf_op jit(solution)/shard_map/ppermute | solution.py:321
  74.0 2.5 %collective-permute-start.7 = (f16[64,256]{1,0:T(8,128)(2,1)S(1)}, f16[64,256]{1,0:T(8,128)(2,1)S(1)}, u32[]{:S(2)}, u32[]{:S(2)}) collective-permute-start(f16[64,256]{1,0:T(8,128)(2,1)S(1)} %multiply_convert_fusion.6), channel_id=1, source_target_pairs={{0,128},{1,129},{2,130},{3,131},{4,132},{5,133},{6,134},{7,135},{8... | collective-permute-start | bytes 98312 | tf_op jit(solution)/shard_map/ppermute | solution.py:321
  76.5 2.8 %collective-permute-start.9 = (f16[64,256]{1,0:T(8,128)(2,1)S(1)}, f16[64,256]{1,0:T(8,128)(2,1)S(1)}, u32[]{:S(2)}, u32[]{:S(2)}) collective-permute-start(f16[64,256]{1,0:T(8,128)(2,1)S(1)} %multiply_convert_fusion.6), channel_id=1, source_target_pairs={{0,192},{1,193},{2,194},{3,195},{4,196},{5,197},{6,198},{7,199},{8... | collective-permute-start | bytes 98312 | tf_op jit(solution)/shard_map/ppermute | solution.py:321
  80.0 0.0 collective-permute-done.8
  80.0 0.7 collective-permute-done.7
  80.8 0.1 collective-permute-done.9
  80.9 0.9 fusion.1
  81.8 0.0 copy-start.1
  81.8 1.1 broadcast_in_dim.21
  82.9 7.4 %all-to-all-start.1 = ((f16[32,64,256]{2,1,0:T(8,128)(2,1)}), f16[32,64,256]{2,1,0:T(8,128)(2,1)S(1)}, u32[]{:S(2)}, u32[]{:S(2)}) async-start(f16[32,64,256]{2,1,0:T(8,128)(2,1)} %broadcast_in_dim.21), calls=%async_computation.1 | async-start | bytes 2097152 | tf_op jit(solution)/shard_map/all_to_all | solution.py:308
  90.3 0.1 broadcast_select_fusion.10
  90.4 1.3 %collective-permute-start.11 = (f16[2,128,256]{2,1,0:T(8,128)(2,1)S(1)}, f16[2,128,256]{2,1,0:T(8,128)(2,1)S(1)}, u32[]{:S(2)}, u32[]{:S(2)}) collective-permute-start(f16[2,128,256]{2,1,0:T(8,128)(2,1)S(1)} %get-tuple-element.26), channel_id=1, source_target_pairs={{0,8},{8,0},{16,24},{24,16},{32,40},{40,32},{48,56},{56,48},{64,72... | collective-permute-start | bytes 393224 | tf_op jit(solution)/shard_map/ppermute | solution.py:353
  91.7 3.7 %collective-permute-start.10 = (f16[2,128,256]{2,1,0:T(8,128)(2,1)S(1)}, f16[2,128,256]{2,1,0:T(8,128)(2,1)S(1)}, u32[]{:S(2)}, u32[]{:S(2)}) collective-permute-start(f16[2,128,256]{2,1,0:T(8,128)(2,1)S(1)} %get-tuple-element.27), channel_id=1, source_target_pairs={{8,16},{16,8},{24,32},{32,24},{40,48},{48,40},{56,64},{64,56},{72,... | collective-permute-start | bytes 393224 | tf_op jit(solution)/shard_map/ppermute | solution.py:354
  95.4 11.3 %collective-permute-done.11 = f16[2,128,256]{2,1,0:T(8,128)(2,1)S(1)} collective-permute-done((f16[2,128,256]{2,1,0:T(8,128)(2,1)S(1)}, f16[2,128,256]{2,1,0:T(8,128)(2,1)S(1)}, u32[]{:S(2)}, u32[]{:S(2)}) %collective-permute-start.11) | collective-permute-done | bytes 131104 | tf_op jit(solution)/shard_map/ppermute | solution.py:353
  106.7 0.4 collective-permute-done.10
  107.1 0.1 broadcast_select_fusion.8
  107.1 0.0 all-to-all-done.1
  107.2 3.1 %collective-permute-start.12 = (f16[8,256,256]{2,1,0:T(8,128)(2,1)S(1)}, f16[8,256,256]{2,1,0:T(8,128)(2,1)S(1)}, u32[]{:S(2)}, u32[]{:S(2)}) collective-permute-start(f16[8,256,256]{2,1,0:T(8,128)(2,1)S(1)} %bitcast.18), channel_id=1, source_target_pairs={{0,1},{1,0},{2,3},{3,2},{4,5},{5,4},{6,7},{7,6},{8,9},{9,8},{10,11... | collective-permute-start | bytes 3145736 | tf_op jit(solution)/shard_map/ppermute | solution.py:313
  110.9 0.9 multiply_subtract_fusion
  111.8 0.7 collective-permute-done.12
  112.6 2.6 %convert_multiply_fusion = f32[2,8,256,256]{3,2,1,0:T(8,128)} fusion(pred[2]{0:T(512)(128)(4,1)S(1)} %iota_compare_fusion, f16[8,256,256]{2,1,0:T(8,128)(2,1)S(1)} %collective-permute-done.12, f16[8,256,256]{2,1,0:T(8,128)(2,1)S(1)} %bitcast.19), kind=kLoop, calls=%fused_computation | loop fusion | flops 3145728 | bytes 6291458 | tf_op jit(solution)/shard_map/mul | solution.py:304
  (16 shorter events, 0.2 us)
Async XLA Ops:
  0.6 15.7 %copy-start.3 = (s32[1,1,2]{2,1,0:T(1,128)S(1)}, s32[1,1,2]{2,1,0:T(1,128)}, u32[]{:S(2)}) copy-start(s32[1,1,2]{2,1,0:T(1,128)} %param.13) | copy-start | bytes 28
  0.6 15.7 %copy-start.4 = (s32[1,1,2]{2,1,0:T(1,128)S(1)}, s32[1,1,2]{2,1,0:T(1,128)}, u32[]{:S(2)}) copy-start(s32[1,1,2]{2,1,0:T(1,128)} %param.12) | copy-start | bytes 28
  1.8 4.8 %collective-permute-start.1 = (bf16[2,128,256]{2,1,0:T(8,128)(2,1)S(1)}, bf16[2,128,256]{2,1,0:T(8,128)(2,1)S(1)}, u32[]{:S(2)}, u32[]{:S(2)}) collective-permute-start(bf16[2,128,256]{2,1,0:T(8,128)(2,1)S(1)} %get-tuple-element.40), channel_id=1, source_target_pairs={{0,8},{8,0},{16,24},{24,16},{32,40},{40,32},{48,56},{56,48},{64,72... | collective-permute-start | bytes 393224 | tf_op jit(solution)/shard_map/ppermute | solution.py:353
  3.2 7.8 %collective-permute-start = (bf16[2,128,256]{2,1,0:T(8,128)(2,1)S(1)}, bf16[2,128,256]{2,1,0:T(8,128)(2,1)S(1)}, u32[]{:S(2)}, u32[]{:S(2)}) collective-permute-start(bf16[2,128,256]{2,1,0:T(8,128)(2,1)S(1)} %get-tuple-element.41), channel_id=1, source_target_pairs={{8,16},{16,8},{24,32},{32,24},{40,48},{48,40},{56,64},{64,56},{72,... | collective-permute-start | bytes 393224 | tf_op jit(solution)/shard_map/ppermute | solution.py:354
  11.1 5.4 %collective-permute-start.3 = (bf16[2,512,128]{2,1,0:T(8,128)(2,1)S(1)}, bf16[2,512,128]{2,1,0:T(8,128)(2,1)S(1)}, u32[]{:S(2)}, u32[]{:S(2)}) collective-permute-start(bf16[2,512,128]{2,1,0:T(8,128)(2,1)S(1)} %get-tuple-element.34), channel_id=1, source_target_pairs={{0,1},{1,0},{2,3},{3,2},{4,5},{5,4},{6,7},{7,6},{8,9},{9,8},{10,11... | collective-permute-start | bytes 786440 | tf_op jit(solution)/shard_map/ppermute | solution.py:353
  13.3 7.7 %collective-permute-start.2 = (bf16[2,512,128]{2,1,0:T(8,128)(2,1)S(1)}, bf16[2,512,128]{2,1,0:T(8,128)(2,1)S(1)}, u32[]{:S(2)}, u32[]{:S(2)}) collective-permute-start(bf16[2,512,128]{2,1,0:T(8,128)(2,1)S(1)} %get-tuple-element.35), channel_id=1, source_target_pairs={{1,2},{2,1},{3,4},{4,3},{5,6},{6,5},{9,10},{10,9},{11,12},{12,11},... | collective-permute-start | bytes 786440 | tf_op jit(solution)/shard_map/ppermute | solution.py:354
  39.4 4.7 %copy-start = (f32[8,256,256]{2,1,0:T(8,128)S(1)}, f32[8,256,256]{2,1,0:T(8,128)}, u32[]{:S(2)}) copy-start(f32[8,256,256]{2,1,0:T(8,128)} %get-tuple-element.14) | copy-start | bytes 6291460
  41.4 2.7 %collective-permute-start.4 = (f16[8,256,256]{2,1,0:T(8,128)(2,1)S(1)}, f16[8,256,256]{2,1,0:T(8,128)(2,1)S(1)}, u32[]{:S(2)}, u32[]{:S(2)}) collective-permute-start(f16[8,256,256]{2,1,0:T(8,128)(2,1)S(1)} %multiply_convert_fusion.1), channel_id=1, source_target_pairs={{0,1},{1,0},{2,3},{3,2},{4,5},{5,4},{6,7},{7,6},{8,9},{9,8},{10,11... | collective-permute-start | bytes 3145736 | tf_op jit(solution)/shard_map/ppermute | solution.py:313
  45.6 23.9 %all-to-all-start = ((f16[32,64,256]{2,1,0:T(8,128)(2,1)}), f16[32,64,256]{2,1,0:T(8,128)(2,1)S(1)}, u32[]{:S(2)}, u32[]{:S(2)}) async-start(f16[32,64,256]{2,1,0:T(8,128)(2,1)} %bitcast.6), calls=%async_computation | async-start | bytes 2097152 | tf_op jit(solution)/shard_map/all_to_all | solution.py:308
  52.5 16.7 %copy-start.2 = (f32[2,512,256]{2,1,0:T(8,128)S(1)}, f32[2,512,256]{2,1,0:T(8,128)}, u32[]{:S(2)}) copy-start(f32[2,512,256]{2,1,0:T(8,128)} %get-tuple-element.16) | copy-start | bytes 3145732
  52.7 16.4 %collective-permute-start.5 = (f16[2,512,128]{2,1,0:T(8,128)(2,1)S(1)}, f16[2,512,128]{2,1,0:T(8,128)(2,1)S(1)}, u32[]{:S(2)}, u32[]{:S(2)}) collective-permute-start(f16[2,512,128]{2,1,0:T(8,128)(2,1)S(1)} %get-tuple-element.28), channel_id=1, source_target_pairs={{1,2},{2,1},{3,4},{4,3},{5,6},{6,5},{9,10},{10,9},{11,12},{12,11},... | collective-permute-start | bytes 786440 | tf_op jit(solution)/shard_map/ppermute | solution.py:354
  56.5 12.6 %collective-permute-start.6 = (f16[2,512,128]{2,1,0:T(8,128)(2,1)S(1)}, f16[2,512,128]{2,1,0:T(8,128)(2,1)S(1)}, u32[]{:S(2)}, u32[]{:S(2)}) collective-permute-start(f16[2,512,128]{2,1,0:T(8,128)(2,1)S(1)} %get-tuple-element.29), channel_id=1, source_target_pairs={{0,1},{1,0},{2,3},{3,2},{4,5},{5,4},{6,7},{7,6},{8,9},{9,8},{10,11... | collective-permute-start | bytes 786440 | tf_op jit(solution)/shard_map/ppermute | solution.py:353
  69.7 10.3 %collective-permute-start.8 = (f16[64,256]{1,0:T(8,128)(2,1)S(1)}, f16[64,256]{1,0:T(8,128)(2,1)S(1)}, u32[]{:S(2)}, u32[]{:S(2)}) collective-permute-start(f16[64,256]{1,0:T(8,128)(2,1)S(1)} %multiply_convert_fusion.6), channel_id=1, source_target_pairs={{0,64},{1,65},{2,66},{3,67},{4,68},{5,69},{6,70},{7,71},{8,72},{9,... | collective-permute-start | bytes 98312 | tf_op jit(solution)/shard_map/ppermute | solution.py:321
  74.0 6.8 %collective-permute-start.7 = (f16[64,256]{1,0:T(8,128)(2,1)S(1)}, f16[64,256]{1,0:T(8,128)(2,1)S(1)}, u32[]{:S(2)}, u32[]{:S(2)}) collective-permute-start(f16[64,256]{1,0:T(8,128)(2,1)S(1)} %multiply_convert_fusion.6), channel_id=1, source_target_pairs={{0,128},{1,129},{2,130},{3,131},{4,132},{5,133},{6,134},{7,135},{8... | collective-permute-start | bytes 98312 | tf_op jit(solution)/shard_map/ppermute | solution.py:321
  76.5 4.4 %collective-permute-start.9 = (f16[64,256]{1,0:T(8,128)(2,1)S(1)}, f16[64,256]{1,0:T(8,128)(2,1)S(1)}, u32[]{:S(2)}, u32[]{:S(2)}) collective-permute-start(f16[64,256]{1,0:T(8,128)(2,1)S(1)} %multiply_convert_fusion.6), channel_id=1, source_target_pairs={{0,192},{1,193},{2,194},{3,195},{4,196},{5,197},{6,198},{7,199},{8... | collective-permute-start | bytes 98312 | tf_op jit(solution)/shard_map/ppermute | solution.py:321
  81.8 29.1 %copy-start.1 = (f32[2,256,256]{2,1,0:T(8,128)S(1)}, f32[2,256,256]{2,1,0:T(8,128)}, u32[]{:S(2)}) copy-start(f32[2,256,256]{2,1,0:T(8,128)} %block_hbm.1) | copy-start | bytes 1572868
  82.9 24.3 %all-to-all-start.1 = ((f16[32,64,256]{2,1,0:T(8,128)(2,1)}), f16[32,64,256]{2,1,0:T(8,128)(2,1)S(1)}, u32[]{:S(2)}, u32[]{:S(2)}) async-start(f16[32,64,256]{2,1,0:T(8,128)(2,1)} %broadcast_in_dim.21), calls=%async_computation.1 | async-start | bytes 2097152 | tf_op jit(solution)/shard_map/all_to_all | solution.py:308
  90.4 16.3 %collective-permute-start.11 = (f16[2,128,256]{2,1,0:T(8,128)(2,1)S(1)}, f16[2,128,256]{2,1,0:T(8,128)(2,1)S(1)}, u32[]{:S(2)}, u32[]{:S(2)}) collective-permute-start(f16[2,128,256]{2,1,0:T(8,128)(2,1)S(1)} %get-tuple-element.26), channel_id=1, source_target_pairs={{0,8},{8,0},{16,24},{24,16},{32,40},{40,32},{48,56},{56,48},{64,72... | collective-permute-start | bytes 393224 | tf_op jit(solution)/shard_map/ppermute | solution.py:353
  91.7 15.4 %collective-permute-start.10 = (f16[2,128,256]{2,1,0:T(8,128)(2,1)S(1)}, f16[2,128,256]{2,1,0:T(8,128)(2,1)S(1)}, u32[]{:S(2)}, u32[]{:S(2)}) collective-permute-start(f16[2,128,256]{2,1,0:T(8,128)(2,1)S(1)} %get-tuple-element.27), channel_id=1, source_target_pairs={{8,16},{16,8},{24,32},{32,24},{40,48},{48,40},{56,64},{64,56},{72,... | collective-permute-start | bytes 393224 | tf_op jit(solution)/shard_map/ppermute | solution.py:354
  107.2 5.4 %collective-permute-start.12 = (f16[8,256,256]{2,1,0:T(8,128)(2,1)S(1)}, f16[8,256,256]{2,1,0:T(8,128)(2,1)S(1)}, u32[]{:S(2)}, u32[]{:S(2)}) collective-permute-start(f16[8,256,256]{2,1,0:T(8,128)(2,1)S(1)} %bitcast.18), channel_id=1, source_target_pairs={{0,1},{1,0},{2,3},{3,2},{4,5},{5,4},{6,7},{7,6},{8,9},{9,8},{10,11... | collective-permute-start | bytes 3145736 | tf_op jit(solution)/shard_map/ppermute | solution.py:313

commit v3 on v2

--- a/solution.py
+++ b/solution.py
@@ -11,7 +11,7 @@
 
 
 UNROLL = 8
-GRANT = 52
+GRANT = 42
 
 
 def padded_2(cells, sides, width):
@@ -31,14 +31,13 @@
     return cells
 
 
-def fourier_blocks(length):
+def fourier_tables(length):
     position = np.arange(length)
     angles = (position[:, None] * position[None, :] % length) * (2.0 * math.pi / length)
     table_scale = 1.0 / math.sqrt(length)
     cosine_table = (np.cos(angles) * table_scale).astype(ml_dtypes.bfloat16)
     sine_table = (np.sin(angles) * table_scale).astype(ml_dtypes.bfloat16)
-    forward = np.block([[cosine_table, sine_table], [-sine_table, cosine_table]])
-    return (jnp.asarray(forward), jnp.asarray(np.ascontiguousarray(forward.T)))
+    return (jnp.asarray(cosine_table), jnp.asarray(sine_table))
 
 
 def fourier_pass(wide, left, right):
@@ -69,13 +68,13 @@
     right_hbm,
     probe_hbm,
     pattern_hbm,
-    forward_hbm,
-    backward_hbm,
-    rim_left_hbm,
-    center_hbm,
-    rim_right_hbm,
-    mine_hbm,
-    other_hbm,
+    cosine_hbm,
+    sine_hbm,
+    rim_left_ref,
+    center_ref,
+    rim_right_ref,
+    mine_ref,
+    other_ref,
     block_ref,
     above_ref,
     below_ref,
@@ -83,13 +82,10 @@
     right_ref,
     probe_ref,
     pattern_ref,
+    cosine_ref,
+    sine_ref,
     forward_ref,
     backward_ref,
-    rim_left_ref,
-    center_ref,
-    rim_right_ref,
-    mine_ref,
-    other_ref,
     padded_ref,
     window_ref,
     far_ref,
@@ -97,9 +93,6 @@
     object_ref,
     probe_sem,
     piece_sem,
-    mine_sem,
-    other_sem,
-    grad_sem,
 ):
     modes, length = probe_ref.shape[1], probe_ref.shape[2]
     half = length // 2
@@ -111,12 +104,6 @@
         return pltpu.make_async_copy(
             probe_hbm.at[:, mode], probe_ref.at[:, mode], probe_sem.at[mode]
         )
-
-    def send_mine(mode):
-        return pltpu.make_async_copy(mine_ref.at[mode], mine_hbm.at[mode], mine_sem.at[mode])
-
-    def send_other(mode):
-        return pltpu.make_async_copy(other_ref.at[mode], other_hbm.at[mode], other_sem.at[mode])
 
     fetches = [
         pltpu.make_async_copy(source, target, piece_sem.at[index])
@@ -127,18 +114,29 @@
                 (above_hbm, above_ref),
                 (below_hbm, below_ref),
                 (block_hbm, block_ref),
-                (forward_hbm, forward_ref),
-                (backward_hbm, backward_ref),
+                (cosine_hbm, cosine_ref),
+                (sine_hbm, sine_ref),
                 (pattern_hbm, pattern_ref),
             )
         )
     ]
-    for fetch in fetches:
+    for fetch in fetches[5:7] + fetches[:5] + fetches[7:]:
         fetch.start()
     for mode in range(modes):
         fetch_probe(mode).start()
     for part_ref in (rim_left_ref, center_ref, rim_right_ref, level_ref, object_ref):
         part_ref[...] = jnp.zeros_like(part_ref)
+    for fetch in fetches[5:7]:
+        fetch.wait()
+    low, high = slice(0, length), slice(length, 2 * length)
+    cosine, sine = cosine_ref[...], sine_ref[...]
+    for table_ref in (forward_ref, backward_ref):
+        table_ref[low, low] = cosine
+        table_ref[high, high] = cosine
+    forward_ref[low, high] = sine
+    backward_ref[high, low] = sine
+    forward_ref[high, low] = -sine
+    backward_ref[low, high] = -sine
     for fetch in fetches[:5]:
         fetch.wait()
     padded_ref[:, :, :half] = left_ref[...].astype(jnp.float32)
@@ -158,8 +156,7 @@
         for part in range(2):
             strip = pltpu.roll(padded_ref[part, span, :], wide - col, 1)[:, :length]
             window_ref[slot, part] = pltpu.roll(strip, length + 8 - shift, 0)[:length]
-    for fetch in fetches[5:]:
-        fetch.wait()
+    fetches[7].wait()
 
     def go_forward(mode, carry):
         fetch_probe(mode).wait()
@@ -204,8 +201,6 @@
             term_imag += win_real * back_imag - win_imag * back_real
         mine_ref[mode] = jnp.where(first, term_real, term_imag)
         other_ref[mode] = jnp.where(first, term_imag, term_real)
-        send_other(mode).start()
-        send_mine(mode).start()
         return carry
 
     lax.fori_loop(0, modes, go_back, 0, unroll=UNROLL)
@@ -223,33 +218,16 @@
             rim_left_ref[part, span, :] += strip[:, :half]
             center_ref[part, span, :] += strip[:, half : half + cols]
             rim_right_ref[part, span, :] += strip[:, half + cols :]
-    sends = [
-        pltpu.make_async_copy(source, target, grad_sem.at[index])
-        for index, (source, target) in enumerate(
-            (
-                (rim_left_ref, rim_left_hbm),
-                (center_ref, center_hbm),
-                (rim_right_ref, rim_right_hbm),
-            )
-        )
-    ]
-    for send in sends:
-        send.start()
-    for mode in range(modes):
-        send_other(mode).wait()
-        send_mine(mode).wait()
-    for send in sends:
-        send.wait()
 
 
 def device_gradients(place, block, above, below, left, right, probe, pattern):
-    forward, backward = fourier_blocks(probe.shape[-1])
+    cosine, sine = fourier_tables(probe.shape[-1])
     _, modes, length, _ = probe.shape
     rows, cols = block.shape[1] + length, block.shape[2] + length
     slots = pattern.shape[0]
     anywhere = pl.BlockSpec(memory_space=pl.ANY)
     f32 = jnp.float32
-    fetched = (block, above, below, left, right, probe, pattern, forward, backward)
+    fetched = (block, above, below, left, right, probe, pattern, cosine, sine)
     made = (
         jax.ShapeDtypeStruct((2, rows, length // 2), f32),
         jax.ShapeDtypeStruct((2, rows, block.shape[2]), f32),
@@ -261,9 +239,11 @@
         gradients_kernel,
         out_shape=made,
         in_specs=[pl.BlockSpec(memory_space=pltpu.SMEM)] + [anywhere] * len(fetched),
-        out_specs=(anywhere,) * len(made),
-        scratch_shapes=[pltpu.VMEM(item.shape, item.dtype) for item in fetched + made]
+        out_specs=(pl.BlockSpec(memory_space=pltpu.VMEM),) * len(made),
+        scratch_shapes=[pltpu.VMEM(item.shape, item.dtype) for item in fetched]
         + [
+            pltpu.VMEM((2 * length, 2 * length), jnp.bfloat16),
+            pltpu.VMEM((2 * length, 2 * length), jnp.bfloat16),
             pltpu.VMEM((2, rows, cols), f32),
             pltpu.VMEM((slots, 2, length, length), f32),
             pltpu.VMEM((modes, slots * length, 2 * length), f32),
@@ -271,9 +251,6 @@
             pltpu.VMEM((slots, 2, length, length), f32),
             pltpu.SemaphoreType.DMA((modes,)),
             pltpu.SemaphoreType.DMA((8,)),
-            pltpu.SemaphoreType.DMA((modes,)),
-            pltpu.SemaphoreType.DMA((modes,)),
-            pltpu.SemaphoreType.DMA((3,)),
         ],
         compiler_params=pltpu.CompilerParams(vmem_limit_bytes=GRANT * 1024 * 1024),
         cost_estimate=pl.CostEstimate(
@@ -388,11 +365,12 @@
     from_left, from_right = trade(rim_left, rim_right, "scan")
     center = center + widen(jnp.concatenate([from_left, from_right], axis=2), 64.0)
     piece, center = lax.optimization_barrier((piece, center))
+    region, scan = lax.axis_index("region"), lax.axis_index("scan")
+    spot = (region % 8 * 4 + scan // 2) * piece.shape[0]
+    flat = probe_modes.reshape(2, -1, probe_modes.shape[-1])
+    mine = lax.dynamic_slice(flat, (core, spot, 0), (1, *piece.shape))[0]
+    piece, mine = lax.optimization_barrier((piece, mine))
     total = sum_far(piece)
-    region, scan = lax.axis_index("region"), lax.axis_index("scan")
-    spot = (region % 8 * 4 + scan // 2) * total.shape[0]
-    flat = probe_modes.reshape(2, -1, probe_modes.shape[-1])
-    mine = lax.dynamic_slice(flat, (core, spot, 0), (1, *total.shape))[0]
     updated = narrow(mine - probe_step[0] * total, 128.0)
     updated, center = lax.optimization_barrier((updated, center))
     from_above, from_below = trade(center[:, :half_width], center[:, -half_width:], "region")

time: 116 us -> 112 us (0.966)
  Pallas kernels: 18.4 us -> 16.1 us
  waiting for transfers between devices: 37.3 us -> 36 us
    convert_element_type x4, other arithmetic: 4.25 us -> 1.69 us  [narrow(): return (values * (1.0 / scale)).astype(jnp.float16)]
    pallas_call x1, Pallas kernels: 18.4 us -> 16.1 us  [device_gradients(): pl.pallas_call(gradients_kernel, out_shape=made, in_specs=[pl.BlockSpec(m...]
    ppermute x4, waiting for transfers between devices: 21.7 us -> 20.4 us  [neighbours(): outer = lax.ppermute(jnp.where(even, head, tail), axis, swaps[1])]
    reduce_sum x1, other arithmetic: 0.22 us -> 1.45 us  [sum_scattered(): return jnp.sum(widen(pieces, 16.0), axis=0)]
  transfers between devices with their start and end apart: 15 -> 15, of which waited for: 9 -> 9; matrix products, arithmetic and copies ran while one was open for 1% -> 3% of each run, Pallas kernels for 0% -> 0%
where the time goes in v3:
time: 112 us
  starting transfers between devices  45.9 us (41%)
  waiting for transfers between devices  36 us (32%)
  Pallas kernels  16.1 us (14%)
  other arithmetic  9.27 us (8%)
  between operations  2.3 us (2%)
  local copies, waits for them, and re-layouts  2.05 us (2%)
    ppermute x4, waiting for transfers between devices, neighbours(): outer = lax.ppermute(jnp.where(even, head, tail), axis, swaps[1])  20.4 us
    pallas_call x1, Pallas kernels, device_gradients(): pl.pallas_call(gradients_kernel, out_shape=made, in_specs=[pl.BlockSpec(m...  16.1 us
    all_to_all x2, starting transfers between devices, exchange(): lax.all_to_all(parts, ('region', 'scan'), 0, 0, axis_index_groups=axis_gr...  14.3 us
    ppermute x4, starting transfers between devices, neighbours(): outer = lax.ppermute(jnp.where(even, head, tail), axis, swaps[1])  13.7 us
    ppermute x4, waiting for transfers between devices, neighbours(): inner = lax.ppermute(jnp.where(even, tail, head), axis, swaps[0])  11.3 us
    ppermute x3, starting transfers between devices, shift_far(): return lax.ppermute(values, ('region', 'scan'), pairs)  9.73 us
    ppermute x4, starting transfers between devices, neighbours(): inner = lax.ppermute(jnp.where(even, tail, head), axis, swaps[0])  4.95 us
    ppermute x2, waiting for transfers between devices, swap_cores(): lax.ppermute(values, ('region', 'scan'), [(i, i ^ 1) for i in range(count)])  3.37 us
  transfers between devices with their start and end apart: 15, of which 9 were waited for; matrix products, arithmetic and copies ran while one was open for 3% of the time, Pallas kernels for 0%

profile of v3, /device:TPU:33, one launch (start us, length us, event | category | flops | bytes accessed | tf_op | source)
XLA Modules:
  0.0 111.6 jit_solution(15719363312358580708)
XLA Ops:
  0.7 1.1 convert_element_type.54
  1.7 0.0 copy-start
  1.8 0.0 copy-start.1
  1.8 0.0 copy-start.2
  1.8 0.0 copy-start.3
  1.8 1.4 %collective-permute-start.1 = (bf16[2,128,256]{2,1,0:T(8,128)(2,1)S(1)}, bf16[2,128,256]{2,1,0:T(8,128)(2,1)S(1)}, u32[]{:S(2)}, u32[]{:S(2)}) collective-permute-start(bf16[2,128,256]{2,1,0:T(8,128)(2,1)S(1)} %get-tuple-element.44), channel_id=1, source_target_pairs={{0,8},{8,0},{16,24},{24,16},{32,40},{40,32},{48,56},{56,48},{64,72... | collective-permute-start | bytes 393224 | tf_op jit(solution)/shard_map/ppermute | solution.py:330
  3.2 3.3 %collective-permute-start = (bf16[2,128,256]{2,1,0:T(8,128)(2,1)S(1)}, bf16[2,128,256]{2,1,0:T(8,128)(2,1)S(1)}, u32[]{:S(2)}, u32[]{:S(2)}) collective-permute-start(bf16[2,128,256]{2,1,0:T(8,128)(2,1)S(1)} %get-tuple-element.45), channel_id=1, source_target_pairs={{8,16},{16,8},{24,32},{32,24},{40,48},{48,40},{56,64},{64,56},{72,... | collective-permute-start | bytes 393224 | tf_op jit(solution)/shard_map/ppermute | solution.py:331
  6.6 0.0 collective-permute-done.1
  6.6 4.4 %collective-permute-done = bf16[2,128,256]{2,1,0:T(8,128)(2,1)S(1)} collective-permute-done((bf16[2,128,256]{2,1,0:T(8,128)(2,1)S(1)}, bf16[2,128,256]{2,1,0:T(8,128)(2,1)S(1)}, u32[]{:S(2)}, u32[]{:S(2)}) %collective-permute-start) | collective-permute-done | bytes 131104 | tf_op jit(solution)/shard_map/ppermute | solution.py:331
  11.1 2.2 %collective-permute-start.3 = (bf16[2,512,128]{2,1,0:T(8,128)(2,1)S(1)}, bf16[2,512,128]{2,1,0:T(8,128)(2,1)S(1)}, u32[]{:S(2)}, u32[]{:S(2)}) collective-permute-start(bf16[2,512,128]{2,1,0:T(8,128)(2,1)S(1)} %get-tuple-element.38), channel_id=1, source_target_pairs={{0,1},{1,0},{2,3},{3,2},{4,5},{5,4},{6,7},{7,6},{8,9},{9,8},{10,11... | collective-permute-start | bytes 786440 | tf_op jit(solution)/shard_map/ppermute | solution.py:330
  13.3 3.0 %collective-permute-start.2 = (bf16[2,512,128]{2,1,0:T(8,128)(2,1)S(1)}, bf16[2,512,128]{2,1,0:T(8,128)(2,1)S(1)}, u32[]{:S(2)}, u32[]{:S(2)}) collective-permute-start(bf16[2,512,128]{2,1,0:T(8,128)(2,1)S(1)} %get-tuple-element.39), channel_id=1, source_target_pairs={{1,2},{2,1},{3,4},{4,3},{5,6},{6,5},{9,10},{10,9},{11,12},{12,11},... | collective-permute-start | bytes 786440 | tf_op jit(solution)/shard_map/ppermute | solution.py:331
  16.4 0.1 pad.9.clone
  16.5 0.1 add_add_fusion.place_ref
  16.5 0.0 collective-permute-done.3
  16.5 4.5 %collective-permute-done.2 = bf16[2,512,128]{2,1,0:T(8,128)(2,1)S(1)} collective-permute-done((bf16[2,512,128]{2,1,0:T(8,128)(2,1)S(1)}, bf16[2,512,128]{2,1,0:T(8,128)(2,1)S(1)}, u32[]{:S(2)}, u32[]{:S(2)}) %collective-permute-start.2) | collective-permute-done | bytes 262176 | tf_op jit(solution)/shard_map/ppermute | solution.py:331
  21.1 16.1 %shard_map.104 = (f32[2,512,128]{2,1,0:T(8,128)S(1)}, f32[2,512,256]{2,1,0:T(8,128)S(1)}, f32[2,512,128]{2,1,0:T(8,128)S(1)}, f32[8,256,256]{2,1,0:T(8,128)S(1)}, f32[8,256,256]{2,1,0:T(8,128)S(1)}) custom-call(s32[3,2]{1,0:T(4,128)S(1)} %add_add_fusion.place_ref, f32[2,256,256]{2,1,0:T(8,128)S(1)} %copy-done, ...), custom_call_target="tpu_custom_call" | custom-call | flops 8589934592 | bytes 16777216 | tf_op jit(solution)/shard_map/pallas_call | solution.py:238
  37.2 0.3 multiply_convert_fusion.1
  37.5 0.1 collective-permute-start.4
  37.6 2.6 %collective-permute-done.4 = f16[8,256,256]{2,1,0:T(8,128)(2,1)S(1)} collective-permute-done((f16[8,256,256]{2,1,0:T(8,128)(2,1)S(1)}, f16[8,256,256]{2,1,0:T(8,128)(2,1)S(1)}, u32[]{:S(2)}, u32[]{:S(2)}) %collective-permute-start.4) | collective-permute-done | bytes 1048608 | tf_op jit(solution)/shard_map/ppermute | solution.py:290
  40.2 1.4 %multiply_convert_fusion = f16[8,256,256]{2,1,0:T(8,128)(2,1)} fusion(f32[8,256,256]{2,1,0:T(8,128)S(1)} %get-tuple-element.16, f16[8,256,256]{2,1,0:T(8,128)(2,1)S(1)} %collective-permute-done.4), kind=kLoop, calls=%fused_computation.2 | loop fusion | flops 2621440 | bytes 4194304 | tf_op jit(solution)/shard_map/convert_element_type | solution.py:277
  41.6 7.0 %all-to-all-start = ((f16[32,64,256]{2,1,0:T(8,128)(2,1)}), f16[32,64,256]{2,1,0:T(8,128)(2,1)}, u32[]{:S(2)}, u32[]{:S(2)}) async-start(f16[32,64,256]{2,1,0:T(8,128)(2,1)} %bitcast.17), calls=%async_computation | async-start | bytes 2097152 | tf_op jit(solution)/shard_map/all_to_all | solution.py:285
  48.6 0.8 broadcast_select_fusion.3
  49.4 3.7 %collective-permute-start.5 = (f16[2,512,128]{2,1,0:T(8,128)(2,1)}, f16[2,512,128]{2,1,0:T(8,128)(2,1)S(1)}, u32[]{:S(2)}, u32[]{:S(2)}) collective-permute-start(f16[2,512,128]{2,1,0:T(8,128)(2,1)} %get-tuple-element.32), channel_id=1, source_target_pairs={{1,2},{2,1},{3,4},{4,3},{5,6},{6,5},{9,10},{10,9},{11,12},{12,11},... | collective-permute-start | bytes 786440 | tf_op jit(solution)/shard_map/ppermute | solution.py:331
  53.1 0.1 collective-permute-start.6
  53.3 0.9 dynamic-slice_bitcast_fusion
  54.1 11.1 %collective-permute-done.5 = f16[2,512,128]{2,1,0:T(8,128)(2,1)S(1)} collective-permute-done((f16[2,512,128]{2,1,0:T(8,128)(2,1)}, f16[2,512,128]{2,1,0:T(8,128)(2,1)S(1)}, u32[]{:S(2)}, u32[]{:S(2)}) %collective-permute-start.5) | collective-permute-done | bytes 262176 | tf_op jit(solution)/shard_map/ppermute | solution.py:331
  65.2 0.1 broadcast_select_fusion.1
  65.4 0.2 multiply_add_fusion
  65.5 1.4 %multiply_reduce_fusion = f32[64,256]{1,0:T(8,128)S(1)} fusion(f16[32,64,256]{2,1,0:T(8,128)(2,1)} %all-to-all-done), kind=kLoop, calls=%fused_computation.1 | loop fusion | flops 1556480 | bytes 1114112 | tf_op jit(solution)/shard_map/reduce_sum | solution.py:307
  67.0 4.4 %collective-permute-start.8 = (f16[64,256]{1,0:T(8,128)(2,1)S(1)}, f16[64,256]{1,0:T(8,128)(2,1)S(1)}, u32[]{:S(2)}, u32[]{:S(2)}) collective-permute-start(f16[64,256]{1,0:T(8,128)(2,1)S(1)} %multiply_convert_fusion.7), channel_id=1, source_target_pairs={{0,64},{1,65},{2,66},{3,67},{4,68},{5,69},{6,70},{7,71},{8,72},{9,... | collective-permute-start | bytes 98312 | tf_op jit(solution)/shard_map/ppermute | solution.py:298
  71.4 2.5 %collective-permute-start.7 = (f16[64,256]{1,0:T(8,128)(2,1)S(1)}, f16[64,256]{1,0:T(8,128)(2,1)S(1)}, u32[]{:S(2)}, u32[]{:S(2)}) collective-permute-start(f16[64,256]{1,0:T(8,128)(2,1)S(1)} %multiply_convert_fusion.7), channel_id=1, source_target_pairs={{0,128},{1,129},{2,130},{3,131},{4,132},{5,133},{6,134},{7,135},{8... | collective-permute-start | bytes 98312 | tf_op jit(solution)/shard_map/ppermute | solution.py:298
  73.9 2.8 %collective-permute-start.9 = (f16[64,256]{1,0:T(8,128)(2,1)S(1)}, f16[64,256]{1,0:T(8,128)(2,1)S(1)}, u32[]{:S(2)}, u32[]{:S(2)}) collective-permute-start(f16[64,256]{1,0:T(8,128)(2,1)S(1)} %multiply_convert_fusion.7), channel_id=1, source_target_pairs={{0,192},{1,193},{2,194},{3,195},{4,196},{5,197},{6,198},{7,199},{8... | collective-permute-start | bytes 98312 | tf_op jit(solution)/shard_map/ppermute | solution.py:298
  77.4 0.0 collective-permute-done.8
  77.4 0.8 collective-permute-done.7
  78.2 0.1 collective-permute-done.9
  78.3 1.1 broadcast_in_dim.21
  79.4 7.3 %all-to-all-start.1 = ((f16[32,64,256]{2,1,0:T(8,128)(2,1)}), f16[32,64,256]{2,1,0:T(8,128)(2,1)S(1)}, u32[]{:S(2)}, u32[]{:S(2)}) async-start(f16[32,64,256]{2,1,0:T(8,128)(2,1)} %broadcast_in_dim.21), calls=%async_computation.1 | async-start | bytes 2097152 | tf_op jit(solution)/shard_map/all_to_all | solution.py:285
  86.8 0.1 broadcast_select_fusion.10
  86.9 1.3 %collective-permute-start.11 = (f16[2,128,256]{2,1,0:T(8,128)(2,1)S(1)}, f16[2,128,256]{2,1,0:T(8,128)(2,1)S(1)}, u32[]{:S(2)}, u32[]{:S(2)}) collective-permute-start(f16[2,128,256]{2,1,0:T(8,128)(2,1)S(1)} %get-tuple-element.30), channel_id=1, source_target_pairs={{0,8},{8,0},{16,24},{24,16},{32,40},{40,32},{48,56},{56,48},{64,72... | collective-permute-start | bytes 393224 | tf_op jit(solution)/shard_map/ppermute | solution.py:330
  88.1 3.7 %collective-permute-start.10 = (f16[2,128,256]{2,1,0:T(8,128)(2,1)S(1)}, f16[2,128,256]{2,1,0:T(8,128)(2,1)S(1)}, u32[]{:S(2)}, u32[]{:S(2)}) collective-permute-start(f16[2,128,256]{2,1,0:T(8,128)(2,1)S(1)} %get-tuple-element.31), channel_id=1, source_target_pairs={{8,16},{16,8},{24,32},{32,24},{40,48},{48,40},{56,64},{64,56},{72,... | collective-permute-start | bytes 393224 | tf_op jit(solution)/shard_map/ppermute | solution.py:331
  91.8 11.3 %collective-permute-done.11 = f16[2,128,256]{2,1,0:T(8,128)(2,1)S(1)} collective-permute-done((f16[2,128,256]{2,1,0:T(8,128)(2,1)S(1)}, f16[2,128,256]{2,1,0:T(8,128)(2,1)S(1)}, u32[]{:S(2)}, u32[]{:S(2)}) %collective-permute-start.11) | collective-permute-done | bytes 131104 | tf_op jit(solution)/shard_map/ppermute | solution.py:330
  103.1 0.4 collective-permute-done.10
  103.5 0.1 broadcast_select_fusion.8
  103.6 0.0 all-to-all-done.1
  103.6 3.1 %collective-permute-start.12 = (f16[8,256,256]{2,1,0:T(8,128)(2,1)S(1)}, f16[8,256,256]{2,1,0:T(8,128)(2,1)S(1)}, u32[]{:S(2)}, u32[]{:S(2)}) collective-permute-start(f16[8,256,256]{2,1,0:T(8,128)(2,1)S(1)} %bitcast.15), channel_id=1, source_target_pairs={{0,1},{1,0},{2,3},{3,2},{4,5},{5,4},{6,7},{7,6},{8,9},{9,8},{10,11... | collective-permute-start | bytes 3145736 | tf_op jit(solution)/shard_map/ppermute | solution.py:290
  107.4 0.9 multiply_subtract_fusion
  108.3 0.7 collective-permute-done.12
  109.0 2.6 %convert_multiply_fusion = f32[2,8,256,256]{3,2,1,0:T(8,128)} fusion(pred[2]{0:T(512)(128)(4,1)S(1)} %iota_compare_fusion, f16[8,256,256]{2,1,0:T(8,128)(2,1)S(1)} %collective-permute-done.12, f16[8,256,256]{2,1,0:T(8,128)(2,1)S(1)} %bitcast.16), kind=kLoop, calls=%fused_computation | loop fusion | flops 3145728 | bytes 6291458 | tf_op jit(solution)/shard_map/mul | solution.py:281
  (19 shorter events, 0.2 us)
Async XLA Ops:
  0.6 15.7 %copy-start.4 = (s32[1,1,2]{2,1,0:T(1,128)S(1)}, s32[1,1,2]{2,1,0:T(1,128)}, u32[]{:S(2)}) copy-start(s32[1,1,2]{2,1,0:T(1,128)} %param.13) | copy-start | bytes 28
  0.6 15.7 %copy-start.5 = (s32[1,1,2]{2,1,0:T(1,128)S(1)}, s32[1,1,2]{2,1,0:T(1,128)}, u32[]{:S(2)}) copy-start(s32[1,1,2]{2,1,0:T(1,128)} %param.12) | copy-start | bytes 28
  1.7 19.3 %copy-start = (f32[2,256,256]{2,1,0:T(8,128)S(1)}, f32[2,256,256]{2,1,0:T(8,128)}, u32[]{:S(2)}) copy-start(f32[2,256,256]{2,1,0:T(8,128)} %block_hbm.1) | copy-start | bytes 1572868
  1.8 19.3 %copy-start.1 = (f32[1,1,2,256,256]{4,3,2,1,0:T(8,128)S(1)}, f32[1,1,2,256,256]{4,3,2,1,0:T(8,128)}, u32[]{:S(2)}) copy-start(f32[1,1,2,256,256]{4,3,2,1,0:T(8,128)} %param.11) | copy-start | bytes 1572868
  1.8 19.3 %copy-start.2 = (bf16[256,256]{1,0:T(8,128)(2,1)S(1)}, bf16[256,256]{1,0:T(8,128)(2,1)}, u32[]{:S(2)}) copy-start(bf16[256,256]{1,0:T(8,128)(2,1)} %constant.109.clone.sine_hbm) | copy-start | bytes 393220
  1.8 19.3 %copy-start.3 = (bf16[256,256]{1,0:T(8,128)(2,1)S(1)}, bf16[256,256]{1,0:T(8,128)(2,1)}, u32[]{:S(2)}) copy-start(bf16[256,256]{1,0:T(8,128)(2,1)} %constant.108.clone.cosine_hbm) | copy-start | bytes 393220
  1.8 4.8 %collective-permute-start.1 = (bf16[2,128,256]{2,1,0:T(8,128)(2,1)S(1)}, bf16[2,128,256]{2,1,0:T(8,128)(2,1)S(1)}, u32[]{:S(2)}, u32[]{:S(2)}) collective-permute-start(bf16[2,128,256]{2,1,0:T(8,128)(2,1)S(1)} %get-tuple-element.44), channel_id=1, source_target_pairs={{0,8},{8,0},{16,24},{24,16},{32,40},{40,32},{48,56},{56,48},{64,72... | collective-permute-start | bytes 393224 | tf_op jit(solution)/shard_map/ppermute | solution.py:330
  3.2 7.8 %collective-permute-start = (bf16[2,128,256]{2,1,0:T(8,128)(2,1)S(1)}, bf16[2,128,256]{2,1,0:T(8,128)(2,1)S(1)}, u32[]{:S(2)}, u32[]{:S(2)}) collective-permute-start(bf16[2,128,256]{2,1,0:T(8,128)(2,1)S(1)} %get-tuple-element.45), channel_id=1, source_target_pairs={{8,16},{16,8},{24,32},{32,24},{40,48},{48,40},{56,64},{64,56},{72,... | collective-permute-start | bytes 393224 | tf_op jit(solution)/shard_map/ppermute | solution.py:331
  11.1 5.4 %collective-permute-start.3 = (bf16[2,512,128]{2,1,0:T(8,128)(2,1)S(1)}, bf16[2,512,128]{2,1,0:T(8,128)(2,1)S(1)}, u32[]{:S(2)}, u32[]{:S(2)}) collective-permute-start(bf16[2,512,128]{2,1,0:T(8,128)(2,1)S(1)} %get-tuple-element.38), channel_id=1, source_target_pairs={{0,1},{1,0},{2,3},{3,2},{4,5},{5,4},{6,7},{7,6},{8,9},{9,8},{10,11... | collective-permute-start | bytes 786440 | tf_op jit(solution)/shard_map/ppermute | solution.py:330
  13.3 7.7 %collective-permute-start.2 = (bf16[2,512,128]{2,1,0:T(8,128)(2,1)S(1)}, bf16[2,512,128]{2,1,0:T(8,128)(2,1)S(1)}, u32[]{:S(2)}, u32[]{:S(2)}) collective-permute-start(bf16[2,512,128]{2,1,0:T(8,128)(2,1)S(1)} %get-tuple-element.39), channel_id=1, source_target_pairs={{1,2},{2,1},{3,4},{4,3},{5,6},{6,5},{9,10},{10,9},{11,12},{12,11},... | collective-permute-start | bytes 786440 | tf_op jit(solution)/shard_map/ppermute | solution.py:331
  37.5 2.7 %collective-permute-start.4 = (f16[8,256,256]{2,1,0:T(8,128)(2,1)S(1)}, f16[8,256,256]{2,1,0:T(8,128)(2,1)S(1)}, u32[]{:S(2)}, u32[]{:S(2)}) collective-permute-start(f16[8,256,256]{2,1,0:T(8,128)(2,1)S(1)} %multiply_convert_fusion.1), channel_id=1, source_target_pairs={{0,1},{1,0},{2,3},{3,2},{4,5},{5,4},{6,7},{7,6},{8,9},{9,8},{10,11... | collective-permute-start | bytes 3145736 | tf_op jit(solution)/shard_map/ppermute | solution.py:290
  41.6 23.9 %all-to-all-start = ((f16[32,64,256]{2,1,0:T(8,128)(2,1)}), f16[32,64,256]{2,1,0:T(8,128)(2,1)}, u32[]{:S(2)}, u32[]{:S(2)}) async-start(f16[32,64,256]{2,1,0:T(8,128)(2,1)} %bitcast.17), calls=%async_computation | async-start | bytes 2097152 | tf_op jit(solution)/shard_map/all_to_all | solution.py:285
  49.4 15.8 %collective-permute-start.5 = (f16[2,512,128]{2,1,0:T(8,128)(2,1)}, f16[2,512,128]{2,1,0:T(8,128)(2,1)S(1)}, u32[]{:S(2)}, u32[]{:S(2)}) collective-permute-start(f16[2,512,128]{2,1,0:T(8,128)(2,1)} %get-tuple-element.32), channel_id=1, source_target_pairs={{1,2},{2,1},{3,4},{4,3},{5,6},{6,5},{9,10},{10,9},{11,12},{12,11},... | collective-permute-start | bytes 786440 | tf_op jit(solution)/shard_map/ppermute | solution.py:331
  53.1 12.1 %collective-permute-start.6 = (f16[2,512,128]{2,1,0:T(8,128)(2,1)S(1)}, f16[2,512,128]{2,1,0:T(8,128)(2,1)S(1)}, u32[]{:S(2)}, u32[]{:S(2)}) collective-permute-start(f16[2,512,128]{2,1,0:T(8,128)(2,1)S(1)} %get-tuple-element.33), channel_id=1, source_target_pairs={{0,1},{1,0},{2,3},{3,2},{4,5},{5,4},{6,7},{7,6},{8,9},{9,8},{10,11... | collective-permute-start | bytes 786440 | tf_op jit(solution)/shard_map/ppermute | solution.py:330
  67.0 10.4 %collective-permute-start.8 = (f16[64,256]{1,0:T(8,128)(2,1)S(1)}, f16[64,256]{1,0:T(8,128)(2,1)S(1)}, u32[]{:S(2)}, u32[]{:S(2)}) collective-permute-start(f16[64,256]{1,0:T(8,128)(2,1)S(1)} %multiply_convert_fusion.7), channel_id=1, source_target_pairs={{0,64},{1,65},{2,66},{3,67},{4,68},{5,69},{6,70},{7,71},{8,72},{9,... | collective-permute-start | bytes 98312 | tf_op jit(solution)/shard_map/ppermute | solution.py:298
  71.4 6.8 %collective-permute-start.7 = (f16[64,256]{1,0:T(8,128)(2,1)S(1)}, f16[64,256]{1,0:T(8,128)(2,1)S(1)}, u32[]{:S(2)}, u32[]{:S(2)}) collective-permute-start(f16[64,256]{1,0:T(8,128)(2,1)S(1)} %multiply_convert_fusion.7), channel_id=1, source_target_pairs={{0,128},{1,129},{2,130},{3,131},{4,132},{5,133},{6,134},{7,135},{8... | collective-permute-start | bytes 98312 | tf_op jit(solution)/shard_map/ppermute | solution.py:298
  73.9 4.4 %collective-permute-start.9 = (f16[64,256]{1,0:T(8,128)(2,1)S(1)}, f16[64,256]{1,0:T(8,128)(2,1)S(1)}, u32[]{:S(2)}, u32[]{:S(2)}) collective-permute-start(f16[64,256]{1,0:T(8,128)(2,1)S(1)} %multiply_convert_fusion.7), channel_id=1, source_target_pairs={{0,192},{1,193},{2,194},{3,195},{4,196},{5,197},{6,198},{7,199},{8... | collective-permute-start | bytes 98312 | tf_op jit(solution)/shard_map/ppermute | solution.py:298
  79.4 24.2 %all-to-all-start.1 = ((f16[32,64,256]{2,1,0:T(8,128)(2,1)}), f16[32,64,256]{2,1,0:T(8,128)(2,1)S(1)}, u32[]{:S(2)}, u32[]{:S(2)}) async-start(f16[32,64,256]{2,1,0:T(8,128)(2,1)} %broadcast_in_dim.21), calls=%async_computation.1 | async-start | bytes 2097152 | tf_op jit(solution)/shard_map/all_to_all | solution.py:285
  86.9 16.3 %collective-permute-start.11 = (f16[2,128,256]{2,1,0:T(8,128)(2,1)S(1)}, f16[2,128,256]{2,1,0:T(8,128)(2,1)S(1)}, u32[]{:S(2)}, u32[]{:S(2)}) collective-permute-start(f16[2,128,256]{2,1,0:T(8,128)(2,1)S(1)} %get-tuple-element.30), channel_id=1, source_target_pairs={{0,8},{8,0},{16,24},{24,16},{32,40},{40,32},{48,56},{56,48},{64,72... | collective-permute-start | bytes 393224 | tf_op jit(solution)/shard_map/ppermute | solution.py:330
  88.1 15.4 %collective-permute-start.10 = (f16[2,128,256]{2,1,0:T(8,128)(2,1)S(1)}, f16[2,128,256]{2,1,0:T(8,128)(2,1)S(1)}, u32[]{:S(2)}, u32[]{:S(2)}) collective-permute-start(f16[2,128,256]{2,1,0:T(8,128)(2,1)S(1)} %get-tuple-element.31), channel_id=1, source_target_pairs={{8,16},{16,8},{24,32},{32,24},{40,48},{48,40},{56,64},{64,56},{72,... | collective-permute-start | bytes 393224 | tf_op jit(solution)/shard_map/ppermute | solution.py:331
  103.6 5.4 %collective-permute-start.12 = (f16[8,256,256]{2,1,0:T(8,128)(2,1)S(1)}, f16[8,256,256]{2,1,0:T(8,128)(2,1)S(1)}, u32[]{:S(2)}, u32[]{:S(2)}) collective-permute-start(f16[8,256,256]{2,1,0:T(8,128)(2,1)S(1)} %bitcast.15), channel_id=1, source_target_pairs={{0,1},{1,0},{2,3},{3,2},{4,5},{5,4},{6,7},{7,6},{8,9},{9,8},{10,11... | collective-permute-start | bytes 3145736 | tf_op jit(solution)/shard_map/ppermute | solution.py:290

commit v4 on v3

--- a/solution.py
+++ b/solution.py
@@ -37,7 +37,53 @@
     table_scale = 1.0 / math.sqrt(length)
     cosine_table = (np.cos(angles) * table_scale).astype(ml_dtypes.bfloat16)
     sine_table = (np.sin(angles) * table_scale).astype(ml_dtypes.bfloat16)
-    return (jnp.asarray(cosine_table), jnp.asarray(sine_table))
+    order = mirrored(length)
+    half = length // 2
+    folded = np.concatenate(
+        [cosine_table[:half], cosine_table[half : half + 1], sine_table[1:half]], axis=0
+    )
+    cosine_table, sine_table = cosine_table[:, order], sine_table[:, order]
+    tables = (folded, folded.T, cosine_table, sine_table, cosine_table.T, sine_table.T)
+    return jnp.asarray(np.stack(tables))
+
+
+def mirrored(length):
+    half = length // 2
+    return np.concatenate([np.arange(half + 1), np.arange(length - 1, half, -1)])
+
+
+def combined(even, odd, swapped_even, swapped_odd, edge):
+    return (
+        even + jnp.where(edge, 0.0, odd),
+        jnp.where(edge, swapped_odd, even) - jnp.where(edge, 0.0, odd),
+        swapped_even - jnp.where(edge, 0.0, swapped_odd),
+        jnp.where(edge, odd, swapped_even) + jnp.where(edge, 0.0, swapped_odd),
+    )
+
+
+def folded_pass(waves, folded, folded_across):
+    length = folded.shape[0]
+    half = length // 2
+    slots = len(waves)
+    wide = jnp.concatenate([part.astype(jnp.bfloat16) for pair in waves for part in pair], axis=1)
+    first = jnp.dot(folded, wide, preferred_element_type=jnp.float32)
+    edge = lax.broadcasted_iota(jnp.int32, (half, length), 0) == 0
+    middle = []
+    for slot in range(slots):
+        real = first[:, 2 * slot * length : (2 * slot + 1) * length]
+        imag = first[:, (2 * slot + 1) * length : (2 * slot + 2) * length]
+        parts = combined(real[:half], imag[half:], imag[:half], real[half:], edge)
+        middle += [part.astype(jnp.bfloat16) for part in parts]
+    middle = jnp.concatenate(middle, axis=0)
+    second = jnp.dot(middle, folded_across, preferred_element_type=jnp.float32)
+    edge = lax.broadcasted_iota(jnp.int32, (length, half), 1) == 0
+    out = []
+    for slot in range(slots):
+        real = second[2 * slot * length : (2 * slot + 1) * length]
+        imag = second[(2 * slot + 1) * length : (2 * slot + 2) * length]
+        parts = combined(real[:, :half], imag[:, half:], imag[:, :half], real[:, half:], edge)
+        out.append(jnp.concatenate(parts, axis=1))
+    return jnp.concatenate(out, axis=0)
 
 
 def fourier_pass(wide, left, right):
@@ -68,8 +114,7 @@
     right_hbm,
     probe_hbm,
     pattern_hbm,
-    cosine_hbm,
-    sine_hbm,
+    tables_hbm,
     rim_left_ref,
     center_ref,
     rim_right_ref,
@@ -82,10 +127,9 @@
     right_ref,
     probe_ref,
     pattern_ref,
-    cosine_ref,
-    sine_ref,
-    forward_ref,
-    backward_ref,
+    tables_ref,
+    left_table_ref,
+    right_table_ref,
     padded_ref,
     window_ref,
     far_ref,
@@ -114,29 +158,27 @@
                 (above_hbm, above_ref),
                 (below_hbm, below_ref),
                 (block_hbm, block_ref),
-                (cosine_hbm, cosine_ref),
-                (sine_hbm, sine_ref),
+                (tables_hbm, tables_ref),
                 (pattern_hbm, pattern_ref),
             )
         )
     ]
-    for fetch in fetches[5:7] + fetches[:5] + fetches[7:]:
+    for fetch in fetches[5:6] + fetches[:5] + fetches[6:]:
         fetch.start()
     for mode in range(modes):
         fetch_probe(mode).start()
     for part_ref in (rim_left_ref, center_ref, rim_right_ref, level_ref, object_ref):
         part_ref[...] = jnp.zeros_like(part_ref)
-    for fetch in fetches[5:7]:
-        fetch.wait()
+    fetches[5].wait()
     low, high = slice(0, length), slice(length, 2 * length)
-    cosine, sine = cosine_ref[...], sine_ref[...]
-    for table_ref in (forward_ref, backward_ref):
+    for table_ref, cosine, sine in (
+        (left_table_ref, tables_ref[2], -tables_ref[3]),
+        (right_table_ref, tables_ref[4], tables_ref[5]),
+    ):
         table_ref[low, low] = cosine
         table_ref[high, high] = cosine
-    forward_ref[low, high] = sine
-    backward_ref[high, low] = sine
-    forward_ref[high, low] = -sine
-    backward_ref[low, high] = -sine
+        table_ref[low, high] = sine
+        table_ref[high, low] = -sine
     for fetch in fetches[:5]:
         fetch.wait()
     padded_ref[:, :, :half] = left_ref[...].astype(jnp.float32)
@@ -156,7 +198,7 @@
         for part in range(2):
             strip = pltpu.roll(padded_ref[part, span, :], wide - col, 1)[:, :length]
             window_ref[slot, part] = pltpu.roll(strip, length + 8 - shift, 0)[:length]
-    fetches[7].wait()
+    fetches[6].wait()
 
     def go_forward(mode, carry):
         fetch_probe(mode).wait()
@@ -170,7 +212,7 @@
                     probe_real * win_imag + probe_imag * win_real,
                 )
             )
-        far = fourier_pass(stacked(waves), forward_ref[...], backward_ref[...])
+        far = folded_pass(waves, tables_ref[0], tables_ref[1])
         far_ref[mode] = far
         far_real, far_imag = far[:, :length], far[:, length:]
         level_ref[...] += far_real * far_real + far_imag * far_imag
@@ -188,7 +230,7 @@
             factor = level_ref[band]
             far = far_ref[mode, band]
             corrected.append((factor * far[:, :length], factor * far[:, length:]))
-        back = fourier_pass(stacked(corrected), backward_ref[...], forward_ref[...])
+        back = fourier_pass(stacked(corrected), left_table_ref[...], right_table_ref[...])
         probe_real, probe_imag = probe_ref[0, mode], probe_ref[1, mode]
         term_real = term_imag = 0.0
         for slot in range(slots):
@@ -221,13 +263,13 @@
 
 
 def device_gradients(place, block, above, below, left, right, probe, pattern):
-    cosine, sine = fourier_tables(probe.shape[-1])
+    tables = fourier_tables(probe.shape[-1])
     _, modes, length, _ = probe.shape
     rows, cols = block.shape[1] + length, block.shape[2] + length
     slots = pattern.shape[0]
     anywhere = pl.BlockSpec(memory_space=pl.ANY)
     f32 = jnp.float32
-    fetched = (block, above, below, left, right, probe, pattern, cosine, sine)
+    fetched = (block, above, below, left, right, probe, pattern, tables)
     made = (
         jax.ShapeDtypeStruct((2, rows, length // 2), f32),
         jax.ShapeDtypeStruct((2, rows, block.shape[2]), f32),
@@ -354,17 +396,21 @@
             jnp.broadcast_to(core, rows_at.shape[2:]).astype(jnp.int32),
         ]
     )
+    targets = pattern[0, 0]
+    for dim in (1, 2):
+        nearer = lax.slice_in_dim(targets, 0, half_width + 1, axis=dim)
+        farther = lax.slice_in_dim(targets, half_width + 1, 2 * half_width, axis=dim)
+        targets = jnp.concatenate([nearer, lax.rev(farther, (dim,))], axis=dim)
     cells = object_field.astype(jnp.bfloat16)
     above, below = edges(cells, "region", 1, half_width)
     tall = jnp.concatenate([above, cells, below], axis=1)
     left, right = edges(tall, "scan", 2, half_width)
     rim_left, center, rim_right, mine, other = device_gradients(
-        place, object_field, above, below, left, right, probe_modes, pattern[0, 0]
+        place, object_field, above, below, left, right, probe_modes, targets
     )
     piece = sum_scattered(mine, other)
     from_left, from_right = trade(rim_left, rim_right, "scan")
     center = center + widen(jnp.concatenate([from_left, from_right], axis=2), 64.0)
-    piece, center = lax.optimization_barrier((piece, center))
     region, scan = lax.axis_index("region"), lax.axis_index("scan")
     spot = (region % 8 * 4 + scan // 2) * piece.shape[0]
     flat = probe_modes.reshape(2, -1, probe_modes.shape[-1])

time: 112 us -> 110 us (0.982)
  local copies, waits for them, and re-layouts: 2.05 us -> 4.55 us
  starting transfers between devices: 45.9 us -> 44 us
  waiting for transfers between devices: 36 us -> 34.5 us
    ppermute x4, waiting for transfers between devices: 11.3 us -> 1.86 us  [neighbours(): inner = lax.ppermute(jnp.where(even, tail, head), axis, swaps[0])]
    ppermute x4, waiting for transfers between devices: 20.4 us -> 27.8 us  [neighbours(): outer = lax.ppermute(jnp.where(even, head, tail), axis, swaps[1])]
    ppermute x4, starting transfers between devices: 4.95 us -> 0.68 us  [neighbours(): inner = lax.ppermute(jnp.where(even, tail, head), axis, swaps[0])]
    ppermute x4, starting transfers between devices: 13.7 us -> 17.3 us  [neighbours(): outer = lax.ppermute(jnp.where(even, head, tail), axis, swaps[1])]
    slice x0 -> x2, local copies, waits for them, and re-layouts: none -> 1.95 us  [the longest x1 0.98 us: on_device(): nearer = lax.slice_in_dim(targets, 0, half_width + 1, axis=dim)]
    ppermute x2, starting transfers between devices: 3.21 us -> 1.42 us  [swap_cores(): lax.ppermute(values, ('region', 'scan'), [(i, i ^ 1) for i in range(count)])]
  transfers between devices with their start and end apart: 15 -> 15, of which waited for: 9 -> 8; matrix products, arithmetic and copies ran while one was open for 3% -> 5% of each run, Pallas kernels for 0% -> 0%
where the time goes in v4:
time: 110 us
  starting transfers between devices  44 us (40%)
  waiting for transfers between devices  34.5 us (31%)
  Pallas kernels  15.5 us (14%)
  other arithmetic  8.84 us (8%)
  local copies, waits for them, and re-layouts  4.55 us (4%)
  between operations  2.3 us (2%)
    ppermute x4, waiting for transfers between devices, neighbours(): outer = lax.ppermute(jnp.where(even, head, tail), axis, swaps[1])  27.8 us
    ppermute x4, starting transfers between devices, neighbours(): outer = lax.ppermute(jnp.where(even, head, tail), axis, swaps[1])  17.3 us
    pallas_call x1, Pallas kernels, device_gradients(): pl.pallas_call(gradients_kernel, out_shape=made, in_specs=[pl.BlockSpec(m...  15.5 us
    all_to_all x2, starting transfers between devices, exchange(): lax.all_to_all(parts, ('region', 'scan'), 0, 0, axis_index_groups=axis_gr...  14.8 us
    ppermute x3, starting transfers between devices, shift_far(): return lax.ppermute(values, ('region', 'scan'), pairs)  9.7 us
    ppermute x2, waiting for transfers between devices, swap_cores(): lax.ppermute(values, ('region', 'scan'), [(i, i ^ 1) for i in range(count)])  3.37 us
    mul x1, other arithmetic, widen(): return values.astype(jnp.float32) * scale  2.64 us
  transfers between devices with their start and end apart: 15, of which 8 were waited for; matrix products, arithmetic and copies ran while one was open for 5% of the time, Pallas kernels for 0%

profile of v4, /device:TPU:33, one launch (start us, length us, event | category | flops | bytes accessed | tf_op | source)
XLA Modules:
  0.0 109.6 jit_solution(11563210770784344450)
XLA Ops:
  0.7 1.1 convert_element_type.54
  1.8 4.2 %collective-permute-start = (bf16[2,128,256]{2,1,0:T(8,128)(2,1)S(1)}, bf16[2,128,256]{2,1,0:T(8,128)(2,1)S(1)}, u32[]{:S(2)}, u32[]{:S(2)}) collective-permute-start(bf16[2,128,256]{2,1,0:T(8,128)(2,1)S(1)} %get-tuple-element.41), channel_id=1, source_target_pairs={{8,16},{16,8},{24,32},{32,24},{40,48},{48,40},{56,64},{64,56},{72,... | collective-permute-start | bytes 393224 | tf_op jit(solution)/shard_map/ppermute | solution.py:373
  6.0 0.4 collective-permute-start.1
  6.4 1.0 slice.49
  7.3 1.0 slice.48
  8.3 0.2 rev.6
  8.6 0.1 pad_maximum_fusion.2
  8.7 0.4 rev.7
  9.1 0.1 slice_maximum_fusion
  9.1 1.0 collective-permute-done
  10.1 0.0 collective-permute-done.1
  10.2 0.0 copy-start.1
  10.3 4.9 %collective-permute-start.2 = (bf16[2,512,128]{2,1,0:T(8,128)(2,1)S(1)}, bf16[2,512,128]{2,1,0:T(8,128)(2,1)S(1)}, u32[]{:S(2)}, u32[]{:S(2)}) collective-permute-start(bf16[2,512,128]{2,1,0:T(8,128)(2,1)S(1)} %get-tuple-element.35), channel_id=1, source_target_pairs={{1,2},{2,1},{3,4},{4,3},{5,6},{6,5},{9,10},{10,9},{11,12},{12,11},... | collective-permute-start | bytes 786440 | tf_op jit(solution)/shard_map/ppermute | solution.py:373
  15.3 0.1 collective-permute-start.3
  15.4 0.1 pad_maximum_fusion.1.pattern_hbm
  15.5 0.1 pad.13.clone
  15.6 0.1 add_add_fusion.place_ref
  15.7 3.6 %collective-permute-done.2 = bf16[2,512,128]{2,1,0:T(8,128)(2,1)S(1)} collective-permute-done((bf16[2,512,128]{2,1,0:T(8,128)(2,1)S(1)}, bf16[2,512,128]{2,1,0:T(8,128)(2,1)S(1)}, u32[]{:S(2)}, u32[]{:S(2)}) %collective-permute-start.2) | collective-permute-done | bytes 262176 | tf_op jit(solution)/shard_map/ppermute | solution.py:373
  19.4 15.5 %shard_map.95 = (f32[2,512,128]{2,1,0:T(8,128)S(1)}, f32[2,512,256]{2,1,0:T(8,128)S(1)}, f32[2,512,128]{2,1,0:T(8,128)S(1)}, f32[8,256,256]{2,1,0:T(8,128)S(1)}, f32[8,256,256]{2,1,0:T(8,128)S(1)}) custom-call(s32[3,2]{1,0:T(4,128)S(1)} %add_add_fusion.place_ref, f32[2,256,256]{2,1,0:T(8,128)S(1)} %copy-done, ...), custom_call_target="tpu_custom_call" | custom-call | flops 8589934592 | bytes 16777216 | tf_op jit(solution)/shard_map/pallas_call | solution.py:280
  34.9 0.2 multiply_convert_fusion.1
  35.1 0.1 collective-permute-start.4
  35.2 2.6 %collective-permute-done.4 = f16[8,256,256]{2,1,0:T(8,128)(2,1)S(1)} collective-permute-done((f16[8,256,256]{2,1,0:T(8,128)(2,1)S(1)}, f16[8,256,256]{2,1,0:T(8,128)(2,1)S(1)}, u32[]{:S(2)}, u32[]{:S(2)}) %collective-permute-start.4) | collective-permute-done | bytes 1048608 | tf_op jit(solution)/shard_map/ppermute | solution.py:332
  37.9 1.4 %multiply_convert_fusion = f16[8,256,256]{2,1,0:T(8,128)(2,1)} fusion(f32[8,256,256]{2,1,0:T(8,128)S(1)} %get-tuple-element.14, f16[8,256,256]{2,1,0:T(8,128)(2,1)S(1)} %collective-permute-done.4), kind=kLoop, calls=%fused_computation.2 | loop fusion | flops 2621440 | bytes 4194304 | tf_op jit(solution)/shard_map/convert_element_type | solution.py:319
  39.2 7.8 %all-to-all-start = ((f16[32,64,256]{2,1,0:T(8,128)(2,1)}), f16[32,64,256]{2,1,0:T(8,128)(2,1)}, u32[]{:S(2)}, u32[]{:S(2)}) async-start(f16[32,64,256]{2,1,0:T(8,128)(2,1)} %bitcast.16), calls=%async_computation | async-start | bytes 2097152 | tf_op jit(solution)/shard_map/all_to_all | solution.py:327
  47.0 0.1 broadcast_select_fusion.3
  47.2 3.9 %collective-permute-start.8 = (f16[2,512,128]{2,1,0:T(8,128)(2,1)S(1)}, f16[2,512,128]{2,1,0:T(8,128)(2,1)S(1)}, u32[]{:S(2)}, u32[]{:S(2)}) collective-permute-start(f16[2,512,128]{2,1,0:T(8,128)(2,1)S(1)} %get-tuple-element.28), channel_id=1, source_target_pairs={{1,2},{2,1},{3,4},{4,3},{5,6},{6,5},{9,10},{10,9},{11,12},{12,11},... | collective-permute-start | bytes 786440 | tf_op jit(solution)/shard_map/ppermute | solution.py:373
  51.1 0.1 collective-permute-start.9
  51.9 0.9 dynamic-slice_bitcast_fusion
  52.8 10.9 %collective-permute-done.8 = f16[2,512,128]{2,1,0:T(8,128)(2,1)S(1)} collective-permute-done((f16[2,512,128]{2,1,0:T(8,128)(2,1)S(1)}, f16[2,512,128]{2,1,0:T(8,128)(2,1)S(1)}, u32[]{:S(2)}, u32[]{:S(2)}) %collective-permute-start.8) | collective-permute-done | bytes 262176 | tf_op jit(solution)/shard_map/ppermute | solution.py:373
  63.7 0.1 broadcast_select_fusion.1
  63.8 1.4 %multiply_reduce_fusion = f32[64,256]{1,0:T(8,128)S(1)} fusion(f16[32,64,256]{2,1,0:T(8,128)(2,1)} %all-to-all-done), kind=kLoop, calls=%fused_computation.1 | loop fusion | flops 1556480 | bytes 1114112 | tf_op jit(solution)/shard_map/reduce_sum | solution.py:349
  65.3 6.1 %collective-permute-start.5 = (f16[64,256]{1,0:T(8,128)(2,1)S(1)}, f16[64,256]{1,0:T(8,128)(2,1)S(1)}, u32[]{:S(2)}, u32[]{:S(2)}) collective-permute-start(f16[64,256]{1,0:T(8,128)(2,1)S(1)} %multiply_convert_fusion.7), channel_id=1, source_target_pairs={{0,128},{1,129},{2,130},{3,131},{4,132},{5,133},{6,134},{7,135},{8... | collective-permute-start | bytes 98312 | tf_op jit(solution)/shard_map/ppermute | solution.py:340
  71.4 0.7 collective-permute-start.6
  72.1 2.8 %collective-permute-start.7 = (f16[64,256]{1,0:T(8,128)(2,1)S(1)}, f16[64,256]{1,0:T(8,128)(2,1)S(1)}, u32[]{:S(2)}, u32[]{:S(2)}) collective-permute-start(f16[64,256]{1,0:T(8,128)(2,1)S(1)} %multiply_convert_fusion.7), channel_id=1, source_target_pairs={{0,192},{1,193},{2,194},{3,195},{4,196},{5,197},{6,198},{7,199},{8... | collective-permute-start | bytes 98312 | tf_op jit(solution)/shard_map/ppermute | solution.py:340
  75.0 0.2 multiply_add_fusion
  75.2 1.5 %collective-permute-done.6 = f16[64,256]{1,0:T(8,128)(2,1)S(1)} collective-permute-done((f16[64,256]{1,0:T(8,128)(2,1)S(1)}, f16[64,256]{1,0:T(8,128)(2,1)S(1)}, u32[]{:S(2)}, u32[]{:S(2)}) %collective-permute-start.6) | collective-permute-done | bytes 32800 | tf_op jit(solution)/shard_map/ppermute | solution.py:340
  76.7 1.1 broadcast_in_dim.21
  77.8 7.0 %all-to-all-start.1 = ((f16[32,64,256]{2,1,0:T(8,128)(2,1)}), f16[32,64,256]{2,1,0:T(8,128)(2,1)S(1)}, u32[]{:S(2)}, u32[]{:S(2)}) async-start(f16[32,64,256]{2,1,0:T(8,128)(2,1)} %broadcast_in_dim.21), calls=%async_computation.1 | async-start | bytes 2097152 | tf_op jit(solution)/shard_map/all_to_all | solution.py:327
  84.8 0.1 broadcast_select_fusion.10
  84.9 4.3 %collective-permute-start.10 = (f16[2,128,256]{2,1,0:T(8,128)(2,1)S(1)}, f16[2,128,256]{2,1,0:T(8,128)(2,1)S(1)}, u32[]{:S(2)}, u32[]{:S(2)}) collective-permute-start(f16[2,128,256]{2,1,0:T(8,128)(2,1)S(1)} %get-tuple-element.27), channel_id=1, source_target_pairs={{8,16},{16,8},{24,32},{32,24},{40,48},{48,40},{56,64},{64,56},{72,... | collective-permute-start | bytes 393224 | tf_op jit(solution)/shard_map/ppermute | solution.py:373
  89.2 0.1 collective-permute-start.11
  89.3 12.2 %collective-permute-done.10 = f16[2,128,256]{2,1,0:T(8,128)(2,1)S(1)} collective-permute-done((f16[2,128,256]{2,1,0:T(8,128)(2,1)S(1)}, f16[2,128,256]{2,1,0:T(8,128)(2,1)S(1)}, u32[]{:S(2)}, u32[]{:S(2)}) %collective-permute-start.10) | collective-permute-done | bytes 131104 | tf_op jit(solution)/shard_map/ppermute | solution.py:373
  101.5 1.8 %collective-permute-done.11 = f16[2,128,256]{2,1,0:T(8,128)(2,1)S(1)} collective-permute-done((f16[2,128,256]{2,1,0:T(8,128)(2,1)S(1)}, f16[2,128,256]{2,1,0:T(8,128)(2,1)S(1)}, u32[]{:S(2)}, u32[]{:S(2)}) %collective-permute-start.11) | collective-permute-done | bytes 131104 | tf_op jit(solution)/shard_map/ppermute | solution.py:372
  103.3 0.1 broadcast_select_fusion.8
  103.4 1.3 %collective-permute-start.12 = (f16[8,256,256]{2,1,0:T(8,128)(2,1)S(1)}, f16[8,256,256]{2,1,0:T(8,128)(2,1)S(1)}, u32[]{:S(2)}, u32[]{:S(2)}) collective-permute-start(f16[8,256,256]{2,1,0:T(8,128)(2,1)S(1)} %bitcast.14), channel_id=1, source_target_pairs={{0,1},{1,0},{2,3},{3,2},{4,5},{5,4},{6,7},{7,6},{8,9},{9,8},{10,11... | collective-permute-start | bytes 3145736 | tf_op jit(solution)/shard_map/ppermute | solution.py:332
  105.4 0.9 multiply_subtract_fusion
  106.3 0.7 collective-permute-done.12
  107.0 2.6 %convert_multiply_fusion = f32[2,8,256,256]{3,2,1,0:T(8,128)} fusion(pred[2]{0:T(512)(128)(4,1)S(1)} %iota_compare_fusion, f16[8,256,256]{2,1,0:T(8,128)(2,1)S(1)} %collective-permute-done.12, f16[8,256,256]{2,1,0:T(8,128)(2,1)S(1)} %bitcast.15), kind=kLoop, calls=%fused_computation | loop fusion | flops 3145728 | bytes 6291458 | tf_op jit(solution)/shard_map/mul | solution.py:323
  (22 shorter events, 0.3 us)
Async XLA Ops:
  0.6 7.9 %copy-start.3 = (s32[1,1,2]{2,1,0:T(1,128)S(1)}, s32[1,1,2]{2,1,0:T(1,128)}, u32[]{:S(2)}) copy-start(s32[1,1,2]{2,1,0:T(1,128)} %param.11) | copy-start | bytes 28
  0.6 7.9 %copy-start.2 = (s32[1,1,2]{2,1,0:T(1,128)S(1)}, s32[1,1,2]{2,1,0:T(1,128)}, u32[]{:S(2)}) copy-start(s32[1,1,2]{2,1,0:T(1,128)} %param.12) | copy-start | bytes 28
  1.8 8.4 %collective-permute-start = (bf16[2,128,256]{2,1,0:T(8,128)(2,1)S(1)}, bf16[2,128,256]{2,1,0:T(8,128)(2,1)S(1)}, u32[]{:S(2)}, u32[]{:S(2)}) collective-permute-start(bf16[2,128,256]{2,1,0:T(8,128)(2,1)S(1)} %get-tuple-element.41), channel_id=1, source_target_pairs={{8,16},{16,8},{24,32},{32,24},{40,48},{48,40},{56,64},{64,56},{72,... | collective-permute-start | bytes 393224 | tf_op jit(solution)/shard_map/ppermute | solution.py:373
  6.0 4.2 %collective-permute-start.1 = (bf16[2,128,256]{2,1,0:T(8,128)(2,1)S(1)}, bf16[2,128,256]{2,1,0:T(8,128)(2,1)S(1)}, u32[]{:S(2)}, u32[]{:S(2)}) collective-permute-start(bf16[2,128,256]{2,1,0:T(8,128)(2,1)S(1)} %get-tuple-element.40), channel_id=1, source_target_pairs={{0,8},{8,0},{16,24},{24,16},{32,40},{40,32},{48,56},{56,48},{64,72... | collective-permute-start | bytes 393224 | tf_op jit(solution)/shard_map/ppermute | solution.py:372
  10.2 9.2 %copy-start = (f32[2,256,256]{2,1,0:T(8,128)S(1)}, f32[2,256,256]{2,1,0:T(8,128)}, u32[]{:S(2)}) copy-start(f32[2,256,256]{2,1,0:T(8,128)} %block_hbm.1) | copy-start | bytes 1572868
  10.2 9.2 %copy-start.1 = (bf16[6,256,256]{2,1,0:T(8,128)(2,1)S(1)}, bf16[6,256,256]{2,1,0:T(8,128)(2,1)}, u32[]{:S(2)}) copy-start(bf16[6,256,256]{2,1,0:T(8,128)(2,1)} %constant.106.clone.tables_hbm) | copy-start | bytes 2359300
  10.3 9.0 %collective-permute-start.2 = (bf16[2,512,128]{2,1,0:T(8,128)(2,1)S(1)}, bf16[2,512,128]{2,1,0:T(8,128)(2,1)S(1)}, u32[]{:S(2)}, u32[]{:S(2)}) collective-permute-start(bf16[2,512,128]{2,1,0:T(8,128)(2,1)S(1)} %get-tuple-element.35), channel_id=1, source_target_pairs={{1,2},{2,1},{3,4},{4,3},{5,6},{6,5},{9,10},{10,9},{11,12},{12,11},... | collective-permute-start | bytes 786440 | tf_op jit(solution)/shard_map/ppermute | solution.py:373
  15.3 4.0 %collective-permute-start.3 = (bf16[2,512,128]{2,1,0:T(8,128)(2,1)S(1)}, bf16[2,512,128]{2,1,0:T(8,128)(2,1)S(1)}, u32[]{:S(2)}, u32[]{:S(2)}) collective-permute-start(bf16[2,512,128]{2,1,0:T(8,128)(2,1)S(1)} %get-tuple-element.34), channel_id=1, source_target_pairs={{0,1},{1,0},{2,3},{3,2},{4,5},{5,4},{6,7},{7,6},{8,9},{9,8},{10,11... | collective-permute-start | bytes 786440 | tf_op jit(solution)/shard_map/ppermute | solution.py:372
  35.1 2.7 %collective-permute-start.4 = (f16[8,256,256]{2,1,0:T(8,128)(2,1)S(1)}, f16[8,256,256]{2,1,0:T(8,128)(2,1)S(1)}, u32[]{:S(2)}, u32[]{:S(2)}) collective-permute-start(f16[8,256,256]{2,1,0:T(8,128)(2,1)S(1)} %multiply_convert_fusion.1), channel_id=1, source_target_pairs={{0,1},{1,0},{2,3},{3,2},{4,5},{5,4},{6,7},{7,6},{8,9},{9,8},{10,11... | collective-permute-start | bytes 3145736 | tf_op jit(solution)/shard_map/ppermute | solution.py:332
  39.2 24.6 %all-to-all-start = ((f16[32,64,256]{2,1,0:T(8,128)(2,1)}), f16[32,64,256]{2,1,0:T(8,128)(2,1)}, u32[]{:S(2)}, u32[]{:S(2)}) async-start(f16[32,64,256]{2,1,0:T(8,128)(2,1)} %bitcast.16), calls=%async_computation | async-start | bytes 2097152 | tf_op jit(solution)/shard_map/all_to_all | solution.py:327
  47.2 16.5 %collective-permute-start.8 = (f16[2,512,128]{2,1,0:T(8,128)(2,1)S(1)}, f16[2,512,128]{2,1,0:T(8,128)(2,1)S(1)}, u32[]{:S(2)}, u32[]{:S(2)}) collective-permute-start(f16[2,512,128]{2,1,0:T(8,128)(2,1)S(1)} %get-tuple-element.28), channel_id=1, source_target_pairs={{1,2},{2,1},{3,4},{4,3},{5,6},{6,5},{9,10},{10,9},{11,12},{12,11},... | collective-permute-start | bytes 786440 | tf_op jit(solution)/shard_map/ppermute | solution.py:373
  51.1 12.6 %collective-permute-start.9 = (f16[2,512,128]{2,1,0:T(8,128)(2,1)S(1)}, f16[2,512,128]{2,1,0:T(8,128)(2,1)S(1)}, u32[]{:S(2)}, u32[]{:S(2)}) collective-permute-start(f16[2,512,128]{2,1,0:T(8,128)(2,1)S(1)} %get-tuple-element.29), channel_id=1, source_target_pairs={{0,1},{1,0},{2,3},{3,2},{4,5},{5,4},{6,7},{7,6},{8,9},{9,8},{10,11... | collective-permute-start | bytes 786440 | tf_op jit(solution)/shard_map/ppermute | solution.py:372
  65.3 9.9 %collective-permute-start.5 = (f16[64,256]{1,0:T(8,128)(2,1)S(1)}, f16[64,256]{1,0:T(8,128)(2,1)S(1)}, u32[]{:S(2)}, u32[]{:S(2)}) collective-permute-start(f16[64,256]{1,0:T(8,128)(2,1)S(1)} %multiply_convert_fusion.7), channel_id=1, source_target_pairs={{0,128},{1,129},{2,130},{3,131},{4,132},{5,133},{6,134},{7,135},{8... | collective-permute-start | bytes 98312 | tf_op jit(solution)/shard_map/ppermute | solution.py:340
  71.4 5.2 %collective-permute-start.6 = (f16[64,256]{1,0:T(8,128)(2,1)S(1)}, f16[64,256]{1,0:T(8,128)(2,1)S(1)}, u32[]{:S(2)}, u32[]{:S(2)}) collective-permute-start(f16[64,256]{1,0:T(8,128)(2,1)S(1)} %multiply_convert_fusion.7), channel_id=1, source_target_pairs={{0,64},{1,65},{2,66},{3,67},{4,68},{5,69},{6,70},{7,71},{8,72},{9,... | collective-permute-start | bytes 98312 | tf_op jit(solution)/shard_map/ppermute | solution.py:340
  72.1 4.5 %collective-permute-start.7 = (f16[64,256]{1,0:T(8,128)(2,1)S(1)}, f16[64,256]{1,0:T(8,128)(2,1)S(1)}, u32[]{:S(2)}, u32[]{:S(2)}) collective-permute-start(f16[64,256]{1,0:T(8,128)(2,1)S(1)} %multiply_convert_fusion.7), channel_id=1, source_target_pairs={{0,192},{1,193},{2,194},{3,195},{4,196},{5,197},{6,198},{7,199},{8... | collective-permute-start | bytes 98312 | tf_op jit(solution)/shard_map/ppermute | solution.py:340
  77.8 25.6 %all-to-all-start.1 = ((f16[32,64,256]{2,1,0:T(8,128)(2,1)}), f16[32,64,256]{2,1,0:T(8,128)(2,1)S(1)}, u32[]{:S(2)}, u32[]{:S(2)}) async-start(f16[32,64,256]{2,1,0:T(8,128)(2,1)} %broadcast_in_dim.21), calls=%async_computation.1 | async-start | bytes 2097152 | tf_op jit(solution)/shard_map/all_to_all | solution.py:327
  84.9 16.6 %collective-permute-start.10 = (f16[2,128,256]{2,1,0:T(8,128)(2,1)S(1)}, f16[2,128,256]{2,1,0:T(8,128)(2,1)S(1)}, u32[]{:S(2)}, u32[]{:S(2)}) collective-permute-start(f16[2,128,256]{2,1,0:T(8,128)(2,1)S(1)} %get-tuple-element.27), channel_id=1, source_target_pairs={{8,16},{16,8},{24,32},{32,24},{40,48},{48,40},{56,64},{64,56},{72,... | collective-permute-start | bytes 393224 | tf_op jit(solution)/shard_map/ppermute | solution.py:373
  89.2 14.1 %collective-permute-start.11 = (f16[2,128,256]{2,1,0:T(8,128)(2,1)S(1)}, f16[2,128,256]{2,1,0:T(8,128)(2,1)S(1)}, u32[]{:S(2)}, u32[]{:S(2)}) collective-permute-start(f16[2,128,256]{2,1,0:T(8,128)(2,1)S(1)} %get-tuple-element.26), channel_id=1, source_target_pairs={{0,8},{8,0},{16,24},{24,16},{32,40},{40,32},{48,56},{56,48},{64,72... | collective-permute-start | bytes 393224 | tf_op jit(solution)/shard_map/ppermute | solution.py:372
  103.4 3.6 %collective-permute-start.12 = (f16[8,256,256]{2,1,0:T(8,128)(2,1)S(1)}, f16[8,256,256]{2,1,0:T(8,128)(2,1)S(1)}, u32[]{:S(2)}, u32[]{:S(2)}) collective-permute-start(f16[8,256,256]{2,1,0:T(8,128)(2,1)S(1)} %bitcast.14), channel_id=1, source_target_pairs={{0,1},{1,0},{2,3},{3,2},{4,5},{5,4},{6,7},{7,6},{8,9},{9,8},{10,11... | collective-permute-start | bytes 3145736 | tf_op jit(solution)/shard_map/ppermute | solution.py:332

commit v5 on v4

--- a/solution.py
+++ b/solution.py
@@ -221,7 +221,7 @@
     lax.fori_loop(0, modes, go_forward, 0, unroll=UNROLL)
     amplitude = jnp.maximum(jnp.sqrt(level_ref[...]), 1.0)
     targets = jnp.concatenate([pattern_ref[slot] for slot in range(slots)], axis=0)
-    level_ref[...] = 1.0 - jnp.sqrt(targets) / amplitude
+    level_ref[...] = 1.0 - targets / amplitude
 
     def go_back(mode, carry):
         corrected = []
@@ -362,26 +362,20 @@
     return exchange(pieces, ("pair", "y", "x")).reshape(modes, -1, cols)
 
 
-def neighbours(head, tail, axis):
+def neighbours(head, tail, axis, kind):
     count = lax.axis_size(axis)
     even = lax.axis_index(axis) % 2 == 0
     swaps = [
         [pair for i in range(start, count - 1, 2) for pair in ((i, i + 1), (i + 1, i))]
         for start in (0, 1)
     ]
-    inner = lax.ppermute(jnp.where(even, tail, head), axis, swaps[0])
-    outer = lax.ppermute(jnp.where(even, head, tail), axis, swaps[1])
+    outer = lax.ppermute(jnp.where(even, head, tail).astype(kind), axis, swaps[1])
+    inner = lax.ppermute(jnp.where(even, tail, head).astype(kind), axis, swaps[0])
     return (jnp.where(even, outer, inner), jnp.where(even, inner, outer))
 
 
-def edges(cells, axis, dim, width):
-    head = lax.slice_in_dim(cells, 0, width, axis=dim)
-    tail = lax.slice_in_dim(cells, cells.shape[dim] - width, cells.shape[dim], axis=dim)
-    return neighbours(head, tail, axis)
-
-
 def trade(head, tail, axis):
-    return neighbours(narrow(head, 64.0), narrow(tail, 64.0), axis)
+    return neighbours(narrow(head, 64.0), narrow(tail, 64.0), axis, jnp.float16)
 
 
 def on_device(object_field, probe_modes, pattern, rows_at, cols_at, object_step, probe_step):
@@ -396,15 +390,20 @@
             jnp.broadcast_to(core, rows_at.shape[2:]).astype(jnp.int32),
         ]
     )
-    targets = pattern[0, 0]
+    targets = jnp.sqrt(pattern[0, 0])
     for dim in (1, 2):
         nearer = lax.slice_in_dim(targets, 0, half_width + 1, axis=dim)
         farther = lax.slice_in_dim(targets, half_width + 1, 2 * half_width, axis=dim)
         targets = jnp.concatenate([nearer, lax.rev(farther, (dim,))], axis=dim)
-    cells = object_field.astype(jnp.bfloat16)
-    above, below = edges(cells, "region", 1, half_width)
-    tall = jnp.concatenate([above, cells, below], axis=1)
-    left, right = edges(tall, "scan", 2, half_width)
+    kind = jnp.bfloat16
+    above, below = neighbours(
+        object_field[:, :half_width], object_field[:, -half_width:], "region", kind
+    )
+    sides = [
+        jnp.concatenate([above[:, :, cut], object_field[:, :, cut].astype(kind), below[:, :, cut]], 1)
+        for cut in (slice(0, half_width), slice(block_cols - half_width, block_cols))
+    ]
+    left, right = neighbours(*sides, "scan", kind)
     rim_left, center, rim_right, mine, other = device_gradients(
         place, object_field, above, below, left, right, probe_modes, targets
     )

time: 110 us -> 110 us (level)
    sqrt x0 -> x1, local copies, waits for them, and re-layouts: none -> 1.17 us  [on_device(): targets = jnp.sqrt(pattern[0, 0])]
where the time goes in v5:
time: 110 us
  starting transfers between devices  44 us (40%)
  waiting for transfers between devices  34.1 us (31%)
  Pallas kernels  15.4 us (14%)
  other arithmetic  9.92 us (9%)
  local copies, waits for them, and re-layouts  3.91 us (4%)
  between operations  2.32 us (2%)
    ppermute x4, waiting for transfers between devices, neighbours(): lax.ppermute(jnp.where(even, head, tail).astype(kind), axis, swaps[1])  27.4 us
    ppermute x4, starting transfers between devices, neighbours(): lax.ppermute(jnp.where(even, head, tail).astype(kind), axis, swaps[1])  17.3 us
    pallas_call x1, Pallas kernels, device_gradients(): pl.pallas_call(gradients_kernel, out_shape=made, in_specs=[pl.BlockSpec(m...  15.4 us
    all_to_all x2, starting transfers between devices, exchange(): lax.all_to_all(parts, ('region', 'scan'), 0, 0, axis_index_groups=axis_gr...  14.9 us
    ppermute x3, starting transfers between devices, shift_far(): return lax.ppermute(values, ('region', 'scan'), pairs)  9.65 us
    ppermute x2, waiting for transfers between devices, swap_cores(): lax.ppermute(values, ('region', 'scan'), [(i, i ^ 1) for i in range(count)])  3.37 us
    mul x1, other arithmetic, widen(): return values.astype(jnp.float32) * scale  2.64 us
  transfers between devices with their start and end apart: 15, of which 8 were waited for; matrix products, arithmetic and copies ran while one was open for 5% of the time, Pallas kernels for 0%

profile of v5, /device:TPU:33, one launch (start us, length us, event | category | flops | bytes accessed | tf_op | source)
XLA Modules:
  0.0 109.6 jit_solution(11229007796516783275)
XLA Ops:
  0.6 1.1 select_convert_fusion
  1.7 4.2 %collective-permute-start = (bf16[2,128,256]{2,1,0:T(8,128)(2,1)S(1)}, bf16[2,128,256]{2,1,0:T(8,128)(2,1)S(1)}, u32[]{:S(2)}, u32[]{:S(2)}) collective-permute-start(bf16[2,128,256]{2,1,0:T(8,128)(2,1)S(1)} %get-tuple-element.37), channel_id=1, source_target_pairs={{8,16},{16,8},{24,32},{32,24},{40,48},{48,40},{56,64},{64,56},{72,... | collective-permute-start | bytes 393224 | tf_op jit(solution)/shard_map/ppermute | solution.py:372
  5.9 0.4 collective-permute-start.1
  6.3 1.1 convert.4
  7.4 1.2 %sqrt_bitcast_fusion = f32[2,256,256]{2,1,0:T(8,128)S(1)} fusion(f32[1,1,2,256,256]{4,3,2,1,0:T(8,128)} %param.10), kind=kLoop, calls=%fused_computation.10 | loop fusion | bytes 1048576 | tf_op jit(solution)/shard_map/sqrt | solution.py:393
  8.7 0.2 rev.6
  8.9 0.1 pad_maximum_fusion.1
  9.1 0.4 rev.7
  9.4 0.1 slice_maximum_fusion
  9.5 0.6 collective-permute-done
  10.1 0.0 collective-permute-done.1
  10.2 0.1 broadcast_select_fusion.6
  10.4 4.9 %collective-permute-start.2 = (bf16[2,512,128]{2,1,0:T(8,128)(2,1)S(1)}, bf16[2,512,128]{2,1,0:T(8,128)(2,1)S(1)}, u32[]{:S(2)}, u32[]{:S(2)}) collective-permute-start(bf16[2,512,128]{2,1,0:T(8,128)(2,1)S(1)} %get-tuple-element.35), channel_id=1, source_target_pairs={{1,2},{2,1},{3,4},{4,3},{5,6},{6,5},{9,10},{10,9},{11,12},{12,11},... | collective-permute-start | bytes 786440 | tf_op jit(solution)/shard_map/ppermute | solution.py:372
  15.3 0.1 collective-permute-start.3
  15.4 0.1 pad_maximum_fusion.pattern_hbm
  15.6 0.1 pad.16.clone
  15.6 0.1 add_add_fusion.place_ref
  15.7 3.6 %collective-permute-done.2 = bf16[2,512,128]{2,1,0:T(8,128)(2,1)S(1)} collective-permute-done((bf16[2,512,128]{2,1,0:T(8,128)(2,1)S(1)}, bf16[2,512,128]{2,1,0:T(8,128)(2,1)S(1)}, u32[]{:S(2)}, u32[]{:S(2)}) %collective-permute-start.2) | collective-permute-done | bytes 262176 | tf_op jit(solution)/shard_map/ppermute | solution.py:372
  19.4 15.4 %shard_map.95 = (f32[2,512,128]{2,1,0:T(8,128)S(1)}, f32[2,512,256]{2,1,0:T(8,128)S(1)}, f32[2,512,128]{2,1,0:T(8,128)S(1)}, f32[8,256,256]{2,1,0:T(8,128)S(1)}, f32[8,256,256]{2,1,0:T(8,128)S(1)}) custom-call(s32[3,2]{1,0:T(4,128)S(1)} %add_add_fusion.place_ref, f32[2,256,256]{2,1,0:T(8,128)S(1)} %copy-done, ...), custom_call_target="tpu_custom_call" | custom-call | flops 8589934592 | bytes 16777216 | tf_op jit(solution)/shard_map/pallas_call | solution.py:280
  34.9 0.2 multiply_convert_fusion.1
  35.1 0.1 collective-permute-start.4
  35.2 2.6 %collective-permute-done.4 = f16[8,256,256]{2,1,0:T(8,128)(2,1)S(1)} collective-permute-done((f16[8,256,256]{2,1,0:T(8,128)(2,1)S(1)}, f16[8,256,256]{2,1,0:T(8,128)(2,1)S(1)}, u32[]{:S(2)}, u32[]{:S(2)}) %collective-permute-start.4) | collective-permute-done | bytes 1048608 | tf_op jit(solution)/shard_map/ppermute | solution.py:332
  37.8 1.4 %multiply_convert_fusion = f16[8,256,256]{2,1,0:T(8,128)(2,1)} fusion(f32[8,256,256]{2,1,0:T(8,128)S(1)} %get-tuple-element.14, f16[8,256,256]{2,1,0:T(8,128)(2,1)S(1)} %collective-permute-done.4), kind=kLoop, calls=%fused_computation.2 | loop fusion | flops 2621440 | bytes 4194304 | tf_op jit(solution)/shard_map/convert_element_type | solution.py:319
  39.2 7.8 %all-to-all-start = ((f16[32,64,256]{2,1,0:T(8,128)(2,1)}), f16[32,64,256]{2,1,0:T(8,128)(2,1)}, u32[]{:S(2)}, u32[]{:S(2)}) async-start(f16[32,64,256]{2,1,0:T(8,128)(2,1)} %bitcast.17), calls=%async_computation | async-start | bytes 2097152 | tf_op jit(solution)/shard_map/all_to_all | solution.py:327
  47.1 0.1 broadcast_select_fusion.3
  47.2 3.9 %collective-permute-start.8 = (f16[2,512,128]{2,1,0:T(8,128)(2,1)S(1)}, f16[2,512,128]{2,1,0:T(8,128)(2,1)S(1)}, u32[]{:S(2)}, u32[]{:S(2)}) collective-permute-start(f16[2,512,128]{2,1,0:T(8,128)(2,1)S(1)} %get-tuple-element.28), channel_id=1, source_target_pairs={{1,2},{2,1},{3,4},{4,3},{5,6},{6,5},{9,10},{10,9},{11,12},{12,11},... | collective-permute-start | bytes 786440 | tf_op jit(solution)/shard_map/ppermute | solution.py:372
  51.1 0.1 collective-permute-start.9
  51.9 0.9 dynamic-slice_bitcast_fusion
  52.8 10.9 %collective-permute-done.8 = f16[2,512,128]{2,1,0:T(8,128)(2,1)S(1)} collective-permute-done((f16[2,512,128]{2,1,0:T(8,128)(2,1)S(1)}, f16[2,512,128]{2,1,0:T(8,128)(2,1)S(1)}, u32[]{:S(2)}, u32[]{:S(2)}) %collective-permute-start.8) | collective-permute-done | bytes 262176 | tf_op jit(solution)/shard_map/ppermute | solution.py:372
  63.7 0.1 broadcast_select_fusion.1
  63.9 1.4 %multiply_reduce_fusion = f32[64,256]{1,0:T(8,128)S(1)} fusion(f16[32,64,256]{2,1,0:T(8,128)(2,1)} %all-to-all-done), kind=kLoop, calls=%fused_computation.1 | loop fusion | flops 1556480 | bytes 1114112 | tf_op jit(solution)/shard_map/reduce_sum | solution.py:349
  65.3 6.1 %collective-permute-start.5 = (f16[64,256]{1,0:T(8,128)(2,1)S(1)}, f16[64,256]{1,0:T(8,128)(2,1)S(1)}, u32[]{:S(2)}, u32[]{:S(2)}) collective-permute-start(f16[64,256]{1,0:T(8,128)(2,1)S(1)} %multiply_convert_fusion.7), channel_id=1, source_target_pairs={{0,128},{1,129},{2,130},{3,131},{4,132},{5,133},{6,134},{7,135},{8... | collective-permute-start | bytes 98312 | tf_op jit(solution)/shard_map/ppermute | solution.py:340
  71.4 0.7 collective-permute-start.6
  72.1 2.9 %collective-permute-start.7 = (f16[64,256]{1,0:T(8,128)(2,1)S(1)}, f16[64,256]{1,0:T(8,128)(2,1)S(1)}, u32[]{:S(2)}, u32[]{:S(2)}) collective-permute-start(f16[64,256]{1,0:T(8,128)(2,1)S(1)} %multiply_convert_fusion.7), channel_id=1, source_target_pairs={{0,192},{1,193},{2,194},{3,195},{4,196},{5,197},{6,198},{7,199},{8... | collective-permute-start | bytes 98312 | tf_op jit(solution)/shard_map/ppermute | solution.py:340
  75.0 0.2 multiply_add_fusion
  75.1 1.5 %collective-permute-done.6 = f16[64,256]{1,0:T(8,128)(2,1)S(1)} collective-permute-done((f16[64,256]{1,0:T(8,128)(2,1)S(1)}, f16[64,256]{1,0:T(8,128)(2,1)S(1)}, u32[]{:S(2)}, u32[]{:S(2)}) %collective-permute-start.6) | collective-permute-done | bytes 32800 | tf_op jit(solution)/shard_map/ppermute | solution.py:340
  76.6 1.1 broadcast_in_dim.21
  77.7 7.0 %all-to-all-start.1 = ((f16[32,64,256]{2,1,0:T(8,128)(2,1)}), f16[32,64,256]{2,1,0:T(8,128)(2,1)S(1)}, u32[]{:S(2)}, u32[]{:S(2)}) async-start(f16[32,64,256]{2,1,0:T(8,128)(2,1)} %broadcast_in_dim.21), calls=%async_computation.1 | async-start | bytes 2097152 | tf_op jit(solution)/shard_map/all_to_all | solution.py:327
  84.8 0.1 broadcast_select_fusion.10
  84.8 4.3 %collective-permute-start.10 = (f16[2,128,256]{2,1,0:T(8,128)(2,1)S(1)}, f16[2,128,256]{2,1,0:T(8,128)(2,1)S(1)}, u32[]{:S(2)}, u32[]{:S(2)}) collective-permute-start(f16[2,128,256]{2,1,0:T(8,128)(2,1)S(1)} %get-tuple-element.27), channel_id=1, source_target_pairs={{8,16},{16,8},{24,32},{32,24},{40,48},{48,40},{56,64},{64,56},{72,... | collective-permute-start | bytes 393224 | tf_op jit(solution)/shard_map/ppermute | solution.py:372
  89.1 0.1 collective-permute-start.11
  89.2 12.2 %collective-permute-done.10 = f16[2,128,256]{2,1,0:T(8,128)(2,1)S(1)} collective-permute-done((f16[2,128,256]{2,1,0:T(8,128)(2,1)S(1)}, f16[2,128,256]{2,1,0:T(8,128)(2,1)S(1)}, u32[]{:S(2)}, u32[]{:S(2)}) %collective-permute-start.10) | collective-permute-done | bytes 131104 | tf_op jit(solution)/shard_map/ppermute | solution.py:372
  101.5 1.8 %collective-permute-done.11 = f16[2,128,256]{2,1,0:T(8,128)(2,1)S(1)} collective-permute-done((f16[2,128,256]{2,1,0:T(8,128)(2,1)S(1)}, f16[2,128,256]{2,1,0:T(8,128)(2,1)S(1)}, u32[]{:S(2)}, u32[]{:S(2)}) %collective-permute-start.11) | collective-permute-done | bytes 131104 | tf_op jit(solution)/shard_map/ppermute | solution.py:373
  103.3 0.1 broadcast_select_fusion.8
  103.4 1.3 %collective-permute-start.12 = (f16[8,256,256]{2,1,0:T(8,128)(2,1)S(1)}, f16[8,256,256]{2,1,0:T(8,128)(2,1)S(1)}, u32[]{:S(2)}, u32[]{:S(2)}) collective-permute-start(f16[8,256,256]{2,1,0:T(8,128)(2,1)S(1)} %bitcast.15), channel_id=1, source_target_pairs={{0,1},{1,0},{2,3},{3,2},{4,5},{5,4},{6,7},{7,6},{8,9},{9,8},{10,11... | collective-permute-start | bytes 3145736 | tf_op jit(solution)/shard_map/ppermute | solution.py:332
  105.4 0.9 multiply_subtract_fusion
  106.3 0.7 collective-permute-done.12
  107.0 2.6 %convert_multiply_fusion = f32[2,8,256,256]{3,2,1,0:T(8,128)} fusion(pred[2]{0:T(512)(128)(4,1)S(1)} %iota_compare_fusion, f16[8,256,256]{2,1,0:T(8,128)(2,1)S(1)} %collective-permute-done.12, f16[8,256,256]{2,1,0:T(8,128)(2,1)S(1)} %bitcast.16), kind=kLoop, calls=%fused_computation | loop fusion | flops 3145728 | bytes 6291458 | tf_op jit(solution)/shard_map/mul | solution.py:323
  (24 shorter events, 0.3 us)
Async XLA Ops:
  1.7 7.2 %copy-start.2 = (s32[1,1,2]{2,1,0:T(1,128)S(1)}, s32[1,1,2]{2,1,0:T(1,128)}, u32[]{:S(2)}) copy-start(s32[1,1,2]{2,1,0:T(1,128)} %param.12) | copy-start | bytes 28
  1.7 7.2 %copy-start.3 = (s32[1,1,2]{2,1,0:T(1,128)S(1)}, s32[1,1,2]{2,1,0:T(1,128)}, u32[]{:S(2)}) copy-start(s32[1,1,2]{2,1,0:T(1,128)} %param.11) | copy-start | bytes 28
  1.7 8.4 %collective-permute-start = (bf16[2,128,256]{2,1,0:T(8,128)(2,1)S(1)}, bf16[2,128,256]{2,1,0:T(8,128)(2,1)S(1)}, u32[]{:S(2)}, u32[]{:S(2)}) collective-permute-start(bf16[2,128,256]{2,1,0:T(8,128)(2,1)S(1)} %get-tuple-element.37), channel_id=1, source_target_pairs={{8,16},{16,8},{24,32},{32,24},{40,48},{48,40},{56,64},{64,56},{72,... | collective-permute-start | bytes 393224 | tf_op jit(solution)/shard_map/ppermute | solution.py:372
  5.9 4.2 %collective-permute-start.1 = (bf16[2,128,256]{2,1,0:T(8,128)(2,1)S(1)}, bf16[2,128,256]{2,1,0:T(8,128)(2,1)S(1)}, u32[]{:S(2)}, u32[]{:S(2)}) collective-permute-start(bf16[2,128,256]{2,1,0:T(8,128)(2,1)S(1)} %get-tuple-element.36), channel_id=1, source_target_pairs={{0,8},{8,0},{16,24},{24,16},{32,40},{40,32},{48,56},{56,48},{64,72... | collective-permute-start | bytes 393224 | tf_op jit(solution)/shard_map/ppermute | solution.py:373
  10.2 9.2 %copy-start = (f32[2,256,256]{2,1,0:T(8,128)S(1)}, f32[2,256,256]{2,1,0:T(8,128)}, u32[]{:S(2)}) copy-start(f32[2,256,256]{2,1,0:T(8,128)} %block_hbm.1) | copy-start | bytes 1572868
  10.2 9.2 %copy-start.1 = (bf16[6,256,256]{2,1,0:T(8,128)(2,1)S(1)}, bf16[6,256,256]{2,1,0:T(8,128)(2,1)}, u32[]{:S(2)}) copy-start(bf16[6,256,256]{2,1,0:T(8,128)(2,1)} %constant.106.clone.tables_hbm) | copy-start | bytes 2359300
  10.4 9.0 %collective-permute-start.2 = (bf16[2,512,128]{2,1,0:T(8,128)(2,1)S(1)}, bf16[2,512,128]{2,1,0:T(8,128)(2,1)S(1)}, u32[]{:S(2)}, u32[]{:S(2)}) collective-permute-start(bf16[2,512,128]{2,1,0:T(8,128)(2,1)S(1)} %get-tuple-element.35), channel_id=1, source_target_pairs={{1,2},{2,1},{3,4},{4,3},{5,6},{6,5},{9,10},{10,9},{11,12},{12,11},... | collective-permute-start | bytes 786440 | tf_op jit(solution)/shard_map/ppermute | solution.py:372
  15.3 4.0 %collective-permute-start.3 = (bf16[2,512,128]{2,1,0:T(8,128)(2,1)S(1)}, bf16[2,512,128]{2,1,0:T(8,128)(2,1)S(1)}, u32[]{:S(2)}, u32[]{:S(2)}) collective-permute-start(bf16[2,512,128]{2,1,0:T(8,128)(2,1)S(1)} %get-tuple-element.34), channel_id=1, source_target_pairs={{0,1},{1,0},{2,3},{3,2},{4,5},{5,4},{6,7},{7,6},{8,9},{9,8},{10,11... | collective-permute-start | bytes 786440 | tf_op jit(solution)/shard_map/ppermute | solution.py:373
  35.1 2.7 %collective-permute-start.4 = (f16[8,256,256]{2,1,0:T(8,128)(2,1)S(1)}, f16[8,256,256]{2,1,0:T(8,128)(2,1)S(1)}, u32[]{:S(2)}, u32[]{:S(2)}) collective-permute-start(f16[8,256,256]{2,1,0:T(8,128)(2,1)S(1)} %multiply_convert_fusion.1), channel_id=1, source_target_pairs={{0,1},{1,0},{2,3},{3,2},{4,5},{5,4},{6,7},{7,6},{8,9},{9,8},{10,11... | collective-permute-start | bytes 3145736 | tf_op jit(solution)/shard_map/ppermute | solution.py:332
  39.2 24.6 %all-to-all-start = ((f16[32,64,256]{2,1,0:T(8,128)(2,1)}), f16[32,64,256]{2,1,0:T(8,128)(2,1)}, u32[]{:S(2)}, u32[]{:S(2)}) async-start(f16[32,64,256]{2,1,0:T(8,128)(2,1)} %bitcast.17), calls=%async_computation | async-start | bytes 2097152 | tf_op jit(solution)/shard_map/all_to_all | solution.py:327
  47.2 16.5 %collective-permute-start.8 = (f16[2,512,128]{2,1,0:T(8,128)(2,1)S(1)}, f16[2,512,128]{2,1,0:T(8,128)(2,1)S(1)}, u32[]{:S(2)}, u32[]{:S(2)}) collective-permute-start(f16[2,512,128]{2,1,0:T(8,128)(2,1)S(1)} %get-tuple-element.28), channel_id=1, source_target_pairs={{1,2},{2,1},{3,4},{4,3},{5,6},{6,5},{9,10},{10,9},{11,12},{12,11},... | collective-permute-start | bytes 786440 | tf_op jit(solution)/shard_map/ppermute | solution.py:372
  51.1 12.6 %collective-permute-start.9 = (f16[2,512,128]{2,1,0:T(8,128)(2,1)S(1)}, f16[2,512,128]{2,1,0:T(8,128)(2,1)S(1)}, u32[]{:S(2)}, u32[]{:S(2)}) collective-permute-start(f16[2,512,128]{2,1,0:T(8,128)(2,1)S(1)} %get-tuple-element.29), channel_id=1, source_target_pairs={{0,1},{1,0},{2,3},{3,2},{4,5},{5,4},{6,7},{7,6},{8,9},{9,8},{10,11... | collective-permute-start | bytes 786440 | tf_op jit(solution)/shard_map/ppermute | solution.py:373
  65.3 9.8 %collective-permute-start.5 = (f16[64,256]{1,0:T(8,128)(2,1)S(1)}, f16[64,256]{1,0:T(8,128)(2,1)S(1)}, u32[]{:S(2)}, u32[]{:S(2)}) collective-permute-start(f16[64,256]{1,0:T(8,128)(2,1)S(1)} %multiply_convert_fusion.7), channel_id=1, source_target_pairs={{0,128},{1,129},{2,130},{3,131},{4,132},{5,133},{6,134},{7,135},{8... | collective-permute-start | bytes 98312 | tf_op jit(solution)/shard_map/ppermute | solution.py:340
  71.4 5.2 %collective-permute-start.6 = (f16[64,256]{1,0:T(8,128)(2,1)S(1)}, f16[64,256]{1,0:T(8,128)(2,1)S(1)}, u32[]{:S(2)}, u32[]{:S(2)}) collective-permute-start(f16[64,256]{1,0:T(8,128)(2,1)S(1)} %multiply_convert_fusion.7), channel_id=1, source_target_pairs={{0,64},{1,65},{2,66},{3,67},{4,68},{5,69},{6,70},{7,71},{8,72},{9,... | collective-permute-start | bytes 98312 | tf_op jit(solution)/shard_map/ppermute | solution.py:340
  72.1 4.5 %collective-permute-start.7 = (f16[64,256]{1,0:T(8,128)(2,1)S(1)}, f16[64,256]{1,0:T(8,128)(2,1)S(1)}, u32[]{:S(2)}, u32[]{:S(2)}) collective-permute-start(f16[64,256]{1,0:T(8,128)(2,1)S(1)} %multiply_convert_fusion.7), channel_id=1, source_target_pairs={{0,192},{1,193},{2,194},{3,195},{4,196},{5,197},{6,198},{7,199},{8... | collective-permute-start | bytes 98312 | tf_op jit(solution)/shard_map/ppermute | solution.py:340
  77.7 25.6 %all-to-all-start.1 = ((f16[32,64,256]{2,1,0:T(8,128)(2,1)}), f16[32,64,256]{2,1,0:T(8,128)(2,1)S(1)}, u32[]{:S(2)}, u32[]{:S(2)}) async-start(f16[32,64,256]{2,1,0:T(8,128)(2,1)} %broadcast_in_dim.21), calls=%async_computation.1 | async-start | bytes 2097152 | tf_op jit(solution)/shard_map/all_to_all | solution.py:327
  84.8 16.6 %collective-permute-start.10 = (f16[2,128,256]{2,1,0:T(8,128)(2,1)S(1)}, f16[2,128,256]{2,1,0:T(8,128)(2,1)S(1)}, u32[]{:S(2)}, u32[]{:S(2)}) collective-permute-start(f16[2,128,256]{2,1,0:T(8,128)(2,1)S(1)} %get-tuple-element.27), channel_id=1, source_target_pairs={{8,16},{16,8},{24,32},{32,24},{40,48},{48,40},{56,64},{64,56},{72,... | collective-permute-start | bytes 393224 | tf_op jit(solution)/shard_map/ppermute | solution.py:372
  89.1 14.1 %collective-permute-start.11 = (f16[2,128,256]{2,1,0:T(8,128)(2,1)S(1)}, f16[2,128,256]{2,1,0:T(8,128)(2,1)S(1)}, u32[]{:S(2)}, u32[]{:S(2)}) collective-permute-start(f16[2,128,256]{2,1,0:T(8,128)(2,1)S(1)} %get-tuple-element.26), channel_id=1, source_target_pairs={{0,8},{8,0},{16,24},{24,16},{32,40},{40,32},{48,56},{56,48},{64,72... | collective-permute-start | bytes 393224 | tf_op jit(solution)/shard_map/ppermute | solution.py:373
  103.4 3.6 %collective-permute-start.12 = (f16[8,256,256]{2,1,0:T(8,128)(2,1)S(1)}, f16[8,256,256]{2,1,0:T(8,128)(2,1)S(1)}, u32[]{:S(2)}, u32[]{:S(2)}) collective-permute-start(f16[8,256,256]{2,1,0:T(8,128)(2,1)S(1)} %bitcast.15), channel_id=1, source_target_pairs={{0,1},{1,0},{2,3},{3,2},{4,5},{5,4},{6,7},{7,6},{8,9},{9,8},{10,11... | collective-permute-start | bytes 3145736 | tf_op jit(solution)/shard_map/ppermute | solution.py:332

commit v6 on v5

--- a/solution.py
+++ b/solution.py
@@ -163,12 +163,31 @@
             )
         )
     ]
-    for fetch in fetches[5:6] + fetches[:5] + fetches[6:]:
+    for fetch in fetches:
         fetch.start()
     for mode in range(modes):
         fetch_probe(mode).start()
     for part_ref in (rim_left_ref, center_ref, rim_right_ref, level_ref, object_ref):
         part_ref[...] = jnp.zeros_like(part_ref)
+    for fetch in fetches[:5]:
+        fetch.wait()
+    padded_ref[:, :, :half] = left_ref[...].astype(jnp.float32)
+    padded_ref[:, :, half + cols :] = right_ref[...].astype(jnp.float32)
+    padded_ref[:, :half, half : half + cols] = above_ref[...].astype(jnp.float32)
+    padded_ref[:, half + rows :, half : half + cols] = below_ref[...].astype(jnp.float32)
+    padded_ref[:, half : half + rows, half : half + cols] = (
+        block_ref[...].astype(jnp.bfloat16).astype(jnp.float32)
+    )
+    first = place_ref[2, 0] == 0
+    places = []
+    for slot in range(slots):
+        row, col = place_ref[0, slot], place_ref[1, slot]
+        shift = row % 8
+        span = pl.ds(pl.multiple_of(row - shift, 8), length + 8)
+        places.append((span, shift, col))
+        for part in range(2):
+            strip = pltpu.roll(padded_ref[part, span, :], wide - col, 1)[:, :length]
+            window_ref[slot, part] = pltpu.roll(strip, length + 8 - shift, 0)[:length]
     fetches[5].wait()
     low, high = slice(0, length), slice(length, 2 * length)
     for table_ref, cosine, sine in (
@@ -179,25 +198,6 @@
         table_ref[high, high] = cosine
         table_ref[low, high] = sine
         table_ref[high, low] = -sine
-    for fetch in fetches[:5]:
-        fetch.wait()
-    padded_ref[:, :, :half] = left_ref[...].astype(jnp.float32)
-    padded_ref[:, :, half + cols :] = right_ref[...].astype(jnp.float32)
-    padded_ref[:, :half, half : half + cols] = above_ref[...].astype(jnp.float32)
-    padded_ref[:, half + rows :, half : half + cols] = below_ref[...].astype(jnp.float32)
-    padded_ref[:, half : half + rows, half : half + cols] = (
-        block_ref[...].astype(jnp.bfloat16).astype(jnp.float32)
-    )
-    first = place_ref[2, 0] == 0
-    places = []
-    for slot in range(slots):
-        row, col = place_ref[0, slot], place_ref[1, slot]
-        shift = row % 8
-        span = pl.ds(pl.multiple_of(row - shift, 8), length + 8)
-        places.append((span, shift, col))
-        for part in range(2):
-            strip = pltpu.roll(padded_ref[part, span, :], wide - col, 1)[:, :length]
-            window_ref[slot, part] = pltpu.roll(strip, length + 8 - shift, 0)[:length]
     fetches[6].wait()
 
     def go_forward(mode, carry):

time: 110 us -> 110 us (level)
  no operation moved by 1% of the time
where the time goes in v6:
time: 110 us
  starting transfers between devices  43.9 us (40%)
  waiting for transfers between devices  34.1 us (31%)
  Pallas kernels  15.4 us (14%)
  other arithmetic  9.92 us (9%)
  local copies, waits for them, and re-layouts  3.91 us (4%)
  between operations  2.32 us (2%)
    ppermute x4, waiting for transfers between devices, neighbours(): lax.ppermute(jnp.where(even, head, tail).astype(kind), axis, swaps[1])  27.4 us
    ppermute x4, starting transfers between devices, neighbours(): lax.ppermute(jnp.where(even, head, tail).astype(kind), axis, swaps[1])  17.3 us
    pallas_call x1, Pallas kernels, device_gradients(): pl.pallas_call(gradients_kernel, out_shape=made, in_specs=[pl.BlockSpec(m...  15.4 us
    all_to_all x2, starting transfers between devices, exchange(): lax.all_to_all(parts, ('region', 'scan'), 0, 0, axis_index_groups=axis_gr...  14.9 us
    ppermute x3, starting transfers between devices, shift_far(): return lax.ppermute(values, ('region', 'scan'), pairs)  9.61 us
    ppermute x2, waiting for transfers between devices, swap_cores(): lax.ppermute(values, ('region', 'scan'), [(i, i ^ 1) for i in range(count)])  3.37 us
    mul x1, other arithmetic, widen(): return values.astype(jnp.float32) * scale  2.64 us
  transfers between devices with their start and end apart: 15, of which 8 were waited for; matrix products, arithmetic and copies ran while one was open for 5% of the time, Pallas kernels for 0%

profile of v6, /device:TPU:33, one launch (start us, length us, event | category | flops | bytes accessed | tf_op | source)
XLA Modules:
  0.0 109.6 jit_solution(3706922023097961803)
XLA Ops:
  0.6 1.1 select_convert_fusion
  1.7 4.2 %collective-permute-start = (bf16[2,128,256]{2,1,0:T(8,128)(2,1)S(1)}, bf16[2,128,256]{2,1,0:T(8,128)(2,1)S(1)}, u32[]{:S(2)}, u32[]{:S(2)}) collective-permute-start(bf16[2,128,256]{2,1,0:T(8,128)(2,1)S(1)} %get-tuple-element.37), channel_id=1, source_target_pairs={{8,16},{16,8},{24,32},{32,24},{40,48},{48,40},{56,64},{64,56},{72,... | collective-permute-start | bytes 393224 | tf_op jit(solution)/shard_map/ppermute | solution.py:372
  5.9 0.4 collective-permute-start.1
  6.3 1.1 convert.4
  7.4 1.2 %sqrt_bitcast_fusion = f32[2,256,256]{2,1,0:T(8,128)S(1)} fusion(f32[1,1,2,256,256]{4,3,2,1,0:T(8,128)} %param.10), kind=kLoop, calls=%fused_computation.10 | loop fusion | bytes 1048576 | tf_op jit(solution)/shard_map/sqrt | solution.py:393
  8.7 0.2 rev.6
  8.9 0.1 pad_maximum_fusion.1
  9.1 0.4 rev.7
  9.4 0.1 slice_maximum_fusion
  9.5 0.6 collective-permute-done
  10.1 0.0 collective-permute-done.1
  10.2 0.1 broadcast_select_fusion.6
  10.4 4.9 %collective-permute-start.2 = (bf16[2,512,128]{2,1,0:T(8,128)(2,1)S(1)}, bf16[2,512,128]{2,1,0:T(8,128)(2,1)S(1)}, u32[]{:S(2)}, u32[]{:S(2)}) collective-permute-start(bf16[2,512,128]{2,1,0:T(8,128)(2,1)S(1)} %get-tuple-element.35), channel_id=1, source_target_pairs={{1,2},{2,1},{3,4},{4,3},{5,6},{6,5},{9,10},{10,9},{11,12},{12,11},... | collective-permute-start | bytes 786440 | tf_op jit(solution)/shard_map/ppermute | solution.py:372
  15.3 0.1 collective-permute-start.3
  15.4 0.1 pad_maximum_fusion.pattern_hbm
  15.6 0.1 pad.16.clone
  15.6 0.1 add_add_fusion.place_ref
  15.7 3.6 %collective-permute-done.2 = bf16[2,512,128]{2,1,0:T(8,128)(2,1)S(1)} collective-permute-done((bf16[2,512,128]{2,1,0:T(8,128)(2,1)S(1)}, bf16[2,512,128]{2,1,0:T(8,128)(2,1)S(1)}, u32[]{:S(2)}, u32[]{:S(2)}) %collective-permute-start.2) | collective-permute-done | bytes 262176 | tf_op jit(solution)/shard_map/ppermute | solution.py:372
  19.4 15.4 %shard_map.95 = (f32[2,512,128]{2,1,0:T(8,128)S(1)}, f32[2,512,256]{2,1,0:T(8,128)S(1)}, f32[2,512,128]{2,1,0:T(8,128)S(1)}, f32[8,256,256]{2,1,0:T(8,128)S(1)}, f32[8,256,256]{2,1,0:T(8,128)S(1)}) custom-call(s32[3,2]{1,0:T(4,128)S(1)} %add_add_fusion.place_ref, f32[2,256,256]{2,1,0:T(8,128)S(1)} %copy-done, ...), custom_call_target="tpu_custom_call" | custom-call | flops 8589934592 | bytes 16777216 | tf_op jit(solution)/shard_map/pallas_call | solution.py:280
  34.9 0.2 multiply_convert_fusion.1
  35.1 0.1 collective-permute-start.4
  35.2 2.6 %collective-permute-done.4 = f16[8,256,256]{2,1,0:T(8,128)(2,1)S(1)} collective-permute-done((f16[8,256,256]{2,1,0:T(8,128)(2,1)S(1)}, f16[8,256,256]{2,1,0:T(8,128)(2,1)S(1)}, u32[]{:S(2)}, u32[]{:S(2)}) %collective-permute-start.4) | collective-permute-done | bytes 1048608 | tf_op jit(solution)/shard_map/ppermute | solution.py:332
  37.8 1.4 %multiply_convert_fusion = f16[8,256,256]{2,1,0:T(8,128)(2,1)} fusion(f32[8,256,256]{2,1,0:T(8,128)S(1)} %get-tuple-element.14, f16[8,256,256]{2,1,0:T(8,128)(2,1)S(1)} %collective-permute-done.4), kind=kLoop, calls=%fused_computation.2 | loop fusion | flops 2621440 | bytes 4194304 | tf_op jit(solution)/shard_map/convert_element_type | solution.py:319
  39.2 7.9 %all-to-all-start = ((f16[32,64,256]{2,1,0:T(8,128)(2,1)}), f16[32,64,256]{2,1,0:T(8,128)(2,1)}, u32[]{:S(2)}, u32[]{:S(2)}) async-start(f16[32,64,256]{2,1,0:T(8,128)(2,1)} %bitcast.17), calls=%async_computation | async-start | bytes 2097152 | tf_op jit(solution)/shard_map/all_to_all | solution.py:327
  47.1 0.1 broadcast_select_fusion.3
  47.2 3.9 %collective-permute-start.8 = (f16[2,512,128]{2,1,0:T(8,128)(2,1)S(1)}, f16[2,512,128]{2,1,0:T(8,128)(2,1)S(1)}, u32[]{:S(2)}, u32[]{:S(2)}) collective-permute-start(f16[2,512,128]{2,1,0:T(8,128)(2,1)S(1)} %get-tuple-element.28), channel_id=1, source_target_pairs={{1,2},{2,1},{3,4},{4,3},{5,6},{6,5},{9,10},{10,9},{11,12},{12,11},... | collective-permute-start | bytes 786440 | tf_op jit(solution)/shard_map/ppermute | solution.py:372
  51.1 0.1 collective-permute-start.9
  51.9 0.9 dynamic-slice_bitcast_fusion
  52.8 10.9 %collective-permute-done.8 = f16[2,512,128]{2,1,0:T(8,128)(2,1)S(1)} collective-permute-done((f16[2,512,128]{2,1,0:T(8,128)(2,1)S(1)}, f16[2,512,128]{2,1,0:T(8,128)(2,1)S(1)}, u32[]{:S(2)}, u32[]{:S(2)}) %collective-permute-start.8) | collective-permute-done | bytes 262176 | tf_op jit(solution)/shard_map/ppermute | solution.py:372
  63.7 0.1 broadcast_select_fusion.1
  63.8 1.4 %multiply_reduce_fusion = f32[64,256]{1,0:T(8,128)S(1)} fusion(f16[32,64,256]{2,1,0:T(8,128)(2,1)} %all-to-all-done), kind=kLoop, calls=%fused_computation.1 | loop fusion | flops 1556480 | bytes 1114112 | tf_op jit(solution)/shard_map/reduce_sum | solution.py:349
  65.3 6.0 %collective-permute-start.5 = (f16[64,256]{1,0:T(8,128)(2,1)S(1)}, f16[64,256]{1,0:T(8,128)(2,1)S(1)}, u32[]{:S(2)}, u32[]{:S(2)}) collective-permute-start(f16[64,256]{1,0:T(8,128)(2,1)S(1)} %multiply_convert_fusion.7), channel_id=1, source_target_pairs={{0,128},{1,129},{2,130},{3,131},{4,132},{5,133},{6,134},{7,135},{8... | collective-permute-start | bytes 98312 | tf_op jit(solution)/shard_map/ppermute | solution.py:340
  71.3 0.7 collective-permute-start.6
  72.1 2.8 %collective-permute-start.7 = (f16[64,256]{1,0:T(8,128)(2,1)S(1)}, f16[64,256]{1,0:T(8,128)(2,1)S(1)}, u32[]{:S(2)}, u32[]{:S(2)}) collective-permute-start(f16[64,256]{1,0:T(8,128)(2,1)S(1)} %multiply_convert_fusion.7), channel_id=1, source_target_pairs={{0,192},{1,193},{2,194},{3,195},{4,196},{5,197},{6,198},{7,199},{8... | collective-permute-start | bytes 98312 | tf_op jit(solution)/shard_map/ppermute | solution.py:340
  74.9 0.2 multiply_add_fusion
  75.1 1.5 %collective-permute-done.6 = f16[64,256]{1,0:T(8,128)(2,1)S(1)} collective-permute-done((f16[64,256]{1,0:T(8,128)(2,1)S(1)}, f16[64,256]{1,0:T(8,128)(2,1)S(1)}, u32[]{:S(2)}, u32[]{:S(2)}) %collective-permute-start.6) | collective-permute-done | bytes 32800 | tf_op jit(solution)/shard_map/ppermute | solution.py:340
  76.6 1.1 broadcast_in_dim.21
  77.7 7.0 %all-to-all-start.1 = ((f16[32,64,256]{2,1,0:T(8,128)(2,1)}), f16[32,64,256]{2,1,0:T(8,128)(2,1)S(1)}, u32[]{:S(2)}, u32[]{:S(2)}) async-start(f16[32,64,256]{2,1,0:T(8,128)(2,1)} %broadcast_in_dim.21), calls=%async_computation.1 | async-start | bytes 2097152 | tf_op jit(solution)/shard_map/all_to_all | solution.py:327
  84.7 0.1 broadcast_select_fusion.10
  84.8 4.3 %collective-permute-start.10 = (f16[2,128,256]{2,1,0:T(8,128)(2,1)S(1)}, f16[2,128,256]{2,1,0:T(8,128)(2,1)S(1)}, u32[]{:S(2)}, u32[]{:S(2)}) collective-permute-start(f16[2,128,256]{2,1,0:T(8,128)(2,1)S(1)} %get-tuple-element.27), channel_id=1, source_target_pairs={{8,16},{16,8},{24,32},{32,24},{40,48},{48,40},{56,64},{64,56},{72,... | collective-permute-start | bytes 393224 | tf_op jit(solution)/shard_map/ppermute | solution.py:372
  89.1 0.1 collective-permute-start.11
  89.2 12.2 %collective-permute-done.10 = f16[2,128,256]{2,1,0:T(8,128)(2,1)S(1)} collective-permute-done((f16[2,128,256]{2,1,0:T(8,128)(2,1)S(1)}, f16[2,128,256]{2,1,0:T(8,128)(2,1)S(1)}, u32[]{:S(2)}, u32[]{:S(2)}) %collective-permute-start.10) | collective-permute-done | bytes 131104 | tf_op jit(solution)/shard_map/ppermute | solution.py:372
  101.4 1.8 %collective-permute-done.11 = f16[2,128,256]{2,1,0:T(8,128)(2,1)S(1)} collective-permute-done((f16[2,128,256]{2,1,0:T(8,128)(2,1)S(1)}, f16[2,128,256]{2,1,0:T(8,128)(2,1)S(1)}, u32[]{:S(2)}, u32[]{:S(2)}) %collective-permute-start.11) | collective-permute-done | bytes 131104 | tf_op jit(solution)/shard_map/ppermute | solution.py:373
  103.2 0.1 broadcast_select_fusion.8
  103.3 1.3 %collective-permute-start.12 = (f16[8,256,256]{2,1,0:T(8,128)(2,1)S(1)}, f16[8,256,256]{2,1,0:T(8,128)(2,1)S(1)}, u32[]{:S(2)}, u32[]{:S(2)}) collective-permute-start(f16[8,256,256]{2,1,0:T(8,128)(2,1)S(1)} %bitcast.15), channel_id=1, source_target_pairs={{0,1},{1,0},{2,3},{3,2},{4,5},{5,4},{6,7},{7,6},{8,9},{9,8},{10,11... | collective-permute-start | bytes 3145736 | tf_op jit(solution)/shard_map/ppermute | solution.py:332
  105.3 0.9 multiply_subtract_fusion
  106.2 0.7 collective-permute-done.12
  106.9 2.6 %convert_multiply_fusion = f32[2,8,256,256]{3,2,1,0:T(8,128)} fusion(pred[2]{0:T(512)(128)(4,1)S(1)} %iota_compare_fusion, f16[8,256,256]{2,1,0:T(8,128)(2,1)S(1)} %collective-permute-done.12, f16[8,256,256]{2,1,0:T(8,128)(2,1)S(1)} %bitcast.16), kind=kLoop, calls=%fused_computation | loop fusion | flops 3145728 | bytes 6291458 | tf_op jit(solution)/shard_map/mul | solution.py:323
  (24 shorter events, 0.3 us)
Async XLA Ops:
  1.7 7.2 %copy-start.2 = (s32[1,1,2]{2,1,0:T(1,128)S(1)}, s32[1,1,2]{2,1,0:T(1,128)}, u32[]{:S(2)}) copy-start(s32[1,1,2]{2,1,0:T(1,128)} %param.12) | copy-start | bytes 28
  1.7 7.2 %copy-start.3 = (s32[1,1,2]{2,1,0:T(1,128)S(1)}, s32[1,1,2]{2,1,0:T(1,128)}, u32[]{:S(2)}) copy-start(s32[1,1,2]{2,1,0:T(1,128)} %param.11) | copy-start | bytes 28
  1.7 8.4 %collective-permute-start = (bf16[2,128,256]{2,1,0:T(8,128)(2,1)S(1)}, bf16[2,128,256]{2,1,0:T(8,128)(2,1)S(1)}, u32[]{:S(2)}, u32[]{:S(2)}) collective-permute-start(bf16[2,128,256]{2,1,0:T(8,128)(2,1)S(1)} %get-tuple-element.37), channel_id=1, source_target_pairs={{8,16},{16,8},{24,32},{32,24},{40,48},{48,40},{56,64},{64,56},{72,... | collective-permute-start | bytes 393224 | tf_op jit(solution)/shard_map/ppermute | solution.py:372
  5.9 4.2 %collective-permute-start.1 = (bf16[2,128,256]{2,1,0:T(8,128)(2,1)S(1)}, bf16[2,128,256]{2,1,0:T(8,128)(2,1)S(1)}, u32[]{:S(2)}, u32[]{:S(2)}) collective-permute-start(bf16[2,128,256]{2,1,0:T(8,128)(2,1)S(1)} %get-tuple-element.36), channel_id=1, source_target_pairs={{0,8},{8,0},{16,24},{24,16},{32,40},{40,32},{48,56},{56,48},{64,72... | collective-permute-start | bytes 393224 | tf_op jit(solution)/shard_map/ppermute | solution.py:373
  10.2 9.2 %copy-start = (f32[2,256,256]{2,1,0:T(8,128)S(1)}, f32[2,256,256]{2,1,0:T(8,128)}, u32[]{:S(2)}) copy-start(f32[2,256,256]{2,1,0:T(8,128)} %block_hbm.1) | copy-start | bytes 1572868
  10.2 9.2 %copy-start.1 = (bf16[6,256,256]{2,1,0:T(8,128)(2,1)S(1)}, bf16[6,256,256]{2,1,0:T(8,128)(2,1)}, u32[]{:S(2)}) copy-start(bf16[6,256,256]{2,1,0:T(8,128)(2,1)} %constant.106.clone.tables_hbm) | copy-start | bytes 2359300
  10.4 9.0 %collective-permute-start.2 = (bf16[2,512,128]{2,1,0:T(8,128)(2,1)S(1)}, bf16[2,512,128]{2,1,0:T(8,128)(2,1)S(1)}, u32[]{:S(2)}, u32[]{:S(2)}) collective-permute-start(bf16[2,512,128]{2,1,0:T(8,128)(2,1)S(1)} %get-tuple-element.35), channel_id=1, source_target_pairs={{1,2},{2,1},{3,4},{4,3},{5,6},{6,5},{9,10},{10,9},{11,12},{12,11},... | collective-permute-start | bytes 786440 | tf_op jit(solution)/shard_map/ppermute | solution.py:372
  15.3 4.0 %collective-permute-start.3 = (bf16[2,512,128]{2,1,0:T(8,128)(2,1)S(1)}, bf16[2,512,128]{2,1,0:T(8,128)(2,1)S(1)}, u32[]{:S(2)}, u32[]{:S(2)}) collective-permute-start(bf16[2,512,128]{2,1,0:T(8,128)(2,1)S(1)} %get-tuple-element.34), channel_id=1, source_target_pairs={{0,1},{1,0},{2,3},{3,2},{4,5},{5,4},{6,7},{7,6},{8,9},{9,8},{10,11... | collective-permute-start | bytes 786440 | tf_op jit(solution)/shard_map/ppermute | solution.py:373
  35.1 2.7 %collective-permute-start.4 = (f16[8,256,256]{2,1,0:T(8,128)(2,1)S(1)}, f16[8,256,256]{2,1,0:T(8,128)(2,1)S(1)}, u32[]{:S(2)}, u32[]{:S(2)}) collective-permute-start(f16[8,256,256]{2,1,0:T(8,128)(2,1)S(1)} %multiply_convert_fusion.1), channel_id=1, source_target_pairs={{0,1},{1,0},{2,3},{3,2},{4,5},{5,4},{6,7},{7,6},{8,9},{9,8},{10,11... | collective-permute-start | bytes 3145736 | tf_op jit(solution)/shard_map/ppermute | solution.py:332
  39.2 24.6 %all-to-all-start = ((f16[32,64,256]{2,1,0:T(8,128)(2,1)}), f16[32,64,256]{2,1,0:T(8,128)(2,1)}, u32[]{:S(2)}, u32[]{:S(2)}) async-start(f16[32,64,256]{2,1,0:T(8,128)(2,1)} %bitcast.17), calls=%async_computation | async-start | bytes 2097152 | tf_op jit(solution)/shard_map/all_to_all | solution.py:327
  47.2 16.5 %collective-permute-start.8 = (f16[2,512,128]{2,1,0:T(8,128)(2,1)S(1)}, f16[2,512,128]{2,1,0:T(8,128)(2,1)S(1)}, u32[]{:S(2)}, u32[]{:S(2)}) collective-permute-start(f16[2,512,128]{2,1,0:T(8,128)(2,1)S(1)} %get-tuple-element.28), channel_id=1, source_target_pairs={{1,2},{2,1},{3,4},{4,3},{5,6},{6,5},{9,10},{10,9},{11,12},{12,11},... | collective-permute-start | bytes 786440 | tf_op jit(solution)/shard_map/ppermute | solution.py:372
  51.1 12.6 %collective-permute-start.9 = (f16[2,512,128]{2,1,0:T(8,128)(2,1)S(1)}, f16[2,512,128]{2,1,0:T(8,128)(2,1)S(1)}, u32[]{:S(2)}, u32[]{:S(2)}) collective-permute-start(f16[2,512,128]{2,1,0:T(8,128)(2,1)S(1)} %get-tuple-element.29), channel_id=1, source_target_pairs={{0,1},{1,0},{2,3},{3,2},{4,5},{5,4},{6,7},{7,6},{8,9},{9,8},{10,11... | collective-permute-start | bytes 786440 | tf_op jit(solution)/shard_map/ppermute | solution.py:373
  65.3 9.8 %collective-permute-start.5 = (f16[64,256]{1,0:T(8,128)(2,1)S(1)}, f16[64,256]{1,0:T(8,128)(2,1)S(1)}, u32[]{:S(2)}, u32[]{:S(2)}) collective-permute-start(f16[64,256]{1,0:T(8,128)(2,1)S(1)} %multiply_convert_fusion.7), channel_id=1, source_target_pairs={{0,128},{1,129},{2,130},{3,131},{4,132},{5,133},{6,134},{7,135},{8... | collective-permute-start | bytes 98312 | tf_op jit(solution)/shard_map/ppermute | solution.py:340
  71.3 5.2 %collective-permute-start.6 = (f16[64,256]{1,0:T(8,128)(2,1)S(1)}, f16[64,256]{1,0:T(8,128)(2,1)S(1)}, u32[]{:S(2)}, u32[]{:S(2)}) collective-permute-start(f16[64,256]{1,0:T(8,128)(2,1)S(1)} %multiply_convert_fusion.7), channel_id=1, source_target_pairs={{0,64},{1,65},{2,66},{3,67},{4,68},{5,69},{6,70},{7,71},{8,72},{9,... | collective-permute-start | bytes 98312 | tf_op jit(solution)/shard_map/ppermute | solution.py:340
  72.1 4.5 %collective-permute-start.7 = (f16[64,256]{1,0:T(8,128)(2,1)S(1)}, f16[64,256]{1,0:T(8,128)(2,1)S(1)}, u32[]{:S(2)}, u32[]{:S(2)}) collective-permute-start(f16[64,256]{1,0:T(8,128)(2,1)S(1)} %multiply_convert_fusion.7), channel_id=1, source_target_pairs={{0,192},{1,193},{2,194},{3,195},{4,196},{5,197},{6,198},{7,199},{8... | collective-permute-start | bytes 98312 | tf_op jit(solution)/shard_map/ppermute | solution.py:340
  77.7 25.6 %all-to-all-start.1 = ((f16[32,64,256]{2,1,0:T(8,128)(2,1)}), f16[32,64,256]{2,1,0:T(8,128)(2,1)S(1)}, u32[]{:S(2)}, u32[]{:S(2)}) async-start(f16[32,64,256]{2,1,0:T(8,128)(2,1)} %broadcast_in_dim.21), calls=%async_computation.1 | async-start | bytes 2097152 | tf_op jit(solution)/shard_map/all_to_all | solution.py:327
  84.8 16.6 %collective-permute-start.10 = (f16[2,128,256]{2,1,0:T(8,128)(2,1)S(1)}, f16[2,128,256]{2,1,0:T(8,128)(2,1)S(1)}, u32[]{:S(2)}, u32[]{:S(2)}) collective-permute-start(f16[2,128,256]{2,1,0:T(8,128)(2,1)S(1)} %get-tuple-element.27), channel_id=1, source_target_pairs={{8,16},{16,8},{24,32},{32,24},{40,48},{48,40},{56,64},{64,56},{72,... | collective-permute-start | bytes 393224 | tf_op jit(solution)/shard_map/ppermute | solution.py:372
  89.1 14.1 %collective-permute-start.11 = (f16[2,128,256]{2,1,0:T(8,128)(2,1)S(1)}, f16[2,128,256]{2,1,0:T(8,128)(2,1)S(1)}, u32[]{:S(2)}, u32[]{:S(2)}) collective-permute-start(f16[2,128,256]{2,1,0:T(8,128)(2,1)S(1)} %get-tuple-element.26), channel_id=1, source_target_pairs={{0,8},{8,0},{16,24},{24,16},{32,40},{40,32},{48,56},{56,48},{64,72... | collective-permute-start | bytes 393224 | tf_op jit(solution)/shard_map/ppermute | solution.py:373
  103.3 3.6 %collective-permute-start.12 = (f16[8,256,256]{2,1,0:T(8,128)(2,1)S(1)}, f16[8,256,256]{2,1,0:T(8,128)(2,1)S(1)}, u32[]{:S(2)}, u32[]{:S(2)}) collective-permute-start(f16[8,256,256]{2,1,0:T(8,128)(2,1)S(1)} %bitcast.15), channel_id=1, source_target_pairs={{0,1},{1,0},{2,3},{3,2},{4,5},{5,4},{6,7},{7,6},{8,9},{9,8},{10,11... | collective-permute-start | bytes 3145736 | tf_op jit(solution)/shard_map/ppermute | solution.py:332
